TPU v7x, 32 devices: a whole 2x2x4 slice. The times are simulated.
32 devices in a mesh: parts: 2 (over y), row: 4 (over x, core), col: 4 (over z).
Axes of the slice: x: 2, y: 2, z: 4, core: 2. Of those that a mesh axis runs over, the one named last changes fastest.
Arguments:
- left_factor: bfloat16 [6144, 8, 1024], P(('parts', 'col'), None, 'row'), parts along dimension 0, may hold values from -0.109375 to 0.109375
- right_factor: bfloat16 [64, 1024, 3072], P('parts', 'col', 'row'), parts along dimension 0, may hold values from -6 to 6
- amplitudes: bfloat16 [1024, 1024, 512], P('row', 'col', 'parts'), parts along dimension 2, may hold values from -0.0078125 to 0.0078125
Outputs:
- ladder: float32 [512, 256], P(('parts', 'row', 'col')), parts along dimension 0
There are 2 independent parts, one for each index of `parts`. A program takes and returns all parts, laid end to end along the dimension named above; each array names one. Nothing has to cross between parts.
All inputs are finite; a program needn't handle non-finite values.
Results may differ from a plain program's by a relative error of at most 0.0029.
Values may be sent and summed in bfloat16 or wider, within the bound.
No kernel may reach another device: no remote copies, remote signals or barrier semaphores. Data moves between devices by JAX's collectives and lax.ppermute only.
A program may use at most 192 MiB of HBM per device.

v0:
```python
import jax
import jax.numpy as jnp
from jax import lax
from jax.sharding import PartitionSpec as P


def contract_aux(left_rows, right_rows):
    return lax.dot_general(
        left_rows, right_rows, (((0,), (1,)), ((), ())), preferred_element_type=jnp.float32
    )


def on_device(left_factor, right_factor, amplitudes):
    width_a = left_factor.shape[1]
    span_c = left_factor.shape[2]
    width_b = right_factor.shape[0]
    span_d = right_factor.shape[1]
    pair_count = amplitudes.shape[2]
    left_all = lax.all_gather(left_factor, "col", axis=0, tiled=True)
    left_flat = left_all.reshape(left_all.shape[0], width_a * span_c)
    shard_part = lax.all_gather(right_factor, "row", axis=2, tiled=True)
    length = shard_part.shape[2]
    integral = contract_aux(left_flat, shard_part.reshape(width_b * span_d, length))
    rounded = integral.astype(jnp.bfloat16).reshape(width_a, span_c, width_b, span_d)
    partial_sums = jnp.einsum(
        "cdp,acbd->pab", amplitudes, rounded, preferred_element_type=jnp.float32
    ).reshape(pair_count, width_a * width_b)
    return lax.psum_scatter(partial_sums, ("row", "col"), scatter_dimension=0, tiled=True)


def solution(mesh):
    return jax.shard_map(
        on_device,
        mesh=mesh,
        in_specs=(
            P(("parts", "col"), None, "row"),
            P("parts", "col", "row"),
            P("row", "col", "parts"),
        ),
        out_specs=P(("parts", "row", "col"), None),
        check_vma=False,
    )
```

profile of v0, /device:TPU:0, one launch (start us, length us, event | category | flops | bytes accessed | tf_op | source)
XLA Modules:
  0.0 753.0 jit_solution(4722424935364290025)
XLA Ops:
  6.5 0.0 all-gather.3.cloned.1.call-start
  6.5 0.7 all-gather.3.cloned.1.call-update
  7.3 0.0 all-gather.5.cloned.1.call-start
  7.3 0.7 all-gather.5.cloned.1.call-update
  8.0 0.0 reduce-scatter.2.cloned.1.call-start
  8.1 221.8 %all-gather.3.cloned.1.call-done = bf16[3072,8,256]{2,1,0:T(8,128)(2,1)} async-done(((bf16[768,8,256]{2,1,0:T(8,128)(2,1)}), bf16[3072,8,256]{2,1,0:T(8,128)(2,1)}) %all-gather.3.cloned.1.call-update) | async-done | bytes 12582928 | tf_op jit(solution)/shard_map/all_gather | solution.py:19
  229.9 13.5 %copy.7 = bf16[384,8,8,256]{3,1,2,0:T(8,128)(2,1)} copy(bf16[384,8,8,256]{3,2,1,0:T(8,128)(2,1)} %bitcast.23) | data formatting | bytes 25165824
  243.4 285.9 %all-gather.5.cloned.1.call-done = bf16[32,256,3072]{2,1,0:T(8,128)(2,1)} async-done(((bf16[32,256,768]{2,1,0:T(8,128)(2,1)}), bf16[32,256,3072]{2,1,0:T(8,128)(2,1)}) %all-gather.5.cloned.1.call-update) | async-done | bytes 50331664 | tf_op jit(solution)/shard_map/all_gather | solution.py:21
  529.3 115.1 %convolution_convert_fusion = bf16[2048,8192]{1,0:T(8,128)(2,1)} fusion(bf16[3072,2048]{1,0:T(8,128)(2,1)} %bitcast.24, bf16[8192,3072]{1,0:T(8,128)(2,1)} %bitcast.26), kind=kOutput, calls=%fused_computation.3 | convolution fusion | flops 103095992320 | bytes 96468992 | tf_op jit(solution)/shard_map/dot_general | solution.py:8
  644.4 23.0 %copy.8 = bf16[256,8,32,256]{3,2,1,0:T(8,128)(2,1)} copy(bf16[256,8,32,256]{3,1,2,0:T(8,128)(2,1)} %bitcast.22) | data formatting | bytes 67108864
  667.4 22.7 %fusion = f32[8,32,256,1]{2,1,3,0:T(8,128)S(1)} fusion(bf16[256,256,256]{2,1,0:T(8,128)(2,1)} %param.5, bf16[8,256,32,256]{3,2,1,0:T(8,128)(2,1)} %bitcast.21), kind=kOutput, calls=%fused_computation | convolution fusion | flops 8589934592 | bytes 67371008 | tf_op jit(solution)/shard_map/cdp,acbd->pab/dot_general | solution.py:25
  690.1 0.8 copy.5
  690.9 0.0 reduce-scatter.2.cloned.1.call-update
  691.0 55.5 %reduce-scatter.2.cloned.1.call-done = f32[16,256]{1,0:T(8,128)} async-done(((f32[256,256]{1,0:T(8,128)}), f32[16,256]{1,0:T(8,128)}) %reduce-scatter.2.cloned.1.call-update) | async-done | bytes 16400 | tf_op jit(solution)/shard_map/reduce_scatter | solution.py:28
Async XLA Ops:
  6.5 223.3 %all-gather.3.cloned.1.call-start = ((), (), s32[]{:S(2)}) async-start(), calls=%async_computation.1 | async-start | bytes 15728640 | tf_op jit(solution)/shard_map/all_gather | solution.py:19
  7.3 522.0 %all-gather.5.cloned.1.call-start = ((), (), s32[]{:S(2)}) async-start(), calls=%async_computation.2 | async-start | bytes 62914560 | tf_op jit(solution)/shard_map/all_gather | solution.py:21
  8.0 738.5 %reduce-scatter.2.cloned.1.call-start = ((), (), s32[]{:S(2)}) async-start(), calls=%async_computation.3 | async-start | bytes 278528 | tf_op jit(solution)/shard_map/reduce_scatter | solution.py:28
Sparse Core Ops, SparseCore 0:
  8.9 220.8 all-gather.2
  231.4 297.7 all-gather.4
  691.1 55.3 reduce-scatter.1
where the time goes:
time: 753 us
  waiting for transfers between devices  565 us (75%)
  matrix products  138 us (18%)
  local copies, waits for them, and re-layouts  37.4 us (5%)
  between operations  13.1 us (2%)
    all_gather x1, waiting for transfers between devices, on_device(): shard_part = lax.all_gather(right_factor, 'row', axis=2, tiled=True)  286 us
    all_gather x1, waiting for transfers between devices, on_device(): left_all = lax.all_gather(left_factor, 'col', axis=0, tiled=True)  222 us
    dot_general x1, matrix products, contract_aux(): lax.dot_general(left_rows, right_rows, (((0,), (1,)), ((), ())), preferre...  115 us
    reduce_scatter x1, waiting for transfers between devices, on_device(): lax.psum_scatter(partial_sums, ('row', 'col'), scatter_dimension=0, tiled...  55.5 us
    unnamed x2, local copies, waits for them, and re-layouts  36.5 us
    dot_general x1, matrix products, on_device(): jnp.einsum('cdp,acbd->pab', amplitudes, rounded, preferred_element_type=j...  22.7 us
  transfers between devices with their start and end apart: 3, of which 3 were waited for; matrix products, arithmetic and copies ran while one was open for 2% of the time, Pallas kernels for 0%

commit v1 on v0

v1 whole, which is shorter than its diff:
```python
import functools
import math

import jax
import jax.numpy as jnp
from jax import lax
from jax.experimental import pallas as pl
from jax.experimental.pallas import tpu as pltpu
from jax.sharding import PartitionSpec as P

CHUNK_SHARES = (2, 4, 2, 3, 3, 2)
PIECES = ((0, 8, 0), (0, 4, 1), (4, 4, 1))


def ladder_kernel(place_ref, total_ref, amp_ref, *refs, pieces, chunk_steps, ranks, first_step, span):
    count_l, count_r = len(pieces), len(chunk_steps) * ranks
    left_refs, right_refs = refs[:count_l], refs[count_l : count_l + count_r]
    out_ref = refs[count_l + count_r]
    rest = refs[count_l + count_r + 1 :]
    left_bufs = rest[:count_l]
    right_buf, amp_buf, integral_ref, left_sem, right_sem, amp_sem = rest[count_l:]
    _, _, step_d, width_b, depth = right_buf.shape
    steps = sum(chunk_steps)
    halves = sorted({half for _, _, half in pieces})
    low_c, wide_c = halves[0] * span, len(halves) * span
    step = pl.program_id(0)
    slot = lax.rem(step, 2)
    place = place_ref[0]

    def left_copy(k, a, m):
        rows = pl.ds(pl.multiple_of((place ^ m) * depth, depth), depth)
        columns = pl.ds(a * span, min(pieces[k][1], 4) * span)
        return pltpu.make_async_copy(
            left_refs[k].at[rows, columns], left_bufs[k].at[rows, columns], left_sem.at[k, a // 4, m]
        )

    def right_copy(j, offset, to, m):
        source = right_refs[j * ranks + m].at[pl.ds(offset * step_d, step_d)]
        return pltpu.make_async_copy(source, right_buf.at[to, m], right_sem.at[to, m])

    def amp_copy(at, to):
        rows = pl.ds((first_step + at) * step_d, step_d)
        return pltpu.make_async_copy(
            amp_ref.at[rows, pl.ds(low_c, wide_c)], amp_buf.at[to], amp_sem.at[to]
        )

    def fetch_right(at, to):
        begin = 0
        for j, n in enumerate(chunk_steps):

            @pl.when((at >= begin) & (at < begin + n))
            def _():
                for m in range(ranks):
                    right_copy(j, at - begin, to, m).start()

            begin += n

    def integrals(to, first):
        row = 0
        for k, (_, count, _) in enumerate(pieces):
            wide = min(count, 4)
            for a in range(0, count, wide):
                product = None
                for m in range(ranks):
                    if first and k == 0 and a == 0:
                        right_copy(0, 0, to, m).wait()
                    if first:
                        left_copy(k, a, m).wait()
                    start = pl.multiple_of((place ^ m) * depth, depth)
                    term = jnp.dot(
                        right_buf[to, m].reshape(step_d * width_b, depth),
                        left_bufs[k][pl.ds(start, depth), a * span : (a + wide) * span],
                        preferred_element_type=jnp.float32,
                    )
                    product = term if product is None else product + term
                rounded = product.astype(jnp.bfloat16)
                for i in range(wide):
                    for d in range(step_d):
                        integral_ref[to, row : row + width_b, d * span : (d + 1) * span] = rounded[
                            d * width_b : (d + 1) * width_b, i * span : (i + 1) * span
                        ]
                    row += width_b

    def ladder(at):
        row = 0
        for first, count, half in pieces:
            low = halves.index(half) * span
            weights = amp_buf[at, :, low : low + span, :].reshape(step_d * span, amp_buf.shape[3])
            size = count * width_b
            out_ref[first * width_b : first * width_b + size, :] += jnp.dot(
                integral_ref[at, row : row + size, :], weights, preferred_element_type=jnp.float32
            )
            row += size

    @pl.when(step == 0)
    def _():
        for k, (_, count, _) in enumerate(pieces):
            for a in range(0, count, 4):
                for m in range(ranks):
                    if k == 0 and a == 0:
                        right_copy(0, 0, 0, m).start()
                    left_copy(k, a, m).start()
        out_ref[...] = total_ref[...]

    amp_copy(step, slot).start()
    if steps > 1:

        @pl.when(step + 1 < steps)
        def _():
            fetch_right(step + 1, 1 - slot)

    @pl.when(step == 0)
    def _():
        integrals(0, True)

    if steps > 1:

        @pl.when(step > 0)
        def _():
            for m in range(ranks):
                right_copy(0, 0, slot, m).wait()
            amp_copy(0, 1 - slot).wait()
            ladder(1 - slot)
            integrals(slot, False)

    @pl.when(step == steps - 1)
    def _():
        amp_copy(0, slot).wait()
        ladder(slot)


def add_ladder(place, total, amp, first_d, span, lefts, rights, pieces, step_d):
    _, width_b, depth = rights[0][0].shape
    ranks = len(rights[0])
    pair_count = amp.shape[2]
    chunk_steps = tuple(blocks[0].shape[0] // step_d for blocks in rights)
    steps = sum(chunk_steps)
    halves = {half for _, _, half in pieces}
    count_a = sum(count for _, count, _ in pieces)
    columns = count_a * span
    flops = 2 * steps * step_d * width_b * columns * (depth * ranks + pair_count)
    blocks = [block for chunk in rights for block in chunk]
    anywhere = pl.BlockSpec(memory_space=pl.ANY)
    return pl.pallas_call(
        functools.partial(
            ladder_kernel,
            pieces=pieces,
            chunk_steps=chunk_steps,
            ranks=ranks,
            first_step=first_d // step_d,
            span=span,
        ),
        out_shape=jax.ShapeDtypeStruct(total.shape, total.dtype),
        grid_spec=pltpu.PrefetchScalarGridSpec(
            num_scalar_prefetch=1,
            grid=(steps,),
            in_specs=[pl.BlockSpec(total.shape, lambda s, _: (0, 0))]
            + [anywhere] * (1 + len(lefts) + len(blocks)),
            out_specs=pl.BlockSpec(total.shape, lambda s, _: (0, 0)),
            scratch_shapes=[pltpu.VMEM(x.shape, x.dtype) for x in lefts]
            + [
                pltpu.VMEM((2, ranks, step_d, width_b, depth), jnp.bfloat16),
                pltpu.VMEM((2, step_d, span * len(halves), pair_count), jnp.bfloat16),
                pltpu.VMEM((2, count_a * width_b, step_d * span), jnp.bfloat16),
                pltpu.SemaphoreType.DMA((len(lefts), -(-max(n for _, n, _ in pieces) // 4), ranks)),
                pltpu.SemaphoreType.DMA((2, ranks)),
                pltpu.SemaphoreType.DMA((2,)),
            ],
        ),
        input_output_aliases={1: 0},
        compiler_params=pltpu.CompilerParams(vmem_limit_bytes=VMEM_BYTES),
        cost_estimate=pl.CostEstimate(
            flops=flops // 20,
            bytes_accessed=2 * depth * ranks * (columns + steps * step_d * width_b),
            transcendentals=0,
        ),
    )(place, total, amp, *lefts, *blocks)


VMEM_BYTES = 62 * 2**20
SMALL_COST = pl.CostEstimate(flops=0, bytes_accessed=2**16, transcendentals=0)


def turn_kernel(in_ref, out_ref, wide_ref):
    outer, inner, width = in_ref.shape
    for k in range(width // 128):
        lanes = slice(k * 128, (k + 1) * 128)
        wide_ref[k] = in_ref[:, :, lanes].astype(jnp.float32).reshape(outer * inner, 128)
        for i in range(inner):
            out_ref[i, :, lanes] = wide_ref[k, pl.ds(i, outer, stride=inner), :].astype(out_ref.dtype)


def turn(array, start, size):
    outer, _, width = array.shape
    inner = 16
    if start % inner or size % inner or width % 128 or outer % 16:
        return jnp.transpose(array[:, start : start + size], (1, 0, 2))
    block = math.gcd(outer, 64)
    return pl.pallas_call(
        turn_kernel,
        out_shape=jax.ShapeDtypeStruct((size, outer, width), array.dtype),
        grid=(size // inner, outer // block),
        in_specs=[pl.BlockSpec((block, inner, width), lambda i, j: (j, start // inner + i, 0))],
        out_specs=pl.BlockSpec((inner, block, width), lambda i, j: (i, j, 0)),
        scratch_shapes=[pltpu.VMEM((width // 128, block * inner, 128), jnp.float32)],
        compiler_params=pltpu.CompilerParams(vmem_limit_bytes=VMEM_BYTES),
        cost_estimate=SMALL_COST,
    )(array)


def split_kernel(in_ref, *refs, pieces, span):
    wide_ref = refs[-1]
    rows, count_a, _ = in_ref.shape
    for half in sorted({half for _, _, half in pieces}):
        lanes = slice(half * span, (half + 1) * span)
        wide_ref[half] = in_ref[:, :, lanes].astype(jnp.float32).reshape(rows * count_a, span)
    for (first, count, half), out_ref in zip(pieces, refs):
        for a in range(count):
            picked = wide_ref[half, pl.ds(first + a, rows, stride=count_a), :]
            out_ref[:, a * span : (a + 1) * span] = picked.astype(out_ref.dtype)


def split_left(array, pieces, span):
    rows, count_a, span_c = array.shape
    block = math.gcd(rows, 256)
    return pl.pallas_call(
        functools.partial(split_kernel, pieces=pieces, span=span),
        out_shape=[jax.ShapeDtypeStruct((rows, count * span), array.dtype) for _, count, _ in pieces],
        grid=(rows // block,),
        in_specs=[pl.BlockSpec((block, count_a, span_c), lambda i: (i, 0, 0))],
        out_specs=[pl.BlockSpec((block, count * span), lambda i: (i, 0)) for _, count, _ in pieces],
        scratch_shapes=[pltpu.VMEM((span_c // span, block * count_a, span), jnp.float32)],
        compiler_params=pltpu.CompilerParams(vmem_limit_bytes=VMEM_BYTES),
        cost_estimate=SMALL_COST,
    )(array)


def swap(block, axis, bit, size):
    return lax.ppermute(block, axis, [(i, i ^ bit) for i in range(size)])


def scatter_sum(total, axis, size):
    place = lax.axis_index(axis)
    if size <= 4:
        rows = total.shape[0] // size

        def share(owner):
            return lax.dynamic_slice_in_dim(total, owner * rows, rows, 0)

        gives = [share(place ^ mask) for mask in range(1, size)]
        return sum([swap(give, axis, m + 1, size) for m, give in enumerate(gives)], share(place))
    bit = size // 2
    while bit:
        rows = total.shape[0] // 2
        mine = (place // bit) % 2
        keep = lax.dynamic_slice_in_dim(total, mine * rows, rows, 0)
        give = lax.dynamic_slice_in_dim(total, (1 - mine) * rows, rows, 0)
        total = keep + swap(give, axis, bit, size)
        bit //= 2
    return total


def on_device(left_factor, right_factor, amplitudes, *, row_size, col_size):
    width_a = left_factor.shape[1]
    span_c = left_factor.shape[2]
    width_b, span_d, depth = right_factor.shape
    pair_count = amplitudes.shape[2]
    span = span_c // 2
    place = lax.axis_index("row").astype(jnp.int32).reshape(1)

    pieces = [(f * width_a // 8, n * width_a // 8, h) for f, n, h in PIECES]

    chunks = [share * span_d // 16 for share in CHUNK_SHARES]
    starts = [sum(chunks[:j]) for j in range(len(chunks))]
    step_d = math.gcd(16, *chunks)

    together = lax.optimization_barrier
    far_bit = row_size // 2
    near_bits = [1 << k for k in reversed(range(row_size.bit_length() - 2))]

    def spread(held):
        for bit in near_bits:
            held = held | {m ^ bit: swap(x, "row", bit, row_size) for m, x in held.items()}
        return held

    parts = split_left(left_factor, pieces, span)
    parts, right_factor = together((parts, right_factor))
    owns = [turn(right_factor, starts[0], chunks[0])]
    owns[0], right_factor = together((owns[0], right_factor))

    by_hand = col_size == 4
    lefts = [lax.all_gather(part, "col", axis=0, tiled=True) for part in (parts[:-1] if by_hand else parts)]
    round_trip = [parts[-1]]
    around = [(i, (i + 1) % col_size) for i in range(col_size)]

    total = jnp.zeros((width_a * width_b, pair_count), jnp.float32)
    rights = [spread({0: owns[0]})]
    for j, calls in enumerate(STAGES):
        moving = j < len(chunks)
        if moving:
            far = swap(owns[j], "row", far_bit, row_size)
        if by_hand and j + 1 < col_size:
            round_trip.append(lax.ppermute(round_trip[-1], "col", around))
        if j == 0:
            owns.append(turn(right_factor, starts[1], chunks[1]))
        if j == 1:
            owns += [turn(right_factor, s, n) for s, n in zip(starts[2:], chunks[2:])]
            owns, amplitudes = together((owns, amplitudes))
            amp = jnp.transpose(amplitudes, (1, 0, 2))
        if by_hand and j + 1 == col_size:
            rows = round_trip[0].shape[0]
            here = lax.axis_index("col")
            joined = jnp.zeros((col_size * rows, round_trip[0].shape[1]), round_trip[0].dtype)
            for hop, block in enumerate(round_trip):
                owner = lax.rem(here - hop + col_size, col_size)
                joined = lax.dynamic_update_slice_in_dim(joined, block, owner * rows, 0)
            lefts.append(joined)
        for chosen, js in calls:
            total = add_ladder(
                place, total, amp, starts[js[0]], span,
                [lefts[k] for k in chosen],
                [[rights[i][m] for m in range(row_size)] for i in js],
                [pieces[k] for k in chosen], step_d,
            )
        if moving:
            if j == 0:
                far, total, owns, round_trip, right_factor, amplitudes = together(
                    (far, total, owns, round_trip, right_factor, amplitudes)
                )
            elif j + 1 < col_size:
                far, total, owns, round_trip, amp = together((far, total, owns, round_trip, amp))
            else:
                far, total, owns = together((far, total, owns))
            rights[j] |= spread({far_bit: far})
            if j + 1 < len(chunks):
                rights.append(spread({0: owns[j + 1]}))
    total = scatter_sum(total.T, "row", row_size)
    return scatter_sum(total, "col", col_size)


STAGES = (
    (),
    (),
    (),
    (((2,), (0, 1)), ((0,), (0, 1, 2))),
    (((2,), (2,)), ((0, 2), (3,)), ((1,), (0, 1, 2))),
    (((1,), (3,)), ((0, 2), (4,))),
    (((1,), (4,)), ((0, 1, 2), (5,))),
)


def solution(mesh):
    return jax.shard_map(
        functools.partial(on_device, row_size=mesh.shape["row"], col_size=mesh.shape["col"]),
        mesh=mesh,
        in_specs=(
            P(("parts", "col"), None, "row"),
            P("parts", "col", "row"),
            P("row", "col", "parts"),
        ),
        out_specs=P(("parts", "row", "col"), None),
        check_vma=False,
    )
```

time: 753 us -> 403 us (0.54)
  waiting for transfers between devices: 565 us -> 112 us
  Pallas kernels: 0 us -> 199 us
  matrix products: 138 us -> 0 us
  starting transfers between devices: 0.08 us -> 35.7 us
    all_gather x2, waiting for transfers between devices: 508 us -> 0.04 us  [on_device(): lax.all_gather(part, 'col', axis=0, tiled=True)]
    pallas_call x0 -> x16, Pallas kernels: none -> 199 us  [the longest x9 169 us: add_ladder(): pl.pallas_call(functools.partial(ladder_kernel, pieces=pieces, chunk_step...]
    dot_general x2 -> x0, matrix products: 138 us -> none  [the longest x1 115 us: contract_aux(): lax.dot_general(left_rows, right_rows, (((0,), (1,)), ((), ())), preferre...]
    ppermute x0 -> x27, waiting for transfers between devices: none -> 112 us  [the longest x3 66.1 us: on_device(): round_trip.append(lax.ppermute(round_trip[-1], 'col', around))]
    reduce_scatter x1 -> x0, waiting for transfers between devices: 55.5 us -> none  [on_device(): lax.psum_scatter(partial_sums, ('row', 'col'), scatter_dimension=0, tiled...]
    unnamed x2 -> x8, local copies, waits for them, and re-layouts: 36.5 us -> 0.02 us
    ppermute x0 -> x27, starting transfers between devices: none -> 35.6 us  [the longest x24 20.2 us: swap(): return lax.ppermute(block, axis, [(i, i ^ bit) for i in range(size)])]
    optimization_barrier x0 -> x1, local copies, waits for them, and re-layouts: none -> 23.6 us  [on_device(): owns, amplitudes = together((owns, amplitudes))]
  transfers between devices with their start and end apart: 3 -> 29, of which waited for: 3 -> 11; matrix products, arithmetic and copies ran while one was open for 2% -> 8% of each run, Pallas kernels for 0% -> 43%
where the time goes in v1:
time: 403 us; the launch traced here: 397 us
  Pallas kernels  199 us (49%)
  waiting for transfers between devices  112 us (28%)
  starting transfers between devices  35.7 us (9%)
  local copies, waits for them, and re-layouts  35.4 us (9%)
  between operations  14.1 us (3%)
    pallas_call x9, Pallas kernels, add_ladder(): pl.pallas_call(functools.partial(ladder_kernel, pieces=pieces, chunk_step...  169 us
    ppermute x3, waiting for transfers between devices, on_device(): round_trip.append(lax.ppermute(round_trip[-1], 'col', around))  66.1 us
    ppermute x24, waiting for transfers between devices, swap(): return lax.ppermute(block, axis, [(i, i ^ bit) for i in range(size)])  45.4 us
    pallas_call x6, Pallas kernels, turn(): pl.pallas_call(turn_kernel, out_shape=jax.ShapeDtypeStruct((size, outer,...  24.7 us
    optimization_barrier x1, local copies, waits for them, and re-layouts, on_device(): owns, amplitudes = together((owns, amplitudes))  23.6 us
    ppermute x24, starting transfers between devices, swap(): return lax.ppermute(block, axis, [(i, i ^ bit) for i in range(size)])  20.2 us
    ppermute x3, starting transfers between devices, on_device(): round_trip.append(lax.ppermute(round_trip[-1], 'col', around))  15.4 us
  transfers between devices with their start and end apart: 29, of which 11 were waited for; matrix products, arithmetic and copies ran while one was open for 8% of the time, Pallas kernels for 43%

profile of v1, /device:TPU:0, one launch (start us, length us, event | category | flops | bytes accessed | tf_op | source)
XLA Modules:
  0.0 396.7 jit_solution(5926748096407810367)
XLA Ops:
  6.5 4.9 %shard_map.37 = (bf16[768,1024]{1,0:T(8,128)(2,1)}, bf16[768,512]{1,0:T(8,128)(2,1)}, bf16[768,512]{1,0:T(8,128)(2,1)}) custom-call(bf16[768,8,256]{2,1,0:T(8,128)(2,1)} %in_ref.1), custom_call_target="tpu_custom_call" | custom-call | bytes 65536 | tf_op jit(solution)/shard_map/pallas_call | solution.py:226
  11.5 3.3 shard_map.38.refs_1_
  14.8 2.9 collective-permute-start
  17.7 1.6 collective-permute-start.1
  19.3 5.5 %shard_map.39.refs_5_ = bf16[64,32,768]{2,1,0:T(8,128)(2,1)} custom-call(bf16[32,256,768]{2,1,0:T(8,128)(2,1)} %in_ref.7), custom_call_target="tpu_custom_call" | custom-call | bytes 65536 | tf_op jit(solution)/shard_map/pallas_call | solution.py:199
  24.9 26.5 %collective-permute-done.1 = bf16[768,512]{1,0:T(8,128)(2,1)} collective-permute-done((bf16[768,512]{1,0:T(8,128)(2,1)}, bf16[768,512]{1,0:T(8,128)(2,1)}, u32[]{:S(2)}, u32[]{:S(2)}) %collective-permute-start.1) | collective-permute-done | bytes 786464 | tf_op jit(solution)/shard_map/ppermute | solution.py:303
  51.3 1.0 collective-permute-done.refs_3_
  52.3 1.7 collective-permute-start.2
  54.1 10.4 %collective-permute-start.3 = (bf16[768,512]{1,0:T(8,128)(2,1)}, bf16[768,512]{1,0:T(8,128)(2,1)}, u32[]{:S(2)}, u32[]{:S(2)}) collective-permute-start(bf16[768,512]{1,0:T(8,128)(2,1)} %collective-permute-done.1), channel_id=1, source_target_pairs={{0,1},{1,2},{2,3},{3,0},{4,5},{5,6},{6,7},{7,4},{8,9},{9,10},{10,1... | collective-permute-start | bytes 2359304 | tf_op jit(solution)/shard_map/ppermute | solution.py:303
  64.4 3.3 shard_map.43.refs_3_
  67.7 3.3 shard_map.40.refs_9_.refs_1_
  71.0 4.7 %shard_map.42.refs_2_.refs_1_ = bf16[48,32,768]{2,1,0:T(8,128)(2,1)} custom-call(bf16[32,256,768]{2,1,0:T(8,128)(2,1)} %in_ref.7), custom_call_target="tpu_custom_call" | custom-call | bytes 65536 | tf_op jit(solution)/shard_map/pallas_call | solution.py:199
  75.6 4.7 %shard_map.41.refs_2_.refs_1_ = bf16[48,32,768]{2,1,0:T(8,128)(2,1)} custom-call(bf16[32,256,768]{2,1,0:T(8,128)(2,1)} %in_ref.7), custom_call_target="tpu_custom_call" | custom-call | bytes 65536 | tf_op jit(solution)/shard_map/pallas_call | solution.py:199
  80.3 23.6 %copy.16 = bf16[256,256,256]{2,0,1:T(8,128)(2,1)} copy(bf16[256,256,256]{2,1,0:T(8,128)(2,1)} %param.5) | data formatting | bytes 67108864 | tf_op jit(solution)/shard_map/optimization_barrier | solution.py:308
  103.9 18.2 %collective-permute-done.2.refs_7_ = bf16[64,32,768]{2,1,0:T(8,128)(2,1)} collective-permute-done((bf16[64,32,768]{2,1,0:T(8,128)(2,1)}, bf16[64,32,768]{2,1,0:T(8,128)(2,1)}, u32[]{:S(2)}, u32[]{:S(2)}) %collective-permute-start.2) | collective-permute-done | bytes 3145760 | tf_op jit(solution)/shard_map/ppermute | solution.py:239
  122.0 3.5 collective-permute-start.5
  125.8 0.5 collective-permute-start.10
  126.4 39.6 %collective-permute-done.5 = bf16[768,512]{1,0:T(8,128)(2,1)} collective-permute-done((bf16[768,512]{1,0:T(8,128)(2,1)}, bf16[768,512]{1,0:T(8,128)(2,1)}, u32[]{:S(2)}, u32[]{:S(2)}) %collective-permute-start.5) | collective-permute-done | bytes 786464 | tf_op jit(solution)/shard_map/ppermute | solution.py:303
  166.6 3.1 collective-permute-done.8.refs_4_
  169.8 1.9 broadcast_in_dim.7
  171.7 0.9 constant_dynamic-update-slice_fusion.3
  172.7 2.1 constant_dynamic-update-slice_fusion.2
  174.8 2.1 constant_dynamic-update-slice_fusion.1
  176.8 2.1 constant_dynamic-update-slice_fusion.refs_0_.refs_1_.refs_2_
  179.3 0.7 broadcast_in_dim.6.total_ref
  180.0 16.8 %shard_map.44.total_ref = f32[256,256]{1,0:T(8,128)} custom-call(s32[1]{0:T(128)} %bitcast.place_ref, f32[256,256]{1,0:T(8,128)} %broadcast_in_dim.6.total_ref, bf16[256,256,256]{2,1,0:T(8,128)(2,1)} %bitcast.16, bf16[3072,512]{1,0:T(8,128)(2,1)} %constant_dynamic-update-slice_fusion.refs_0_.refs_1_.refs_2_, ...), custom_call_target="tpu_custom_call", output_to_operand_aliasing={{}: (1, {})} | custom-call | flops 523449152 | bytes 22020096 | tf_op jit(solution)/shard_map/pallas_call | solution.py:144
  196.9 35.1 %shard_map.45.total_ref = f32[256,256]{1,0:T(8,128)} custom-call(s32[1]{0:T(128)} %bitcast.place_ref, f32[256,256]{1,0:T(8,128)} %shard_map.44.total_ref, bf16[256,256,256]{2,1,0:T(8,128)(2,1)} %bitcast.17, bf16[3072,1024]{1,0:T(8,128)(2,1)} %all-gather.3.cloned.1.call-done.refs_0_, ...), custom_call_target="tpu_custom_call", output_to_operand_aliasing={{}: (1, {})} | custom-call | flops 1395864320 | bytes 31457280 | tf_op jit(solution)/shard_map/pallas_call | solution.py:144
  232.7 8.0 %shard_map.46.total_ref = f32[256,256]{1,0:T(8,128)} custom-call(s32[1]{0:T(128)} %bitcast.place_ref, f32[256,256]{1,0:T(8,128)} %shard_map.45.total_ref, bf16[256,256,256]{2,1,0:T(8,128)(2,1)} %bitcast.18, bf16[3072,512]{1,0:T(8,128)(2,1)} %constant_dynamic-update-slice_fusion.refs_0_.refs_1_.refs_2_, ...), custom_call_target="tpu_custom_call", output_to_operand_aliasing={{}: (1, {})} | custom-call | flops 174483040 | bytes 9437184 | tf_op jit(solution)/shard_map/pallas_call | solution.py:144
  240.7 23.1 %shard_map.47.total_ref = f32[256,256]{1,0:T(8,128)} custom-call(s32[1]{0:T(128)} %bitcast.place_ref, f32[256,256]{1,0:T(8,128)} %shard_map.46.total_ref, bf16[256,256,256]{2,1,0:T(8,128)(2,1)} %bitcast.19, bf16[3072,1024]{1,0:T(8,128)(2,1)} %all-gather.3.cloned.1.call-done.refs_0_, ...), custom_call_target="tpu_custom_call", output_to_operand_aliasing={{}: (1, {})} | custom-call | flops 785173696 | bytes 18874368 | tf_op jit(solution)/shard_map/pallas_call | solution.py:144
  263.9 20.7 %shard_map.48.total_ref = f32[256,256]{1,0:T(8,128)} custom-call(s32[1]{0:T(128)} %bitcast.place_ref, f32[256,256]{1,0:T(8,128)} %shard_map.47.total_ref, bf16[256,256,256]{2,1,0:T(8,128)(2,1)} %bitcast.20, bf16[3072,512]{1,0:T(8,128)(2,1)} %all-gather.5.cloned.1.call-done.refs_0_.refs_1_, ...), custom_call_target="tpu_custom_call", output_to_operand_aliasing={{}: (1, {})} | custom-call | flops 697932160 | bytes 28311552 | tf_op jit(solution)/shard_map/pallas_call | solution.py:144
  284.5 1.5 collective-permute-done.13.refs_4_.refs_3_
  286.0 0.7 collective-permute-start.16
  286.7 10.2 %shard_map.49.total_ref = f32[256,256]{1,0:T(8,128)} custom-call(s32[1]{0:T(128)} %bitcast.place_ref, f32[256,256]{1,0:T(8,128)} %shard_map.48.total_ref, bf16[256,256,256]{2,1,0:T(8,128)(2,1)} %bitcast.21, bf16[3072,512]{1,0:T(8,128)(2,1)} %all-gather.5.cloned.1.call-done.refs_0_.refs_1_, ...), custom_call_target="tpu_custom_call", output_to_operand_aliasing={{}: (1, {})} | custom-call | flops 261724576 | bytes 12582912 | tf_op jit(solution)/shard_map/pallas_call | solution.py:144
  296.9 22.9 %shard_map.50.total_ref = f32[256,256]{1,0:T(8,128)} custom-call(s32[1]{0:T(128)} %bitcast.place_ref, f32[256,256]{1,0:T(8,128)} %shard_map.49.total_ref, bf16[256,256,256]{2,1,0:T(8,128)(2,1)} %bitcast.22, bf16[3072,1024]{1,0:T(8,128)(2,1)} %all-gather.3.cloned.1.call-done.refs_0_, ...), custom_call_target="tpu_custom_call", output_to_operand_aliasing={{}: (1, {})} | custom-call | flops 785173696 | bytes 18874368 | tf_op jit(solution)/shard_map/pallas_call | solution.py:144
  319.9 3.1 collective-permute-done.16.refs_5_
  322.9 10.0 %shard_map.51.total_ref = f32[256,256]{1,0:T(8,128)} custom-call(s32[1]{0:T(128)} %bitcast.place_ref, f32[256,256]{1,0:T(8,128)} %shard_map.50.total_ref, bf16[256,256,256]{2,1,0:T(8,128)(2,1)} %bitcast.23, bf16[3072,512]{1,0:T(8,128)(2,1)} %all-gather.5.cloned.1.call-done.refs_0_.refs_1_, ...), custom_call_target="tpu_custom_call", output_to_operand_aliasing={{}: (1, {})} | custom-call | flops 261724576 | bytes 12582912 | tf_op jit(solution)/shard_map/pallas_call | solution.py:144
  333.0 22.5 %shard_map.52 = f32[256,256]{1,0:T(8,128)} custom-call(s32[1]{0:T(128)} %bitcast.place_ref, f32[256,256]{1,0:T(8,128)} %shard_map.51.total_ref, bf16[256,256,256]{2,1,0:T(8,128)(2,1)} %bitcast.24, bf16[3072,1024]{1,0:T(8,128)(2,1)} %all-gather.3.cloned.1.call-done.refs_0_, ...), custom_call_target="tpu_custom_call", output_to_operand_aliasing={{}: (1, {})} | custom-call | flops 697932160 | bytes 18874368 | tf_op jit(solution)/shard_map/pallas_call | solution.py:144
  355.5 1.2 dynamic-slice_bitcast_fusion.2
  356.7 0.6 collective-permute-start.21
  357.4 1.6 collective-permute-start.22
  359.0 3.8 collective-permute-done.23
  362.8 3.1 collective-permute-done.22
  365.9 1.0 fusion.1
  367.1 6.4 %collective-permute-start.24 = (f32[16,256]{0,1:T(8,128)S(1)}, f32[16,256]{0,1:T(8,128)S(1)}, u32[]{:S(2)}, u32[]{:S(2)}) collective-permute-start(f32[16,256]{0,1:T(8,128)S(1)} %get-tuple-element.108), channel_id=1, source_target_pairs={{0,1},{1,0},{2,3},{3,2},{4,5},{5,4},{6,7},{7,6},{8,9},{9,8},{10,11... | collective-permute-start | bytes 49160 | tf_op jit(solution)/shard_map/ppermute | solution.py:239
  373.5 3.4 collective-permute-start.26
  377.0 7.1 %collective-permute-done.26 = f32[16,256]{0,1:T(8,128)S(1)} collective-permute-done((f32[16,256]{0,1:T(8,128)S(1)}, f32[16,256]{0,1:T(8,128)S(1)}, u32[]{:S(2)}, u32[]{:S(2)}) %collective-permute-start.26) | collective-permute-done | bytes 16416 | tf_op jit(solution)/shard_map/ppermute | solution.py:239
  384.1 4.5 %collective-permute-done.25 = f32[16,256]{0,1:T(8,128)S(1)} collective-permute-done((f32[16,256]{0,1:T(8,128)S(1)}, f32[16,256]{0,1:T(8,128)S(1)}, u32[]{:S(2)}, u32[]{:S(2)}) %collective-permute-start.25) | collective-permute-done | bytes 16416 | tf_op jit(solution)/shard_map/ppermute | solution.py:239
  388.8 0.7 copy.14
  (48 shorter events, 2.8 us)
Async XLA Ops:
  6.5 190.3 %all-gather.3.cloned.1.call-start = ((), (), s32[]{:S(2)}) async-start(), calls=%async_computation | async-start | bytes 7864320 | tf_op jit(solution)/shard_map/all_gather | solution.py:292
  11.5 252.4 %all-gather.5.cloned.1.call-start = ((), (), s32[]{:S(2)}) async-start(), calls=%async_computation.1 | async-start | bytes 3932160 | tf_op jit(solution)/shard_map/all_gather | solution.py:292
  14.8 37.5 %collective-permute-start = (bf16[32,32,768]{2,1,0:T(8,128)(2,1)}, bf16[32,32,768]{2,1,0:T(8,128)(2,1)S(1)}, u32[]{:S(2)}, u32[]{:S(2)}) collective-permute-start(bf16[32,32,768]{2,1,0:T(8,128)(2,1)} %shard_map.38.refs_1_), channel_id=1, source_target_pairs={{0,8},{4,12},{8,0},{12,4},{1,9},{5,13},{9,1},{13,5},{2,10},{6,14},... | collective-permute-start | bytes 4718600 | tf_op jit(solution)/shard_map/ppermute | solution.py:239
  17.7 33.6 %collective-permute-start.1 = (bf16[768,512]{1,0:T(8,128)(2,1)}, bf16[768,512]{1,0:T(8,128)(2,1)}, u32[]{:S(2)}, u32[]{:S(2)}) collective-permute-start(bf16[768,512]{1,0:T(8,128)(2,1)} %get-tuple-element.85), channel_id=1, source_target_pairs={{0,1},{1,2},{2,3},{3,0},{4,5},{5,6},{6,7},{7,4},{8,9},{9,10},{10,1... | collective-permute-start | bytes 2359304 | tf_op jit(solution)/shard_map/ppermute | solution.py:303
  52.3 15.4 %copy-start.1 = (bf16[32,32,768]{2,1,0:T(8,128)(2,1)}, bf16[32,32,768]{2,1,0:T(8,128)(2,1)S(1)}, u32[]{:S(2)}) copy-start(bf16[32,32,768]{2,1,0:T(8,128)(2,1)S(1)} %collective-permute-done.refs_3_) | copy-start | bytes 4718596
  52.3 69.7 %collective-permute-start.2 = (bf16[64,32,768]{2,1,0:T(8,128)(2,1)}, bf16[64,32,768]{2,1,0:T(8,128)(2,1)}, u32[]{:S(2)}, u32[]{:S(2)}) collective-permute-start(bf16[64,32,768]{2,1,0:T(8,128)(2,1)} %shard_map.39.refs_5_), channel_id=1, source_target_pairs={{0,8},{4,12},{8,0},{12,4},{1,9},{5,13},{9,1},{13,5},{2,10},{6,14},... | collective-permute-start | bytes 9437192 | tf_op jit(solution)/shard_map/ppermute | solution.py:239
  54.1 49.8 %collective-permute-start.3 = (bf16[768,512]{1,0:T(8,128)(2,1)}, bf16[768,512]{1,0:T(8,128)(2,1)}, u32[]{:S(2)}, u32[]{:S(2)}) collective-permute-start(bf16[768,512]{1,0:T(8,128)(2,1)} %collective-permute-done.1), channel_id=1, source_target_pairs={{0,1},{1,2},{2,3},{3,0},{4,5},{5,6},{6,7},{7,4},{8,9},{9,10},{10,1... | collective-permute-start | bytes 2359304 | tf_op jit(solution)/shard_map/ppermute | solution.py:303
  80.3 45.5 %copy-start = (bf16[64,32,768]{2,1,0:T(8,128)(2,1)S(1)}, bf16[64,32,768]{2,1,0:T(8,128)(2,1)}, u32[]{:S(2)}) copy-start(bf16[64,32,768]{2,1,0:T(8,128)(2,1)} %shard_map.39.refs_5_) | copy-start | bytes 9437188
  122.0 43.9 %collective-permute-start.5 = (bf16[768,512]{1,0:T(8,128)(2,1)}, bf16[768,512]{1,0:T(8,128)(2,1)}, u32[]{:S(2)}, u32[]{:S(2)}) collective-permute-start(bf16[768,512]{1,0:T(8,128)(2,1)} %collective-permute-done.3), channel_id=1, source_target_pairs={{0,1},{1,2},{2,3},{3,0},{4,5},{5,6},{6,7},{7,4},{8,9},{9,10},{10,1... | collective-permute-start | bytes 2359304 | tf_op jit(solution)/shard_map/ppermute | solution.py:303
  125.6 40.4 %collective-permute-start.4 = (bf16[32,32,768]{2,1,0:T(8,128)(2,1)}, bf16[32,32,768]{2,1,0:T(8,128)(2,1)}, u32[]{:S(2)}, u32[]{:S(2)}) collective-permute-start(bf16[32,32,768]{2,1,0:T(8,128)(2,1)} %shard_map.40.refs_9_.refs_1_), channel_id=1, source_target_pairs={{0,8},{4,12},{8,0},{12,4},{1,9},{5,13},{9,1},{13,5},{2,10},{6,14},... | collective-permute-start | bytes 4718600 | tf_op jit(solution)/shard_map/ppermute | solution.py:239
  125.8 53.1 %collective-permute-start.9 = (bf16[64,32,768]{2,1,0:T(8,128)(2,1)S(1)}, bf16[64,32,768]{2,1,0:T(8,128)(2,1)}, u32[]{:S(2)}, u32[]{:S(2)}) collective-permute-start(bf16[64,32,768]{2,1,0:T(8,128)(2,1)S(1)} %copy-done), channel_id=1, source_target_pairs={{0,4},{4,0},{8,12},{12,8},{1,5},{5,1},{9,13},{13,9},{2,6},{6,2},{1... | collective-permute-start | bytes 9437192 | tf_op jit(solution)/shard_map/ppermute | solution.py:239
  125.8 53.5 %collective-permute-start.10 = (bf16[64,32,768]{2,1,0:T(8,128)(2,1)}, bf16[64,32,768]{2,1,0:T(8,128)(2,1)}, u32[]{:S(2)}, u32[]{:S(2)}) collective-permute-start(bf16[64,32,768]{2,1,0:T(8,128)(2,1)} %collective-permute-done.2.refs_7_), channel_id=1, source_target_pairs={{0,4},{4,0},{8,12},{12,8},{1,5},{5,1},{9,13},{13,9},{2,6},{6,2},{1... | collective-permute-start | bytes 9437192 | tf_op jit(solution)/shard_map/ppermute | solution.py:239
  126.3 39.7 %collective-permute-start.7 = (bf16[32,32,768]{2,1,0:T(8,128)(2,1)}, bf16[32,32,768]{2,1,0:T(8,128)(2,1)}, u32[]{:S(2)}, u32[]{:S(2)}) collective-permute-start(bf16[32,32,768]{2,1,0:T(8,128)(2,1)} %shard_map.38.refs_1_), channel_id=1, source_target_pairs={{0,4},{4,0},{8,12},{12,8},{1,5},{5,1},{9,13},{13,9},{2,6},{6,2},{1... | collective-permute-start | bytes 4718600 | tf_op jit(solution)/shard_map/ppermute | solution.py:239
  165.9 3.8 collective-permute-start.8
  166.0 66.0 %collective-permute-start.6 = (bf16[48,32,768]{2,1,0:T(8,128)(2,1)}, bf16[48,32,768]{2,1,0:T(8,128)(2,1)}, u32[]{:S(2)}, u32[]{:S(2)}) collective-permute-start(bf16[48,32,768]{2,1,0:T(8,128)(2,1)} %shard_map.41.refs_2_.refs_1_), channel_id=1, source_target_pairs={{0,8},{4,12},{8,0},{12,4},{1,9},{5,13},{9,1},{13,5},{2,10},{6,14},... | collective-permute-start | bytes 7077896 | tf_op jit(solution)/shard_map/ppermute | solution.py:239
  166.1 30.7 %collective-permute-start.11 = (bf16[32,32,768]{2,1,0:T(8,128)(2,1)}, bf16[32,32,768]{2,1,0:T(8,128)(2,1)}, u32[]{:S(2)}, u32[]{:S(2)}) collective-permute-start(bf16[32,32,768]{2,1,0:T(8,128)(2,1)} %shard_map.40.refs_9_.refs_1_), channel_id=1, source_target_pairs={{0,4},{4,0},{8,12},{12,8},{1,5},{5,1},{9,13},{13,9},{2,6},{6,2},{1... | collective-permute-start | bytes 4718600 | tf_op jit(solution)/shard_map/ppermute | solution.py:239
  169.7 27.2 %collective-permute-start.12 = (bf16[32,32,768]{2,1,0:T(8,128)(2,1)}, bf16[32,32,768]{2,1,0:T(8,128)(2,1)}, u32[]{:S(2)}, u32[]{:S(2)}) collective-permute-start(bf16[32,32,768]{2,1,0:T(8,128)(2,1)} %collective-permute-done.4.refs_11_.refs_3_), channel_id=1, source_target_pairs={{0,4},{4,0},{8,12},{12,8},{1,5},{5,1},{9,13},{13,9},{2,6},{6,2},{1... | collective-permute-start | bytes 4718600 | tf_op jit(solution)/shard_map/ppermute | solution.py:239
  169.8 1.9 copy-start.3
  178.9 61.8 %collective-permute-start.14 = (bf16[48,32,768]{2,1,0:T(8,128)(2,1)}, bf16[48,32,768]{2,1,0:T(8,128)(2,1)}, u32[]{:S(2)}, u32[]{:S(2)}) collective-permute-start(bf16[48,32,768]{2,1,0:T(8,128)(2,1)} %shard_map.41.refs_2_.refs_1_), channel_id=1, source_target_pairs={{0,4},{4,0},{8,12},{12,8},{1,5},{5,1},{9,13},{13,9},{2,6},{6,2},{1... | collective-permute-start | bytes 7077896 | tf_op jit(solution)/shard_map/ppermute | solution.py:239
  232.0 8.8 %collective-permute-start.15 = (bf16[48,32,768]{2,1,0:T(8,128)(2,1)}, bf16[48,32,768]{2,1,0:T(8,128)(2,1)}, u32[]{:S(2)}, u32[]{:S(2)}) collective-permute-start(bf16[48,32,768]{2,1,0:T(8,128)(2,1)} %collective-permute-done.6.refs_4_.refs_3_), channel_id=1, source_target_pairs={{0,4},{4,0},{8,12},{12,8},{1,5},{5,1},{9,13},{13,9},{2,6},{6,2},{1... | collective-permute-start | bytes 7077896 | tf_op jit(solution)/shard_map/ppermute | solution.py:239
  232.2 53.8 %collective-permute-start.13 = (bf16[48,32,768]{2,1,0:T(8,128)(2,1)}, bf16[48,32,768]{2,1,0:T(8,128)(2,1)}, u32[]{:S(2)}, u32[]{:S(2)}) collective-permute-start(bf16[48,32,768]{2,1,0:T(8,128)(2,1)} %shard_map.42.refs_2_.refs_1_), channel_id=1, source_target_pairs={{0,8},{4,12},{8,0},{12,4},{1,9},{5,13},{9,1},{13,5},{2,10},{6,14},... | collective-permute-start | bytes 7077896 | tf_op jit(solution)/shard_map/ppermute | solution.py:239
  232.6 64.3 %collective-permute-start.17 = (bf16[48,32,768]{2,1,0:T(8,128)(2,1)}, bf16[48,32,768]{2,1,0:T(8,128)(2,1)}, u32[]{:S(2)}, u32[]{:S(2)}) collective-permute-start(bf16[48,32,768]{2,1,0:T(8,128)(2,1)} %shard_map.42.refs_2_.refs_1_), channel_id=1, source_target_pairs={{0,4},{4,0},{8,12},{12,8},{1,5},{5,1},{9,13},{13,9},{2,6},{6,2},{1... | collective-permute-start | bytes 7077896 | tf_op jit(solution)/shard_map/ppermute | solution.py:239
  263.8 22.2 %copy-start.2 = (bf16[32,32,768]{2,1,0:T(8,128)(2,1)S(1)}, bf16[32,32,768]{2,1,0:T(8,128)(2,1)}, u32[]{:S(2)}) copy-start(bf16[32,32,768]{2,1,0:T(8,128)(2,1)} %shard_map.43.refs_3_) | copy-start | bytes 4718596
  286.0 10.9 %collective-permute-start.18 = (bf16[48,32,768]{2,1,0:T(8,128)(2,1)}, bf16[48,32,768]{2,1,0:T(8,128)(2,1)}, u32[]{:S(2)}, u32[]{:S(2)}) collective-permute-start(bf16[48,32,768]{2,1,0:T(8,128)(2,1)} %collective-permute-done.13.refs_4_.refs_3_), channel_id=1, source_target_pairs={{0,4},{4,0},{8,12},{12,8},{1,5},{5,1},{9,13},{13,9},{2,6},{6,2},{1... | collective-permute-start | bytes 7077896 | tf_op jit(solution)/shard_map/ppermute | solution.py:239
  286.0 36.9 %collective-permute-start.16 = (bf16[32,32,768]{2,1,0:T(8,128)(2,1)S(1)}, bf16[32,32,768]{2,1,0:T(8,128)(2,1)}, u32[]{:S(2)}, u32[]{:S(2)}) collective-permute-start(bf16[32,32,768]{2,1,0:T(8,128)(2,1)S(1)} %copy-done.2), channel_id=1, source_target_pairs={{0,8},{4,12},{8,0},{12,4},{1,9},{5,13},{9,1},{13,5},{2,10},{6,14},... | collective-permute-start | bytes 4718600 | tf_op jit(solution)/shard_map/ppermute | solution.py:239
  286.7 46.2 %collective-permute-start.19 = (bf16[32,32,768]{2,1,0:T(8,128)(2,1)S(1)}, bf16[32,32,768]{2,1,0:T(8,128)(2,1)}, u32[]{:S(2)}, u32[]{:S(2)}) collective-permute-start(bf16[32,32,768]{2,1,0:T(8,128)(2,1)S(1)} %copy-done.2), channel_id=1, source_target_pairs={{0,4},{4,0},{8,12},{12,8},{1,5},{5,1},{9,13},{13,9},{2,6},{6,2},{1... | collective-permute-start | bytes 4718600 | tf_op jit(solution)/shard_map/ppermute | solution.py:239
  322.9 10.0 %collective-permute-start.20 = (bf16[32,32,768]{2,1,0:T(8,128)(2,1)}, bf16[32,32,768]{2,1,0:T(8,128)(2,1)}, u32[]{:S(2)}, u32[]{:S(2)}) collective-permute-start(bf16[32,32,768]{2,1,0:T(8,128)(2,1)} %collective-permute-done.16.refs_5_), channel_id=1, source_target_pairs={{0,4},{4,0},{8,12},{12,8},{1,5},{5,1},{9,13},{13,9},{2,6},{6,2},{1... | collective-permute-start | bytes 4718600 | tf_op jit(solution)/shard_map/ppermute | solution.py:239
  356.7 2.3 collective-permute-start.21
  357.3 5.5 %collective-permute-start.23 = (f32[64,256]{0,1:T(8,128)S(1)}, f32[64,256]{0,1:T(8,128)S(1)}, u32[]{:S(2)}, u32[]{:S(2)}) collective-permute-start(f32[64,256]{0,1:T(8,128)S(1)} %get-tuple-element.106), channel_id=1, source_target_pairs={{0,12},{4,8},{8,4},{12,0},{1,13},{5,9},{9,5},{13,1},{2,14},{6,10},... | collective-permute-start | bytes 196616 | tf_op jit(solution)/shard_map/ppermute | solution.py:239
  357.4 8.5 %collective-permute-start.22 = (f32[64,256]{0,1:T(8,128)S(1)}, f32[64,256]{0,1:T(8,128)S(1)}, u32[]{:S(2)}, u32[]{:S(2)}) collective-permute-start(f32[64,256]{0,1:T(8,128)S(1)} %get-tuple-element.107), channel_id=1, source_target_pairs={{0,8},{4,12},{8,0},{12,4},{1,9},{5,13},{9,1},{13,5},{2,10},{6,14},... | collective-permute-start | bytes 196616 | tf_op jit(solution)/shard_map/ppermute | solution.py:239
  367.1 9.9 %collective-permute-start.24 = (f32[16,256]{0,1:T(8,128)S(1)}, f32[16,256]{0,1:T(8,128)S(1)}, u32[]{:S(2)}, u32[]{:S(2)}) collective-permute-start(f32[16,256]{0,1:T(8,128)S(1)} %get-tuple-element.108), channel_id=1, source_target_pairs={{0,1},{1,0},{2,3},{3,2},{4,5},{5,4},{6,7},{7,6},{8,9},{9,8},{10,11... | collective-permute-start | bytes 49160 | tf_op jit(solution)/shard_map/ppermute | solution.py:239
  373.5 10.6 %collective-permute-start.26 = (f32[16,256]{0,1:T(8,128)S(1)}, f32[16,256]{0,1:T(8,128)S(1)}, u32[]{:S(2)}, u32[]{:S(2)}) collective-permute-start(f32[16,256]{0,1:T(8,128)S(1)} %get-tuple-element.109), channel_id=1, source_target_pairs={{0,3},{1,2},{2,1},{3,0},{4,7},{5,6},{6,5},{7,4},{8,11},{9,10},{10,... | collective-permute-start | bytes 49160 | tf_op jit(solution)/shard_map/ppermute | solution.py:239
  376.8 11.8 %collective-permute-start.25 = (f32[16,256]{0,1:T(8,128)S(1)}, f32[16,256]{0,1:T(8,128)S(1)}, u32[]{:S(2)}, u32[]{:S(2)}) collective-permute-start(f32[16,256]{0,1:T(8,128)S(1)} %get-tuple-element.110), channel_id=1, source_target_pairs={{0,2},{1,3},{2,0},{3,1},{4,6},{5,7},{6,4},{7,5},{8,10},{9,11},{10,... | collective-permute-start | bytes 49160 | tf_op jit(solution)/shard_map/ppermute | solution.py:239
Sparse Core Ops, SparseCore 0:
  11.6 162.5 all-gather.2
  175.8 61.5 all-gather.4

commit v2 on v1

--- a/solution.py
+++ b/solution.py
@@ -8,7 +8,7 @@
 from jax.experimental.pallas import tpu as pltpu
 from jax.sharding import PartitionSpec as P
 
-CHUNK_SHARES = (2, 4, 2, 3, 3, 2)
+CHUNK_SHARES = (3, 4, 3, 2, 2, 2)
 PIECES = ((0, 8, 0), (0, 4, 1), (4, 4, 1))
 
 
@@ -27,11 +27,10 @@
     slot = lax.rem(step, 2)
     place = place_ref[0]
 
-    def left_copy(k, a, m):
-        rows = pl.ds(pl.multiple_of((place ^ m) * depth, depth), depth)
+    def left_copy(k, a):
         columns = pl.ds(a * span, min(pieces[k][1], 4) * span)
         return pltpu.make_async_copy(
-            left_refs[k].at[rows, columns], left_bufs[k].at[rows, columns], left_sem.at[k, a // 4, m]
+            left_refs[k].at[:, columns], left_bufs[k].at[:, columns], left_sem.at[k, a // 4]
         )
 
     def right_copy(j, offset, to, m):
@@ -60,12 +59,10 @@
         for k, (_, count, _) in enumerate(pieces):
             wide = min(count, 4)
             for a in range(0, count, wide):
+                if first:
+                    left_copy(k, a).wait()
                 product = None
                 for m in range(ranks):
-                    if first and k == 0 and a == 0:
-                        right_copy(0, 0, to, m).wait()
-                    if first:
-                        left_copy(k, a, m).wait()
                     start = pl.multiple_of((place ^ m) * depth, depth)
                     term = jnp.dot(
                         right_buf[to, m].reshape(step_d * width_b, depth),
@@ -94,12 +91,11 @@
 
     @pl.when(step == 0)
     def _():
+        for m in range(ranks):
+            right_copy(0, 0, 0, m).start()
         for k, (_, count, _) in enumerate(pieces):
             for a in range(0, count, 4):
-                for m in range(ranks):
-                    if k == 0 and a == 0:
-                        right_copy(0, 0, 0, m).start()
-                    left_copy(k, a, m).start()
+                left_copy(k, a).start()
         out_ref[...] = total_ref[...]
 
     amp_copy(step, slot).start()
@@ -109,6 +105,9 @@
         def _():
             fetch_right(step + 1, 1 - slot)
 
+    for m in range(ranks):
+        right_copy(0, 0, slot, m).wait()
+
     @pl.when(step == 0)
     def _():
         integrals(0, True)
@@ -117,8 +116,6 @@
 
         @pl.when(step > 0)
         def _():
-            for m in range(ranks):
-                right_copy(0, 0, slot, m).wait()
             amp_copy(0, 1 - slot).wait()
             ladder(1 - slot)
             integrals(slot, False)
@@ -162,7 +159,7 @@
                 pltpu.VMEM((2, ranks, step_d, width_b, depth), jnp.bfloat16),
                 pltpu.VMEM((2, step_d, span * len(halves), pair_count), jnp.bfloat16),
                 pltpu.VMEM((2, count_a * width_b, step_d * span), jnp.bfloat16),
-                pltpu.SemaphoreType.DMA((len(lefts), -(-max(n for _, n, _ in pieces) // 4), ranks)),
+                pltpu.SemaphoreType.DMA((len(lefts), -(-max(n for _, n, _ in pieces) // 4))),
                 pltpu.SemaphoreType.DMA((2, ranks)),
                 pltpu.SemaphoreType.DMA((2,)),
             ],
@@ -239,27 +236,6 @@
     return lax.ppermute(block, axis, [(i, i ^ bit) for i in range(size)])
 
 
-def scatter_sum(total, axis, size):
-    place = lax.axis_index(axis)
-    if size <= 4:
-        rows = total.shape[0] // size
-
-        def share(owner):
-            return lax.dynamic_slice_in_dim(total, owner * rows, rows, 0)
-
-        gives = [share(place ^ mask) for mask in range(1, size)]
-        return sum([swap(give, axis, m + 1, size) for m, give in enumerate(gives)], share(place))
-    bit = size // 2
-    while bit:
-        rows = total.shape[0] // 2
-        mine = (place // bit) % 2
-        keep = lax.dynamic_slice_in_dim(total, mine * rows, rows, 0)
-        give = lax.dynamic_slice_in_dim(total, (1 - mine) * rows, rows, 0)
-        total = keep + swap(give, axis, bit, size)
-        bit //= 2
-    return total
-
-
 def on_device(left_factor, right_factor, amplitudes, *, row_size, col_size):
     width_a = left_factor.shape[1]
     span_c = left_factor.shape[2]
@@ -288,10 +264,7 @@
     owns = [turn(right_factor, starts[0], chunks[0])]
     owns[0], right_factor = together((owns[0], right_factor))
 
-    by_hand = col_size == 4
-    lefts = [lax.all_gather(part, "col", axis=0, tiled=True) for part in (parts[:-1] if by_hand else parts)]
-    round_trip = [parts[-1]]
-    around = [(i, (i + 1) % col_size) for i in range(col_size)]
+    lefts = [lax.all_gather(part, "col", axis=0, tiled=True) for part in parts]
 
     total = jnp.zeros((width_a * width_b, pair_count), jnp.float32)
     rights = [spread({0: owns[0]})]
@@ -299,22 +272,12 @@
         moving = j < len(chunks)
         if moving:
             far = swap(owns[j], "row", far_bit, row_size)
-        if by_hand and j + 1 < col_size:
-            round_trip.append(lax.ppermute(round_trip[-1], "col", around))
         if j == 0:
             owns.append(turn(right_factor, starts[1], chunks[1]))
         if j == 1:
             owns += [turn(right_factor, s, n) for s, n in zip(starts[2:], chunks[2:])]
             owns, amplitudes = together((owns, amplitudes))
             amp = jnp.transpose(amplitudes, (1, 0, 2))
-        if by_hand and j + 1 == col_size:
-            rows = round_trip[0].shape[0]
-            here = lax.axis_index("col")
-            joined = jnp.zeros((col_size * rows, round_trip[0].shape[1]), round_trip[0].dtype)
-            for hop, block in enumerate(round_trip):
-                owner = lax.rem(here - hop + col_size, col_size)
-                joined = lax.dynamic_update_slice_in_dim(joined, block, owner * rows, 0)
-            lefts.append(joined)
         for chosen, js in calls:
             total = add_ladder(
                 place, total, amp, starts[js[0]], span,
@@ -324,28 +287,29 @@
             )
         if moving:
             if j == 0:
-                far, total, owns, round_trip, right_factor, amplitudes = together(
-                    (far, total, owns, round_trip, right_factor, amplitudes)
+                far, total, owns, right_factor, amplitudes = together(
+                    (far, total, owns, right_factor, amplitudes)
                 )
-            elif j + 1 < col_size:
-                far, total, owns, round_trip, amp = together((far, total, owns, round_trip, amp))
+            elif j == 1:
+                far, total, owns, amp, rights = together((far, total, owns, amp, rights))
             else:
                 far, total, owns = together((far, total, owns))
             rights[j] |= spread({far_bit: far})
             if j + 1 < len(chunks):
                 rights.append(spread({0: owns[j + 1]}))
-    total = scatter_sum(total.T, "row", row_size)
-    return scatter_sum(total, "col", col_size)
+    owners = row_size * col_size
+    shares = total.T.reshape(owners, pair_count // owners, width_a * width_b)
+    return lax.all_to_all(shares, ("row", "col"), 0, 0, tiled=True).sum(axis=0)
 
 
 STAGES = (
     (),
     (),
-    (),
-    (((2,), (0, 1)), ((0,), (0, 1, 2))),
-    (((2,), (2,)), ((0, 2), (3,)), ((1,), (0, 1, 2))),
-    (((1,), (3,)), ((0, 2), (4,))),
-    (((1,), (4,)), ((0, 1, 2), (5,))),
+    (((0,), (0, 1)),),
+    (((1,), (0, 1)), ((0,), (2,))),
+    (((1,), (2,)), ((0, 1), (3,)), ((2,), (0,))),
+    (((2,), (1, 2, 3)), ((1, 2), (4,))),
+    (((0,), (4,)), ((0, 1, 2), (5,))),
 )
 
 

time: 403 us -> 373 us (0.926)
  starting transfers between devices: 35.7 us -> 13 us
  waiting for transfers between devices: 112 us -> 96.5 us
  blocking collectives: 0 us -> 14.8 us
  local copies, waits for them, and re-layouts: 35.4 us -> 26.4 us
  Pallas kernels: 199 us -> 205 us
    ppermute x3 -> x0, waiting for transfers between devices: 66.1 us -> none  [on_device(): round_trip.append(lax.ppermute(round_trip[-1], 'col', around))]
    ppermute x24 -> x18, waiting for transfers between devices: 45.4 us -> 96.4 us  [swap(): return lax.ppermute(block, axis, [(i, i ^ bit) for i in range(size)])]
    ppermute x3 -> x0, starting transfers between devices: 15.4 us -> none  [on_device(): round_trip.append(lax.ppermute(round_trip[-1], 'col', around))]
    all_to_all x0 -> x1, blocking collectives: none -> 14.8 us  [on_device(): return lax.all_to_all(shares, ('row', 'col'), 0, 0, tiled=True).sum(axis=0)]
    ppermute x24 -> x18, starting transfers between devices: 20.2 us -> 12.6 us  [swap(): return lax.ppermute(block, axis, [(i, i ^ bit) for i in range(size)])]
    dynamic_update_slice x4 -> x0, local copies, waits for them, and re-layouts: 7.18 us -> none  [on_device(): joined = lax.dynamic_update_slice_in_dim(joined, block, owner * rows, 0)]
    pallas_call x9 -> x10, Pallas kernels: 169 us -> 175 us  [add_ladder(): pl.pallas_call(functools.partial(ladder_kernel, pieces=pieces, chunk_step...]
  transfers between devices with their start and end apart: 29 -> 21, of which waited for: 11 -> 4; matrix products, arithmetic and copies ran while one was open for 8% -> 7% of each run, Pallas kernels for 43% -> 48%
where the time goes in v2:
time: 373 us; the launch traced here: 370 us
  Pallas kernels  205 us (55%)
  waiting for transfers between devices  96.5 us (26%)
  local copies, waits for them, and re-layouts  26.4 us (7%)
  blocking collectives  14.8 us (4%)
  between operations  13.6 us (4%)
  starting transfers between devices  13 us (3%)
    pallas_call x10, Pallas kernels, add_ladder(): pl.pallas_call(functools.partial(ladder_kernel, pieces=pieces, chunk_step...  175 us
    ppermute x18, waiting for transfers between devices, swap(): return lax.ppermute(block, axis, [(i, i ^ bit) for i in range(size)])  96.4 us
    pallas_call x6, Pallas kernels, turn(): pl.pallas_call(turn_kernel, out_shape=jax.ShapeDtypeStruct((size, outer,...  24.7 us
    optimization_barrier x1, local copies, waits for them, and re-layouts, on_device(): owns, amplitudes = together((owns, amplitudes))  23.4 us
    all_to_all x1, blocking collectives, on_device(): return lax.all_to_all(shares, ('row', 'col'), 0, 0, tiled=True).sum(axis=0)  14.8 us
    ppermute x18, starting transfers between devices, swap(): return lax.ppermute(block, axis, [(i, i ^ bit) for i in range(size)])  12.6 us
  transfers between devices with their start and end apart: 21, of which 4 were waited for; matrix products, arithmetic and copies ran while one was open for 7% of the time, Pallas kernels for 48%

profile of v2, /device:TPU:0, one launch (start us, length us, event | category | flops | bytes accessed | tf_op | source)
XLA Modules:
  0.0 370.1 jit_solution(3922850838893371543)
XLA Ops:
  6.5 4.9 %shard_map.37 = (bf16[768,1024]{1,0:T(8,128)(2,1)}, bf16[768,512]{1,0:T(8,128)(2,1)}, bf16[768,512]{1,0:T(8,128)(2,1)}) custom-call(bf16[768,8,256]{2,1,0:T(8,128)(2,1)} %in_ref.1), custom_call_target="tpu_custom_call" | custom-call | bytes 65536 | tf_op jit(solution)/shard_map/pallas_call | solution.py:223
  11.5 0.0 all-gather.4.cloned.1.call-update
  11.5 0.0 all-gather.6.cloned.1.call-start
  11.5 4.7 %shard_map.38.refs_1_ = bf16[48,32,768]{2,1,0:T(8,128)(2,1)} custom-call(bf16[32,256,768]{2,1,0:T(8,128)(2,1)} %in_ref.7), custom_call_target="tpu_custom_call" | custom-call | bytes 65536 | tf_op jit(solution)/shard_map/pallas_call | solution.py:196
  16.2 2.9 collective-permute-start
  19.2 5.5 %shard_map.39.refs_5_.refs_1_ = bf16[64,32,768]{2,1,0:T(8,128)(2,1)} custom-call(bf16[32,256,768]{2,1,0:T(8,128)(2,1)} %in_ref.7), custom_call_target="tpu_custom_call" | custom-call | bytes 65536 | tf_op jit(solution)/shard_map/pallas_call | solution.py:196
  24.7 46.0 %collective-permute-done.refs_3_ = bf16[48,32,768]{2,1,0:T(8,128)(2,1)} collective-permute-done((bf16[48,32,768]{2,1,0:T(8,128)(2,1)}, bf16[48,32,768]{2,1,0:T(8,128)(2,1)}, u32[]{:S(2)}, u32[]{:S(2)}) %collective-permute-start) | collective-permute-done | bytes 2359328 | tf_op jit(solution)/shard_map/ppermute | solution.py:236
  70.7 1.7 collective-permute-start.1
  72.5 0.2 collective-permute-start.2
  72.7 0.3 collective-permute-start.3
  73.0 0.0 all-gather.6.cloned.1.call-update
  73.0 0.3 all-gather.8.cloned.1.call-start
  73.3 3.3 shard_map.43.refs_3_
  76.7 3.3 shard_map.42.refs_2_.refs_1_
  79.9 3.3 shard_map.41.refs_2_.refs_9_
  83.2 4.7 %shard_map.40.refs_1_.refs_5_ = bf16[48,32,768]{2,1,0:T(8,128)(2,1)} custom-call(bf16[32,256,768]{2,1,0:T(8,128)(2,1)} %in_ref.7), custom_call_target="tpu_custom_call" | custom-call | bytes 65536 | tf_op jit(solution)/shard_map/pallas_call | solution.py:196
  87.9 23.4 %copy.18 = bf16[256,256,256]{2,0,1:T(8,128)(2,1)} copy(bf16[256,256,256]{2,1,0:T(8,128)(2,1)} %param.5) | data formatting | bytes 67108864 | tf_op jit(solution)/shard_map/optimization_barrier | solution.py:279
  111.3 0.0 collective-permute-done.2.refs_2_
  111.3 30.2 %collective-permute-done.1.refs_7_.refs_3_ = bf16[64,32,768]{2,1,0:T(8,128)(2,1)} collective-permute-done((bf16[64,32,768]{2,1,0:T(8,128)(2,1)}, bf16[64,32,768]{2,1,0:T(8,128)(2,1)}, u32[]{:S(2)}, u32[]{:S(2)}) %collective-permute-start.1) | collective-permute-done | bytes 3145760 | tf_op jit(solution)/shard_map/ppermute | solution.py:236
  141.6 1.7 collective-permute-start.5
  143.3 0.0 all-gather.8.cloned.1.call-update
  143.3 0.3 collective-permute-start.8
  143.6 3.9 %collective-permute-done.6.refs_8_.refs_4_ = bf16[64,32,768]{2,1,0:T(8,128)(2,1)} collective-permute-done((bf16[64,32,768]{2,1,0:T(8,128)(2,1)}, bf16[64,32,768]{2,1,0:T(8,128)(2,1)}, u32[]{:S(2)}, u32[]{:S(2)}) %collective-permute-start.6) | collective-permute-done | bytes 3145760 | tf_op jit(solution)/shard_map/ppermute | solution.py:236
  147.6 0.7 broadcast_in_dim.3.total_ref
  148.3 31.1 %shard_map.44.total_ref = f32[256,256]{1,0:T(8,128)} custom-call(s32[1]{0:T(128)} %bitcast.place_ref, f32[256,256]{1,0:T(8,128)} %broadcast_in_dim.3.total_ref, bf16[256,256,256]{2,1,0:T(8,128)(2,1)} %bitcast.6, bf16[3072,1024]{1,0:T(8,128)(2,1)} %all-gather.4.cloned.1.call-done.refs_0_, ...), custom_call_target="tpu_custom_call", output_to_operand_aliasing={{}: (1, {})} | custom-call | flops 1221381376 | bytes 28311552 | tf_op jit(solution)/shard_map/pallas_call | solution.py:141
  179.4 16.2 %collective-permute-done.5.refs_3_.refs_7_ = bf16[48,32,768]{2,1,0:T(8,128)(2,1)} collective-permute-done((bf16[48,32,768]{2,1,0:T(8,128)(2,1)}, bf16[48,32,768]{2,1,0:T(8,128)(2,1)}, u32[]{:S(2)}, u32[]{:S(2)}) %collective-permute-start.5) | collective-permute-done | bytes 2359328 | tf_op jit(solution)/shard_map/ppermute | solution.py:236
  195.5 1.7 collective-permute-start.7
  197.3 0.2 collective-permute-start.11
  197.5 19.7 %shard_map.45.total_ref = f32[256,256]{1,0:T(8,128)} custom-call(s32[1]{0:T(128)} %bitcast.place_ref, f32[256,256]{1,0:T(8,128)} %shard_map.44.total_ref, bf16[256,256,256]{2,1,0:T(8,128)(2,1)} %bitcast.7, bf16[3072,512]{1,0:T(8,128)(2,1)} %all-gather.6.cloned.1.call-done.refs_0_.refs_1_, ...), custom_call_target="tpu_custom_call", output_to_operand_aliasing={{}: (1, {})} | custom-call | flops 610690688 | bytes 25165824 | tf_op jit(solution)/shard_map/pallas_call | solution.py:141
  217.2 16.6 %shard_map.46.total_ref = f32[256,256]{1,0:T(8,128)} custom-call(s32[1]{0:T(128)} %bitcast.place_ref, f32[256,256]{1,0:T(8,128)} %shard_map.45.total_ref, bf16[256,256,256]{2,1,0:T(8,128)(2,1)} %bitcast.8, bf16[3072,1024]{1,0:T(8,128)(2,1)} %all-gather.4.cloned.1.call-done.refs_0_, ...), custom_call_target="tpu_custom_call", output_to_operand_aliasing={{}: (1, {})} | custom-call | flops 523449152 | bytes 15728640 | tf_op jit(solution)/shard_map/pallas_call | solution.py:141
  233.9 0.3 collective-permute-start.12
  234.2 0.2 collective-permute-start.10
  234.4 0.2 collective-permute-start.14
  234.6 10.9 %shard_map.47.total_ref = f32[256,256]{1,0:T(8,128)} custom-call(s32[1]{0:T(128)} %bitcast.place_ref, f32[256,256]{1,0:T(8,128)} %shard_map.46.total_ref, bf16[256,256,256]{2,1,0:T(8,128)(2,1)} %bitcast.9, bf16[3072,512]{1,0:T(8,128)(2,1)} %all-gather.6.cloned.1.call-done.refs_0_.refs_1_, ...), custom_call_target="tpu_custom_call", output_to_operand_aliasing={{}: (1, {})} | custom-call | flops 261724576 | bytes 12582912 | tf_op jit(solution)/shard_map/pallas_call | solution.py:141
  245.6 16.3 %shard_map.48.total_ref = f32[256,256]{1,0:T(8,128)} custom-call(s32[1]{0:T(128)} %bitcast.place_ref, f32[256,256]{1,0:T(8,128)} %shard_map.47.total_ref, bf16[256,256,256]{2,1,0:T(8,128)(2,1)} %bitcast.10, bf16[3072,1024]{1,0:T(8,128)(2,1)} %all-gather.4.cloned.1.call-done.refs_0_, ...), custom_call_target="tpu_custom_call", output_to_operand_aliasing={{}: (1, {})} | custom-call | flops 523449152 | bytes 15728640 | tf_op jit(solution)/shard_map/pallas_call | solution.py:141
  261.9 0.0 all-gather.8.cloned.1.call-done.refs_0_.refs_1_.refs_2_
  261.9 10.9 %shard_map.49.total_ref = f32[256,256]{1,0:T(8,128)} custom-call(s32[1]{0:T(128)} %bitcast.place_ref, f32[256,256]{1,0:T(8,128)} %shard_map.48.total_ref, bf16[256,256,256]{2,1,0:T(8,128)(2,1)} %bitcast.11, bf16[3072,512]{1,0:T(8,128)(2,1)} %all-gather.8.cloned.1.call-done.refs_0_.refs_1_.refs_2_, ...), custom_call_target="tpu_custom_call", output_to_operand_aliasing={{}: (1, {})} | custom-call | flops 261724576 | bytes 12582912 | tf_op jit(solution)/shard_map/pallas_call | solution.py:141
  272.8 0.3 collective-permute-start.15
  273.1 1.8 collective-permute-start.13
  274.9 23.6 %shard_map.50.total_ref = f32[256,256]{1,0:T(8,128)} custom-call(s32[1]{0:T(128)} %bitcast.place_ref, f32[256,256]{1,0:T(8,128)} %shard_map.49.total_ref, bf16[256,256,256]{2,1,0:T(8,128)(2,1)} %bitcast.12, bf16[3072,512]{1,0:T(8,128)(2,1)} %all-gather.8.cloned.1.call-done.refs_0_.refs_1_.refs_2_, ...), custom_call_target="tpu_custom_call", output_to_operand_aliasing={{}: (1, {})} | custom-call | flops 785173696 | bytes 31457280 | tf_op jit(solution)/shard_map/pallas_call | solution.py:141
  298.5 12.4 %shard_map.51.total_ref = f32[256,256]{1,0:T(8,128)} custom-call(s32[1]{0:T(128)} %bitcast.place_ref, f32[256,256]{1,0:T(8,128)} %shard_map.50.total_ref, bf16[256,256,256]{2,1,0:T(8,128)(2,1)} %bitcast.13, bf16[3072,512]{1,0:T(8,128)(2,1)} %all-gather.6.cloned.1.call-done.refs_0_.refs_1_, ...), custom_call_target="tpu_custom_call", output_to_operand_aliasing={{}: (1, {})} | custom-call | flops 348966080 | bytes 12582912 | tf_op jit(solution)/shard_map/pallas_call | solution.py:141
  310.9 0.6 collective-permute-start.17
  311.5 12.3 %shard_map.52.total_ref = f32[256,256]{1,0:T(8,128)} custom-call(s32[1]{0:T(128)} %bitcast.place_ref, f32[256,256]{1,0:T(8,128)} %shard_map.51.total_ref, bf16[256,256,256]{2,1,0:T(8,128)(2,1)} %bitcast.14, bf16[3072,1024]{1,0:T(8,128)(2,1)} %all-gather.4.cloned.1.call-done.refs_0_, ...), custom_call_target="tpu_custom_call", output_to_operand_aliasing={{}: (1, {})} | custom-call | flops 348966080 | bytes 12582912 | tf_op jit(solution)/shard_map/pallas_call | solution.py:141
  323.8 1.2 copy-done.1
  325.0 21.8 %shard_map.53 = f32[256,256]{1,0:T(8,128)} custom-call(s32[1]{0:T(128)} %bitcast.place_ref, f32[256,256]{1,0:T(8,128)} %shard_map.52.total_ref, bf16[256,256,256]{2,1,0:T(8,128)(2,1)} %bitcast.15, bf16[3072,1024]{1,0:T(8,128)(2,1)} %all-gather.4.cloned.1.call-done.refs_0_, ...), custom_call_target="tpu_custom_call", output_to_operand_aliasing={{}: (1, {})} | custom-call | flops 697932160 | bytes 18874368 | tf_op jit(solution)/shard_map/pallas_call | solution.py:141
  346.8 1.1 copy.16
  347.8 14.8 %all_to_all.5 = f32[16,16,256]{2,1,0:T(8,128)S(1)} all-to-all(f32[16,16,256]{2,1,0:T(8,128)S(1)} %bitcast.17), channel_id=1, replica_groups=mesh['parts'=2,'row'=4,'col'=4] {'row','col'}, dimensions={0} | all-to-all | bytes 524288 | tf_op jit(solution)/shard_map/all_to_all | solution.py:302
  362.7 0.6 reduce_sum.9
  (23 shorter events, 0.1 us)
Async XLA Ops:
  6.5 141.0 %all-gather.4.cloned.1.call-start = ((), (), s32[]{:S(2)}) async-start(), calls=%async_computation.1 | async-start | bytes 7864320 | tf_op jit(solution)/shard_map/all_gather | solution.py:267
  11.5 186.0 %all-gather.6.cloned.1.call-start = ((), (), s32[]{:S(2)}) async-start(), calls=%async_computation.2 | async-start | bytes 3932160 | tf_op jit(solution)/shard_map/all_gather | solution.py:267
  16.2 54.5 %collective-permute-start = (bf16[48,32,768]{2,1,0:T(8,128)(2,1)}, bf16[48,32,768]{2,1,0:T(8,128)(2,1)}, u32[]{:S(2)}, u32[]{:S(2)}) collective-permute-start(bf16[48,32,768]{2,1,0:T(8,128)(2,1)} %shard_map.38.refs_1_), channel_id=1, source_target_pairs={{0,8},{4,12},{8,0},{12,4},{1,9},{5,13},{9,1},{13,5},{2,10},{6,14},... | collective-permute-start | bytes 7077896 | tf_op jit(solution)/shard_map/ppermute | solution.py:236
  70.7 40.6 %collective-permute-start.4 = (bf16[64,32,768]{2,1,0:T(8,128)(2,1)}, bf16[64,32,768]{2,1,0:T(8,128)(2,1)}, u32[]{:S(2)}, u32[]{:S(2)}) collective-permute-start(bf16[64,32,768]{2,1,0:T(8,128)(2,1)} %shard_map.39.refs_5_.refs_1_), channel_id=1, source_target_pairs={{0,4},{4,0},{8,12},{12,8},{1,5},{5,1},{9,13},{13,9},{2,6},{6,2},{1... | collective-permute-start | bytes 9437192 | tf_op jit(solution)/shard_map/ppermute | solution.py:236
  70.7 70.8 %collective-permute-start.1 = (bf16[64,32,768]{2,1,0:T(8,128)(2,1)}, bf16[64,32,768]{2,1,0:T(8,128)(2,1)}, u32[]{:S(2)}, u32[]{:S(2)}) collective-permute-start(bf16[64,32,768]{2,1,0:T(8,128)(2,1)} %shard_map.39.refs_5_.refs_1_), channel_id=1, source_target_pairs={{0,8},{4,12},{8,0},{12,4},{1,9},{5,13},{9,1},{13,5},{2,10},{6,14},... | collective-permute-start | bytes 9437192 | tf_op jit(solution)/shard_map/ppermute | solution.py:236
  72.5 38.8 %collective-permute-start.2 = (bf16[48,32,768]{2,1,0:T(8,128)(2,1)}, bf16[48,32,768]{2,1,0:T(8,128)(2,1)}, u32[]{:S(2)}, u32[]{:S(2)}) collective-permute-start(bf16[48,32,768]{2,1,0:T(8,128)(2,1)} %shard_map.38.refs_1_), channel_id=1, source_target_pairs={{0,4},{4,0},{8,12},{12,8},{1,5},{5,1},{9,13},{13,9},{2,6},{6,2},{1... | collective-permute-start | bytes 7077896 | tf_op jit(solution)/shard_map/ppermute | solution.py:236
  72.7 38.6 %collective-permute-start.3 = (bf16[48,32,768]{2,1,0:T(8,128)(2,1)}, bf16[48,32,768]{2,1,0:T(8,128)(2,1)}, u32[]{:S(2)}, u32[]{:S(2)}) collective-permute-start(bf16[48,32,768]{2,1,0:T(8,128)(2,1)} %collective-permute-done.refs_3_), channel_id=1, source_target_pairs={{0,4},{4,0},{8,12},{12,8},{1,5},{5,1},{9,13},{13,9},{2,6},{6,2},{1... | collective-permute-start | bytes 7077896 | tf_op jit(solution)/shard_map/ppermute | solution.py:236
  73.0 188.9 %all-gather.8.cloned.1.call-start = ((), (), s32[]{:S(2)}) async-start(), calls=%async_computation.3 | async-start | bytes 3932160 | tf_op jit(solution)/shard_map/all_gather | solution.py:267
  141.6 6.0 %collective-permute-start.6 = (bf16[64,32,768]{2,1,0:T(8,128)(2,1)}, bf16[64,32,768]{2,1,0:T(8,128)(2,1)}, u32[]{:S(2)}, u32[]{:S(2)}) collective-permute-start(bf16[64,32,768]{2,1,0:T(8,128)(2,1)} %collective-permute-done.1.refs_7_.refs_3_), channel_id=1, source_target_pairs={{0,4},{4,0},{8,12},{12,8},{1,5},{5,1},{9,13},{13,9},{2,6},{6,2},{1... | collective-permute-start | bytes 9437192 | tf_op jit(solution)/shard_map/ppermute | solution.py:236
  141.6 54.0 %collective-permute-start.5 = (bf16[48,32,768]{2,1,0:T(8,128)(2,1)}, bf16[48,32,768]{2,1,0:T(8,128)(2,1)}, u32[]{:S(2)}, u32[]{:S(2)}) collective-permute-start(bf16[48,32,768]{2,1,0:T(8,128)(2,1)} %shard_map.40.refs_1_.refs_5_), channel_id=1, source_target_pairs={{0,8},{4,12},{8,0},{12,4},{1,9},{5,13},{9,1},{13,5},{2,10},{6,14},... | collective-permute-start | bytes 7077896 | tf_op jit(solution)/shard_map/ppermute | solution.py:236
  143.3 73.9 %collective-permute-start.8 = (bf16[48,32,768]{2,1,0:T(8,128)(2,1)}, bf16[48,32,768]{2,1,0:T(8,128)(2,1)}, u32[]{:S(2)}, u32[]{:S(2)}) collective-permute-start(bf16[48,32,768]{2,1,0:T(8,128)(2,1)} %shard_map.40.refs_1_.refs_5_), channel_id=1, source_target_pairs={{0,4},{4,0},{8,12},{12,8},{1,5},{5,1},{9,13},{13,9},{2,6},{6,2},{1... | collective-permute-start | bytes 7077896 | tf_op jit(solution)/shard_map/ppermute | solution.py:236
  195.5 21.7 %collective-permute-start.9 = (bf16[48,32,768]{2,1,0:T(8,128)(2,1)}, bf16[48,32,768]{2,1,0:T(8,128)(2,1)}, u32[]{:S(2)}, u32[]{:S(2)}) collective-permute-start(bf16[48,32,768]{2,1,0:T(8,128)(2,1)} %collective-permute-done.5.refs_3_.refs_7_), channel_id=1, source_target_pairs={{0,4},{4,0},{8,12},{12,8},{1,5},{5,1},{9,13},{13,9},{2,6},{6,2},{1... | collective-permute-start | bytes 7077896 | tf_op jit(solution)/shard_map/ppermute | solution.py:236
  195.5 38.3 %collective-permute-start.7 = (bf16[32,32,768]{2,1,0:T(8,128)(2,1)}, bf16[32,32,768]{2,1,0:T(8,128)(2,1)}, u32[]{:S(2)}, u32[]{:S(2)}) collective-permute-start(bf16[32,32,768]{2,1,0:T(8,128)(2,1)} %shard_map.41.refs_2_.refs_9_), channel_id=1, source_target_pairs={{0,8},{4,12},{8,0},{12,4},{1,9},{5,13},{9,1},{13,5},{2,10},{6,14},... | collective-permute-start | bytes 4718600 | tf_op jit(solution)/shard_map/ppermute | solution.py:236
  197.3 48.3 %collective-permute-start.11 = (bf16[32,32,768]{2,1,0:T(8,128)(2,1)}, bf16[32,32,768]{2,1,0:T(8,128)(2,1)}, u32[]{:S(2)}, u32[]{:S(2)}) collective-permute-start(bf16[32,32,768]{2,1,0:T(8,128)(2,1)} %shard_map.41.refs_2_.refs_9_), channel_id=1, source_target_pairs={{0,4},{4,0},{8,12},{12,8},{1,5},{5,1},{9,13},{13,9},{2,6},{6,2},{1... | collective-permute-start | bytes 4718600 | tf_op jit(solution)/shard_map/ppermute | solution.py:236
  217.2 17.0 %copy-start = (bf16[32,32,768]{2,1,0:T(8,128)(2,1)S(1)}, bf16[32,32,768]{2,1,0:T(8,128)(2,1)}, u32[]{:S(2)}) copy-start(bf16[32,32,768]{2,1,0:T(8,128)(2,1)} %shard_map.42.refs_2_.refs_1_) | copy-start | bytes 4718596
  233.9 11.7 %collective-permute-start.12 = (bf16[32,32,768]{2,1,0:T(8,128)(2,1)}, bf16[32,32,768]{2,1,0:T(8,128)(2,1)}, u32[]{:S(2)}, u32[]{:S(2)}) collective-permute-start(bf16[32,32,768]{2,1,0:T(8,128)(2,1)} %collective-permute-done.7.refs_4_.refs_11_), channel_id=1, source_target_pairs={{0,4},{4,0},{8,12},{12,8},{1,5},{5,1},{9,13},{13,9},{2,6},{6,2},{1... | collective-permute-start | bytes 4718600 | tf_op jit(solution)/shard_map/ppermute | solution.py:236
  234.2 38.6 %collective-permute-start.10 = (bf16[32,32,768]{2,1,0:T(8,128)(2,1)S(1)}, bf16[32,32,768]{2,1,0:T(8,128)(2,1)}, u32[]{:S(2)}, u32[]{:S(2)}) collective-permute-start(bf16[32,32,768]{2,1,0:T(8,128)(2,1)S(1)} %copy-done), channel_id=1, source_target_pairs={{0,8},{4,12},{8,0},{12,4},{1,9},{5,13},{9,1},{13,5},{2,10},{6,14},... | collective-permute-start | bytes 4718600 | tf_op jit(solution)/shard_map/ppermute | solution.py:236
  234.4 64.1 %collective-permute-start.14 = (bf16[32,32,768]{2,1,0:T(8,128)(2,1)S(1)}, bf16[32,32,768]{2,1,0:T(8,128)(2,1)}, u32[]{:S(2)}, u32[]{:S(2)}) collective-permute-start(bf16[32,32,768]{2,1,0:T(8,128)(2,1)S(1)} %copy-done), channel_id=1, source_target_pairs={{0,4},{4,0},{8,12},{12,8},{1,5},{5,1},{9,13},{13,9},{2,6},{6,2},{1... | collective-permute-start | bytes 4718600 | tf_op jit(solution)/shard_map/ppermute | solution.py:236
  272.8 25.7 %collective-permute-start.15 = (bf16[32,32,768]{2,1,0:T(8,128)(2,1)}, bf16[32,32,768]{2,1,0:T(8,128)(2,1)}, u32[]{:S(2)}, u32[]{:S(2)}) collective-permute-start(bf16[32,32,768]{2,1,0:T(8,128)(2,1)} %collective-permute-done.10.refs_4_.refs_3_), channel_id=1, source_target_pairs={{0,4},{4,0},{8,12},{12,8},{1,5},{5,1},{9,13},{13,9},{2,6},{6,2},{1... | collective-permute-start | bytes 4718600 | tf_op jit(solution)/shard_map/ppermute | solution.py:236
  273.1 37.8 %collective-permute-start.13 = (bf16[32,32,768]{2,1,0:T(8,128)(2,1)}, bf16[32,32,768]{2,1,0:T(8,128)(2,1)}, u32[]{:S(2)}, u32[]{:S(2)}) collective-permute-start(bf16[32,32,768]{2,1,0:T(8,128)(2,1)} %shard_map.43.refs_3_), channel_id=1, source_target_pairs={{0,8},{4,12},{8,0},{12,4},{1,9},{5,13},{9,1},{13,5},{2,10},{6,14},... | collective-permute-start | bytes 4718600 | tf_op jit(solution)/shard_map/ppermute | solution.py:236
  274.9 48.9 %collective-permute-start.16 = (bf16[32,32,768]{2,1,0:T(8,128)(2,1)}, bf16[32,32,768]{2,1,0:T(8,128)(2,1)}, u32[]{:S(2)}, u32[]{:S(2)}) collective-permute-start(bf16[32,32,768]{2,1,0:T(8,128)(2,1)} %shard_map.43.refs_3_), channel_id=1, source_target_pairs={{0,4},{4,0},{8,12},{12,8},{1,5},{5,1},{9,13},{13,9},{2,6},{6,2},{1... | collective-permute-start | bytes 4718600 | tf_op jit(solution)/shard_map/ppermute | solution.py:236
  310.9 12.9 %collective-permute-start.17 = (bf16[32,32,768]{2,1,0:T(8,128)(2,1)}, bf16[32,32,768]{2,1,0:T(8,128)(2,1)S(1)}, u32[]{:S(2)}, u32[]{:S(2)}) collective-permute-start(bf16[32,32,768]{2,1,0:T(8,128)(2,1)} %collective-permute-done.13.refs_5_), channel_id=1, source_target_pairs={{0,4},{4,0},{8,12},{12,8},{1,5},{5,1},{9,13},{13,9},{2,6},{6,2},{1... | collective-permute-start | bytes 4718600 | tf_op jit(solution)/shard_map/ppermute | solution.py:236
  323.8 1.2 copy-start.1
Sparse Core Ops, SparseCore 0:
  11.6 118.0 all-gather.3
  131.3 61.7 all-gather.5
  194.6 62.1 all-gather.7

commit v3 on v2

--- a/solution.py
+++ b/solution.py
@@ -8,7 +8,7 @@
 from jax.experimental.pallas import tpu as pltpu
 from jax.sharding import PartitionSpec as P
 
-CHUNK_SHARES = (3, 4, 3, 2, 2, 2)
+CHUNK_SHARES = (2, 3, 3, 2, 2, 2, 2)
 PIECES = ((0, 8, 0), (0, 4, 1), (4, 4, 1))
 
 
@@ -18,7 +18,7 @@
     out_ref = refs[count_l + count_r]
     rest = refs[count_l + count_r + 1 :]
     left_bufs = rest[:count_l]
-    right_buf, amp_buf, integral_ref, left_sem, right_sem, amp_sem = rest[count_l:]
+    right_buf, amp_buf, integral_ref, left_sem, right_sem, amp_sem, total_sem = rest[count_l:]
     _, _, step_d, width_b, depth = right_buf.shape
     steps = sum(chunk_steps)
     halves = sorted({half for _, _, half in pieces})
@@ -27,11 +27,19 @@
     slot = lax.rem(step, 2)
     place = place_ref[0]
 
-    def left_copy(k, a):
+    def left_copies(k, a):
         columns = pl.ds(a * span, min(pieces[k][1], 4) * span)
-        return pltpu.make_async_copy(
-            left_refs[k].at[:, columns], left_bufs[k].at[:, columns], left_sem.at[k, a // 4]
-        )
+        return [
+            pltpu.make_async_copy(
+                left_refs[k].at[pl.ds(m * depth, depth), columns],
+                left_bufs[k].at[pl.ds(m * depth, depth), columns],
+                left_sem.at[k, a // 4, m],
+            )
+            for m in range(ranks)
+        ]
+
+    def total_copy():
+        return pltpu.make_async_copy(total_ref, out_ref, total_sem)
 
     def right_copy(j, offset, to, m):
         source = right_refs[j * ranks + m].at[pl.ds(offset * step_d, step_d)]
@@ -60,7 +68,8 @@
             wide = min(count, 4)
             for a in range(0, count, wide):
                 if first:
-                    left_copy(k, a).wait()
+                    for copy in left_copies(k, a):
+                        copy.wait()
                 product = None
                 for m in range(ranks):
                     start = pl.multiple_of((place ^ m) * depth, depth)
@@ -95,8 +104,9 @@
             right_copy(0, 0, 0, m).start()
         for k, (_, count, _) in enumerate(pieces):
             for a in range(0, count, 4):
-                left_copy(k, a).start()
-        out_ref[...] = total_ref[...]
+                for copy in left_copies(k, a):
+                    copy.start()
+        total_copy().start()
 
     amp_copy(step, slot).start()
     if steps > 1:
@@ -111,6 +121,7 @@
     @pl.when(step == 0)
     def _():
         integrals(0, True)
+        total_copy().wait()
 
     if steps > 1:
 
@@ -151,17 +162,17 @@
         grid_spec=pltpu.PrefetchScalarGridSpec(
             num_scalar_prefetch=1,
             grid=(steps,),
-            in_specs=[pl.BlockSpec(total.shape, lambda s, _: (0, 0))]
-            + [anywhere] * (1 + len(lefts) + len(blocks)),
+            in_specs=[anywhere] * (2 + len(lefts) + len(blocks)),
             out_specs=pl.BlockSpec(total.shape, lambda s, _: (0, 0)),
             scratch_shapes=[pltpu.VMEM(x.shape, x.dtype) for x in lefts]
             + [
                 pltpu.VMEM((2, ranks, step_d, width_b, depth), jnp.bfloat16),
                 pltpu.VMEM((2, step_d, span * len(halves), pair_count), jnp.bfloat16),
                 pltpu.VMEM((2, count_a * width_b, step_d * span), jnp.bfloat16),
-                pltpu.SemaphoreType.DMA((len(lefts), -(-max(n for _, n, _ in pieces) // 4))),
+                pltpu.SemaphoreType.DMA((len(lefts), -(-max(n for _, n, _ in pieces) // 4), ranks)),
                 pltpu.SemaphoreType.DMA((2, ranks)),
                 pltpu.SemaphoreType.DMA((2,)),
+                pltpu.SemaphoreType.DMA(()),
             ],
         ),
         input_output_aliases={1: 0},
@@ -306,10 +317,11 @@
     (),
     (),
     (((0,), (0, 1)),),
-    (((1,), (0, 1)), ((0,), (2,))),
-    (((1,), (2,)), ((0, 1), (3,)), ((2,), (0,))),
-    (((2,), (1, 2, 3)), ((1, 2), (4,))),
-    (((0,), (4,)), ((0, 1, 2), (5,))),
+    (((0,), (2,)),),
+    (((1,), (0, 1, 2)), ((0, 1), (3,))),
+    (((0, 1), (4,)), ((2,), (0, 1))),
+    (((2,), (2, 3)), ((0, 1, 2), (5,))),
+    (((2,), (4,)), ((0, 1, 2), (6,))),
 )
 
 

time: 373 us -> 369 us (0.989)
    ppermute x18 -> x21, waiting for transfers between devices: 96.4 us -> 75.8 us  [swap(): return lax.ppermute(block, axis, [(i, i ^ bit) for i in range(size)])]
    all_gather x3, waiting for transfers between devices: 0.02 us -> 18.3 us  [on_device(): lefts = [lax.all_gather(part, 'col', axis=0, tiled=True) for part in parts]]
    pallas_call x6 -> x7, Pallas kernels: 24.7 us -> 25.8 us  [turn(): pl.pallas_call(turn_kernel, out_shape=jax.ShapeDtypeStruct((size, outer,...]
    ppermute x18 -> x21, starting transfers between devices: 12.6 us -> 12.1 us  [swap(): return lax.ppermute(block, axis, [(i, i ^ bit) for i in range(size)])]
  transfers between devices with their start and end apart: 21 -> 24, of which waited for: 4 -> 10; matrix products, arithmetic and copies ran while one was open for 7% -> 7% of each run, Pallas kernels for 48% -> 49%
where the time goes in v3:
time: 369 us; the launch traced here: 366 us
  Pallas kernels  204 us (55%)
  waiting for transfers between devices  94.1 us (26%)
  local copies, waits for them, and re-layouts  25.3 us (7%)
  blocking collectives  15.8 us (4%)
  between operations  13.8 us (4%)
  starting transfers between devices  12.4 us (3%)
    pallas_call x10, Pallas kernels, add_ladder(): pl.pallas_call(functools.partial(ladder_kernel, pieces=pieces, chunk_step...  173 us
    ppermute x21, waiting for transfers between devices, swap(): return lax.ppermute(block, axis, [(i, i ^ bit) for i in range(size)])  75.8 us
    pallas_call x7, Pallas kernels, turn(): pl.pallas_call(turn_kernel, out_shape=jax.ShapeDtypeStruct((size, outer,...  25.8 us
    optimization_barrier x1, local copies, waits for them, and re-layouts, on_device(): owns, amplitudes = together((owns, amplitudes))  23.5 us
    all_gather x3, waiting for transfers between devices, on_device(): lefts = [lax.all_gather(part, 'col', axis=0, tiled=True) for part in parts]  18.3 us
    all_to_all x1, blocking collectives, on_device(): return lax.all_to_all(shares, ('row', 'col'), 0, 0, tiled=True).sum(axis=0)  15.8 us
    ppermute x21, starting transfers between devices, swap(): return lax.ppermute(block, axis, [(i, i ^ bit) for i in range(size)])  12.1 us
  transfers between devices with their start and end apart: 24, of which 10 were waited for; matrix products, arithmetic and copies ran while one was open for 7% of the time, Pallas kernels for 49%

profile of v3, /device:TPU:0, one launch (start us, length us, event | category | flops | bytes accessed | tf_op | source)
XLA Modules:
  0.0 365.7 jit_solution(10290397202350581207)
XLA Ops:
  6.5 4.9 %shard_map.37 = (bf16[768,1024]{1,0:T(8,128)(2,1)}, bf16[768,512]{1,0:T(8,128)(2,1)}, bf16[768,512]{1,0:T(8,128)(2,1)}) custom-call(bf16[768,8,256]{2,1,0:T(8,128)(2,1)} %in_ref.1), custom_call_target="tpu_custom_call" | custom-call | bytes 65536 | tf_op jit(solution)/shard_map/pallas_call | solution.py:234
  11.5 3.3 shard_map.38.refs_1_
  14.9 2.9 collective-permute-start
  17.8 4.7 %shard_map.39.refs_5_ = bf16[48,32,768]{2,1,0:T(8,128)(2,1)} custom-call(bf16[32,256,768]{2,1,0:T(8,128)(2,1)} %in_ref.8), custom_call_target="tpu_custom_call" | custom-call | bytes 65536 | tf_op jit(solution)/shard_map/pallas_call | solution.py:207
  22.5 30.1 %collective-permute-done.refs_3_ = bf16[32,32,768]{2,1,0:T(8,128)(2,1)} collective-permute-done((bf16[32,32,768]{2,1,0:T(8,128)(2,1)}, bf16[32,32,768]{2,1,0:T(8,128)(2,1)}, u32[]{:S(2)}, u32[]{:S(2)}) %collective-permute-start) | collective-permute-done | bytes 1572896 | tf_op jit(solution)/shard_map/ppermute | solution.py:247
  52.6 1.7 collective-permute-start.1
  54.3 0.2 collective-permute-start.2
  54.5 0.3 collective-permute-start.3
  54.8 0.3 all-gather.8.cloned.1.call-start
  55.1 3.3 shard_map.44.refs_3_
  58.4 3.3 shard_map.43.refs_3_
  61.6 3.3 shard_map.42.refs_2_.refs_1_
  64.9 3.2 shard_map.41.refs_2_.refs_5_
  68.2 4.7 %shard_map.40.refs_1_.refs_9_ = bf16[48,32,768]{2,1,0:T(8,128)(2,1)} custom-call(bf16[32,256,768]{2,1,0:T(8,128)(2,1)} %in_ref.8), custom_call_target="tpu_custom_call" | custom-call | bytes 65536 | tf_op jit(solution)/shard_map/pallas_call | solution.py:207
  72.8 23.5 %copy.18 = bf16[256,256,256]{2,0,1:T(8,128)(2,1)} copy(bf16[256,256,256]{2,1,0:T(8,128)(2,1)} %param.5) | data formatting | bytes 67108864 | tf_op jit(solution)/shard_map/optimization_barrier | solution.py:290
  96.3 10.3 %collective-permute-done.1.refs_7_ = bf16[48,32,768]{2,1,0:T(8,128)(2,1)} collective-permute-done((bf16[48,32,768]{2,1,0:T(8,128)(2,1)}, bf16[48,32,768]{2,1,0:T(8,128)(2,1)}, u32[]{:S(2)}, u32[]{:S(2)}) %collective-permute-start.1) | collective-permute-done | bytes 2359328 | tf_op jit(solution)/shard_map/ppermute | solution.py:247
  106.6 1.7 collective-permute-start.5
  108.3 0.2 collective-permute-start.8
  108.5 3.0 collective-permute-done.6.refs_8_
  111.5 18.2 %all-gather.4.cloned.1.call-done.refs_0_ = bf16[3072,1024]{1,0:T(8,128)(2,1)} async-done(((bf16[768,1024]{1,0:T(8,128)(2,1)}), bf16[3072,1024]{1,0:T(8,128)(2,1)}) %all-gather.4.cloned.1.call-update) | async-done | bytes 6291472 | tf_op jit(solution)/shard_map/all_gather | solution.py:278
  129.7 0.7 broadcast_in_dim.3.total_ref
  130.4 23.4 %shard_map.45.total_ref = f32[256,256]{1,0:T(8,128)} custom-call(s32[1]{0:T(128)} %bitcast.place_ref, f32[256,256]{1,0:T(8,128)} %broadcast_in_dim.3.total_ref, bf16[256,256,256]{2,1,0:T(8,128)(2,1)} %bitcast.6, bf16[3072,1024]{1,0:T(8,128)(2,1)} %all-gather.4.cloned.1.call-done.refs_0_, ...), custom_call_target="tpu_custom_call", output_to_operand_aliasing={{}: (1, {})} | custom-call | flops 872415232 | bytes 22020096 | tf_op jit(solution)/shard_map/pallas_call | solution.py:152
  153.9 6.7 %collective-permute-done.5.refs_3_.refs_11_ = bf16[48,32,768]{2,1,0:T(8,128)(2,1)} collective-permute-done((bf16[48,32,768]{2,1,0:T(8,128)(2,1)}, bf16[48,32,768]{2,1,0:T(8,128)(2,1)}, u32[]{:S(2)}, u32[]{:S(2)}) %collective-permute-start.5) | collective-permute-done | bytes 2359328 | tf_op jit(solution)/shard_map/ppermute | solution.py:247
  160.6 1.7 collective-permute-start.7
  162.3 0.3 collective-permute-start.11
  162.6 2.9 collective-permute-done.9.refs_4_.refs_12_
  165.4 15.4 %shard_map.46.total_ref = f32[256,256]{1,0:T(8,128)} custom-call(s32[1]{0:T(128)} %bitcast.place_ref, f32[256,256]{1,0:T(8,128)} %shard_map.45.total_ref, bf16[256,256,256]{2,1,0:T(8,128)(2,1)} %bitcast.7, bf16[3072,1024]{1,0:T(8,128)(2,1)} %all-gather.4.cloned.1.call-done.refs_0_, ...), custom_call_target="tpu_custom_call", output_to_operand_aliasing={{}: (1, {})} | custom-call | flops 523449152 | bytes 15728640 | tf_op jit(solution)/shard_map/pallas_call | solution.py:152
  180.9 16.8 %collective-permute-done.7.refs_4_.refs_7_ = bf16[32,32,768]{2,1,0:T(8,128)(2,1)} collective-permute-done((bf16[32,32,768]{2,1,0:T(8,128)(2,1)}, bf16[32,32,768]{2,1,0:T(8,128)(2,1)}, u32[]{:S(2)}, u32[]{:S(2)}) %collective-permute-start.7) | collective-permute-done | bytes 1572896 | tf_op jit(solution)/shard_map/ppermute | solution.py:247
  197.7 1.7 collective-permute-start.10
  199.4 0.2 collective-permute-start.14
  199.6 21.8 %shard_map.47.total_ref = f32[256,256]{1,0:T(8,128)} custom-call(s32[1]{0:T(128)} %bitcast.place_ref, f32[256,256]{1,0:T(8,128)} %shard_map.46.total_ref, bf16[256,256,256]{2,1,0:T(8,128)(2,1)} %bitcast.8, bf16[3072,512]{1,0:T(8,128)(2,1)} %all-gather.6.cloned.1.call-done.refs_0_.refs_1_, ...), custom_call_target="tpu_custom_call", output_to_operand_aliasing={{}: (1, {})} | custom-call | flops 697932160 | bytes 28311552 | tf_op jit(solution)/shard_map/pallas_call | solution.py:152
  221.5 16.4 %shard_map.48.total_ref = f32[256,256]{1,0:T(8,128)} custom-call(s32[1]{0:T(128)} %bitcast.place_ref, f32[256,256]{1,0:T(8,128)} %shard_map.47.total_ref, bf16[256,256,256]{2,1,0:T(8,128)(2,1)} %bitcast.9, bf16[3072,1024]{1,0:T(8,128)(2,1)} %all-gather.4.cloned.1.call-done.refs_0_, ...), custom_call_target="tpu_custom_call", output_to_operand_aliasing={{}: (1, {})} | custom-call | flops 523449152 | bytes 15728640 | tf_op jit(solution)/shard_map/pallas_call | solution.py:152
  237.9 0.3 collective-permute-start.15
  238.3 0.3 collective-permute-start.13
  238.6 3.2 collective-permute-done.15.refs_5_.refs_4_
  241.7 16.1 %shard_map.49.total_ref = f32[256,256]{1,0:T(8,128)} custom-call(s32[1]{0:T(128)} %bitcast.place_ref, f32[256,256]{1,0:T(8,128)} %shard_map.48.total_ref, bf16[256,256,256]{2,1,0:T(8,128)(2,1)} %bitcast.10, bf16[3072,1024]{1,0:T(8,128)(2,1)} %all-gather.4.cloned.1.call-done.refs_0_, ...), custom_call_target="tpu_custom_call", output_to_operand_aliasing={{}: (1, {})} | custom-call | flops 523449152 | bytes 15728640 | tf_op jit(solution)/shard_map/pallas_call | solution.py:152
  257.8 15.0 %shard_map.50.total_ref = f32[256,256]{1,0:T(8,128)} custom-call(s32[1]{0:T(128)} %bitcast.place_ref, f32[256,256]{1,0:T(8,128)} %shard_map.49.total_ref, bf16[256,256,256]{2,1,0:T(8,128)(2,1)} %bitcast.11, bf16[3072,512]{1,0:T(8,128)(2,1)} %all-gather.8.cloned.1.call-done.refs_0_.refs_2_, ...), custom_call_target="tpu_custom_call", output_to_operand_aliasing={{}: (1, {})} | custom-call | flops 436207616 | bytes 18874368 | tf_op jit(solution)/shard_map/pallas_call | solution.py:152
  272.9 2.2 collective-permute-done.13.refs_5_
  275.1 0.3 collective-permute-start.16
  275.4 0.2 collective-permute-start.19
  275.6 15.1 %shard_map.51.total_ref = f32[256,256]{1,0:T(8,128)} custom-call(s32[1]{0:T(128)} %bitcast.place_ref, f32[256,256]{1,0:T(8,128)} %shard_map.50.total_ref, bf16[256,256,256]{2,1,0:T(8,128)(2,1)} %bitcast.12, bf16[3072,512]{1,0:T(8,128)(2,1)} %all-gather.8.cloned.1.call-done.refs_0_.refs_2_, ...), custom_call_target="tpu_custom_call", output_to_operand_aliasing={{}: (1, {})} | custom-call | flops 436207616 | bytes 18874368 | tf_op jit(solution)/shard_map/pallas_call | solution.py:152
  290.7 20.6 %shard_map.52.total_ref = f32[256,256]{1,0:T(8,128)} custom-call(s32[1]{0:T(128)} %bitcast.place_ref, f32[256,256]{1,0:T(8,128)} %shard_map.51.total_ref, bf16[256,256,256]{2,1,0:T(8,128)(2,1)} %bitcast.13, bf16[3072,1024]{1,0:T(8,128)(2,1)} %all-gather.4.cloned.1.call-done.refs_0_, ...), custom_call_target="tpu_custom_call", output_to_operand_aliasing={{}: (1, {})} | custom-call | flops 697932160 | bytes 18874368 | tf_op jit(solution)/shard_map/pallas_call | solution.py:152
  311.3 0.7 collective-permute-done.16.refs_5_
  312.0 8.6 %shard_map.53.total_ref = f32[256,256]{1,0:T(8,128)} custom-call(s32[1]{0:T(128)} %bitcast.place_ref, f32[256,256]{1,0:T(8,128)} %shard_map.52.total_ref, bf16[256,256,256]{2,1,0:T(8,128)(2,1)} %bitcast.14, bf16[3072,512]{1,0:T(8,128)(2,1)} %all-gather.8.cloned.1.call-done.refs_0_.refs_2_, ...), custom_call_target="tpu_custom_call", output_to_operand_aliasing={{}: (1, {})} | custom-call | flops 174483040 | bytes 9437184 | tf_op jit(solution)/shard_map/pallas_call | solution.py:152
  320.7 20.6 %shard_map.54 = f32[256,256]{1,0:T(8,128)} custom-call(s32[1]{0:T(128)} %bitcast.place_ref, f32[256,256]{1,0:T(8,128)} %shard_map.53.total_ref, bf16[256,256,256]{2,1,0:T(8,128)(2,1)} %bitcast.15, bf16[3072,1024]{1,0:T(8,128)(2,1)} %all-gather.4.cloned.1.call-done.refs_0_, ...), custom_call_target="tpu_custom_call", output_to_operand_aliasing={{}: (1, {})} | custom-call | flops 697932160 | bytes 18874368 | tf_op jit(solution)/shard_map/pallas_call | solution.py:152
  341.3 1.1 copy.16
  342.4 15.8 %all_to_all.5 = f32[16,16,256]{2,1,0:T(8,128)S(1)} all-to-all(f32[16,16,256]{2,1,0:T(8,128)S(1)} %bitcast.17), channel_id=1, replica_groups=mesh['parts'=2,'row'=4,'col'=4] {'row','col'}, dimensions={0} | all-to-all | bytes 524288 | tf_op jit(solution)/shard_map/all_to_all | solution.py:313
  358.1 0.6 reduce_sum.9
  (32 shorter events, 0.2 us)
Async XLA Ops:
  6.5 123.2 %all-gather.4.cloned.1.call-start = ((), (), s32[]{:S(2)}) async-start(), calls=%async_computation.1 | async-start | bytes 7864320 | tf_op jit(solution)/shard_map/all_gather | solution.py:278
  11.5 188.1 %all-gather.6.cloned.1.call-start = ((), (), s32[]{:S(2)}) async-start(), calls=%async_computation.2 | async-start | bytes 3932160 | tf_op jit(solution)/shard_map/all_gather | solution.py:278
  14.9 39.4 %copy-start = (bf16[32,32,768]{2,1,0:T(8,128)(2,1)S(1)}, bf16[32,32,768]{2,1,0:T(8,128)(2,1)}, u32[]{:S(2)}) copy-start(bf16[32,32,768]{2,1,0:T(8,128)(2,1)} %shard_map.38.refs_1_) | copy-start | bytes 4718596
  14.9 37.7 %collective-permute-start = (bf16[32,32,768]{2,1,0:T(8,128)(2,1)}, bf16[32,32,768]{2,1,0:T(8,128)(2,1)}, u32[]{:S(2)}, u32[]{:S(2)}) collective-permute-start(bf16[32,32,768]{2,1,0:T(8,128)(2,1)} %shard_map.38.refs_1_), channel_id=1, source_target_pairs={{0,8},{4,12},{8,0},{12,4},{1,9},{5,13},{9,1},{13,5},{2,10},{6,14},... | collective-permute-start | bytes 4718600 | tf_op jit(solution)/shard_map/ppermute | solution.py:247
  52.6 43.7 %collective-permute-start.4 = (bf16[48,32,768]{2,1,0:T(8,128)(2,1)}, bf16[48,32,768]{2,1,0:T(8,128)(2,1)}, u32[]{:S(2)}, u32[]{:S(2)}) collective-permute-start(bf16[48,32,768]{2,1,0:T(8,128)(2,1)} %shard_map.39.refs_5_), channel_id=1, source_target_pairs={{0,4},{4,0},{8,12},{12,8},{1,5},{5,1},{9,13},{13,9},{2,6},{6,2},{1... | collective-permute-start | bytes 7077896 | tf_op jit(solution)/shard_map/ppermute | solution.py:247
  52.6 54.0 %collective-permute-start.1 = (bf16[48,32,768]{2,1,0:T(8,128)(2,1)}, bf16[48,32,768]{2,1,0:T(8,128)(2,1)}, u32[]{:S(2)}, u32[]{:S(2)}) collective-permute-start(bf16[48,32,768]{2,1,0:T(8,128)(2,1)} %shard_map.39.refs_5_), channel_id=1, source_target_pairs={{0,8},{4,12},{8,0},{12,4},{1,9},{5,13},{9,1},{13,5},{2,10},{6,14},... | collective-permute-start | bytes 7077896 | tf_op jit(solution)/shard_map/ppermute | solution.py:247
  54.3 42.0 %collective-permute-start.2 = (bf16[32,32,768]{2,1,0:T(8,128)(2,1)S(1)}, bf16[32,32,768]{2,1,0:T(8,128)(2,1)}, u32[]{:S(2)}, u32[]{:S(2)}) collective-permute-start(bf16[32,32,768]{2,1,0:T(8,128)(2,1)S(1)} %copy-done), channel_id=1, source_target_pairs={{0,4},{4,0},{8,12},{12,8},{1,5},{5,1},{9,13},{13,9},{2,6},{6,2},{1... | collective-permute-start | bytes 4718600 | tf_op jit(solution)/shard_map/ppermute | solution.py:247
  54.5 41.8 %collective-permute-start.3 = (bf16[32,32,768]{2,1,0:T(8,128)(2,1)}, bf16[32,32,768]{2,1,0:T(8,128)(2,1)}, u32[]{:S(2)}, u32[]{:S(2)}) collective-permute-start(bf16[32,32,768]{2,1,0:T(8,128)(2,1)} %collective-permute-done.refs_3_), channel_id=1, source_target_pairs={{0,4},{4,0},{8,12},{12,8},{1,5},{5,1},{9,13},{13,9},{2,6},{6,2},{1... | collective-permute-start | bytes 4718600 | tf_op jit(solution)/shard_map/ppermute | solution.py:247
  54.8 203.0 %all-gather.8.cloned.1.call-start = ((), (), s32[]{:S(2)}) async-start(), calls=%async_computation.3 | async-start | bytes 3932160 | tf_op jit(solution)/shard_map/all_gather | solution.py:278
  106.6 4.9 %collective-permute-start.6 = (bf16[48,32,768]{2,1,0:T(8,128)(2,1)}, bf16[48,32,768]{2,1,0:T(8,128)(2,1)}, u32[]{:S(2)}, u32[]{:S(2)}) collective-permute-start(bf16[48,32,768]{2,1,0:T(8,128)(2,1)} %collective-permute-done.1.refs_7_), channel_id=1, source_target_pairs={{0,4},{4,0},{8,12},{12,8},{1,5},{5,1},{9,13},{13,9},{2,6},{6,2},{1... | collective-permute-start | bytes 7077896 | tf_op jit(solution)/shard_map/ppermute | solution.py:247
  106.6 54.0 %collective-permute-start.5 = (bf16[48,32,768]{2,1,0:T(8,128)(2,1)}, bf16[48,32,768]{2,1,0:T(8,128)(2,1)}, u32[]{:S(2)}, u32[]{:S(2)}) collective-permute-start(bf16[48,32,768]{2,1,0:T(8,128)(2,1)} %shard_map.40.refs_1_.refs_9_), channel_id=1, source_target_pairs={{0,8},{4,12},{8,0},{12,4},{1,9},{5,13},{9,1},{13,5},{2,10},{6,14},... | collective-permute-start | bytes 7077896 | tf_op jit(solution)/shard_map/ppermute | solution.py:247
  108.3 54.3 %collective-permute-start.8 = (bf16[48,32,768]{2,1,0:T(8,128)(2,1)}, bf16[48,32,768]{2,1,0:T(8,128)(2,1)}, u32[]{:S(2)}, u32[]{:S(2)}) collective-permute-start(bf16[48,32,768]{2,1,0:T(8,128)(2,1)} %shard_map.40.refs_1_.refs_9_), channel_id=1, source_target_pairs={{0,4},{4,0},{8,12},{12,8},{1,5},{5,1},{9,13},{13,9},{2,6},{6,2},{1... | collective-permute-start | bytes 7077896 | tf_op jit(solution)/shard_map/ppermute | solution.py:247
  160.6 4.9 %collective-permute-start.9 = (bf16[48,32,768]{2,1,0:T(8,128)(2,1)}, bf16[48,32,768]{2,1,0:T(8,128)(2,1)}, u32[]{:S(2)}, u32[]{:S(2)}) collective-permute-start(bf16[48,32,768]{2,1,0:T(8,128)(2,1)} %collective-permute-done.5.refs_3_.refs_11_), channel_id=1, source_target_pairs={{0,4},{4,0},{8,12},{12,8},{1,5},{5,1},{9,13},{13,9},{2,6},{6,2},{1... | collective-permute-start | bytes 7077896 | tf_op jit(solution)/shard_map/ppermute | solution.py:247
  160.6 37.1 %collective-permute-start.7 = (bf16[32,32,768]{2,1,0:T(8,128)(2,1)}, bf16[32,32,768]{2,1,0:T(8,128)(2,1)}, u32[]{:S(2)}, u32[]{:S(2)}) collective-permute-start(bf16[32,32,768]{2,1,0:T(8,128)(2,1)} %shard_map.41.refs_2_.refs_5_), channel_id=1, source_target_pairs={{0,8},{4,12},{8,0},{12,4},{1,9},{5,13},{9,1},{13,5},{2,10},{6,14},... | collective-permute-start | bytes 4718600 | tf_op jit(solution)/shard_map/ppermute | solution.py:247
  162.3 35.4 %copy-start.1 = (bf16[32,32,768]{2,1,0:T(8,128)(2,1)S(1)}, bf16[32,32,768]{2,1,0:T(8,128)(2,1)}, u32[]{:S(2)}) copy-start(bf16[32,32,768]{2,1,0:T(8,128)(2,1)} %shard_map.42.refs_2_.refs_1_) | copy-start | bytes 4718596
  162.3 59.2 %collective-permute-start.11 = (bf16[32,32,768]{2,1,0:T(8,128)(2,1)}, bf16[32,32,768]{2,1,0:T(8,128)(2,1)}, u32[]{:S(2)}, u32[]{:S(2)}) collective-permute-start(bf16[32,32,768]{2,1,0:T(8,128)(2,1)} %shard_map.41.refs_2_.refs_5_), channel_id=1, source_target_pairs={{0,4},{4,0},{8,12},{12,8},{1,5},{5,1},{9,13},{13,9},{2,6},{6,2},{1... | collective-permute-start | bytes 4718600 | tf_op jit(solution)/shard_map/ppermute | solution.py:247
  197.7 23.8 %collective-permute-start.12 = (bf16[32,32,768]{2,1,0:T(8,128)(2,1)}, bf16[32,32,768]{2,1,0:T(8,128)(2,1)}, u32[]{:S(2)}, u32[]{:S(2)}) collective-permute-start(bf16[32,32,768]{2,1,0:T(8,128)(2,1)} %collective-permute-done.7.refs_4_.refs_7_), channel_id=1, source_target_pairs={{0,4},{4,0},{8,12},{12,8},{1,5},{5,1},{9,13},{13,9},{2,6},{6,2},{1... | collective-permute-start | bytes 4718600 | tf_op jit(solution)/shard_map/ppermute | solution.py:247
  197.7 40.2 %collective-permute-start.10 = (bf16[32,32,768]{2,1,0:T(8,128)(2,1)S(1)}, bf16[32,32,768]{2,1,0:T(8,128)(2,1)}, u32[]{:S(2)}, u32[]{:S(2)}) collective-permute-start(bf16[32,32,768]{2,1,0:T(8,128)(2,1)S(1)} %copy-done.1), channel_id=1, source_target_pairs={{0,8},{4,12},{8,0},{12,4},{1,9},{5,13},{9,1},{13,5},{2,10},{6,14},... | collective-permute-start | bytes 4718600 | tf_op jit(solution)/shard_map/ppermute | solution.py:247
  199.4 39.2 %collective-permute-start.14 = (bf16[32,32,768]{2,1,0:T(8,128)(2,1)S(1)}, bf16[32,32,768]{2,1,0:T(8,128)(2,1)}, u32[]{:S(2)}, u32[]{:S(2)}) collective-permute-start(bf16[32,32,768]{2,1,0:T(8,128)(2,1)S(1)} %copy-done.1), channel_id=1, source_target_pairs={{0,4},{4,0},{8,12},{12,8},{1,5},{5,1},{9,13},{13,9},{2,6},{6,2},{1... | collective-permute-start | bytes 4718600 | tf_op jit(solution)/shard_map/ppermute | solution.py:247
  237.9 3.8 %collective-permute-start.15 = (bf16[32,32,768]{2,1,0:T(8,128)(2,1)}, bf16[32,32,768]{2,1,0:T(8,128)(2,1)}, u32[]{:S(2)}, u32[]{:S(2)}) collective-permute-start(bf16[32,32,768]{2,1,0:T(8,128)(2,1)} %collective-permute-done.10.refs_4_.refs_3_), channel_id=1, source_target_pairs={{0,4},{4,0},{8,12},{12,8},{1,5},{5,1},{9,13},{13,9},{2,6},{6,2},{1... | collective-permute-start | bytes 4718600 | tf_op jit(solution)/shard_map/ppermute | solution.py:247
  238.3 36.8 %collective-permute-start.13 = (bf16[32,32,768]{2,1,0:T(8,128)(2,1)}, bf16[32,32,768]{2,1,0:T(8,128)(2,1)}, u32[]{:S(2)}, u32[]{:S(2)}) collective-permute-start(bf16[32,32,768]{2,1,0:T(8,128)(2,1)} %shard_map.43.refs_3_), channel_id=1, source_target_pairs={{0,8},{4,12},{8,0},{12,4},{1,9},{5,13},{9,1},{13,5},{2,10},{6,14},... | collective-permute-start | bytes 4718600 | tf_op jit(solution)/shard_map/ppermute | solution.py:247
  238.6 52.2 %collective-permute-start.17 = (bf16[32,32,768]{2,1,0:T(8,128)(2,1)}, bf16[32,32,768]{2,1,0:T(8,128)(2,1)}, u32[]{:S(2)}, u32[]{:S(2)}) collective-permute-start(bf16[32,32,768]{2,1,0:T(8,128)(2,1)} %shard_map.43.refs_3_), channel_id=1, source_target_pairs={{0,4},{4,0},{8,12},{12,8},{1,5},{5,1},{9,13},{13,9},{2,6},{6,2},{1... | collective-permute-start | bytes 4718600 | tf_op jit(solution)/shard_map/ppermute | solution.py:247
  257.8 17.3 %copy-start.2 = (bf16[32,32,768]{2,1,0:T(8,128)(2,1)S(1)}, bf16[32,32,768]{2,1,0:T(8,128)(2,1)}, u32[]{:S(2)}) copy-start(bf16[32,32,768]{2,1,0:T(8,128)(2,1)} %shard_map.44.refs_3_) | copy-start | bytes 4718596
  275.1 15.6 %collective-permute-start.18 = (bf16[32,32,768]{2,1,0:T(8,128)(2,1)}, bf16[32,32,768]{2,1,0:T(8,128)(2,1)}, u32[]{:S(2)}, u32[]{:S(2)}) collective-permute-start(bf16[32,32,768]{2,1,0:T(8,128)(2,1)} %collective-permute-done.13.refs_5_), channel_id=1, source_target_pairs={{0,4},{4,0},{8,12},{12,8},{1,5},{5,1},{9,13},{13,9},{2,6},{6,2},{1... | collective-permute-start | bytes 4718600 | tf_op jit(solution)/shard_map/ppermute | solution.py:247
  275.1 36.9 %collective-permute-start.16 = (bf16[32,32,768]{2,1,0:T(8,128)(2,1)S(1)}, bf16[32,32,768]{2,1,0:T(8,128)(2,1)}, u32[]{:S(2)}, u32[]{:S(2)}) collective-permute-start(bf16[32,32,768]{2,1,0:T(8,128)(2,1)S(1)} %copy-done.2), channel_id=1, source_target_pairs={{0,8},{4,12},{8,0},{12,4},{1,9},{5,13},{9,1},{13,5},{2,10},{6,14},... | collective-permute-start | bytes 4718600 | tf_op jit(solution)/shard_map/ppermute | solution.py:247
  275.4 45.3 %collective-permute-start.19 = (bf16[32,32,768]{2,1,0:T(8,128)(2,1)S(1)}, bf16[32,32,768]{2,1,0:T(8,128)(2,1)}, u32[]{:S(2)}, u32[]{:S(2)}) collective-permute-start(bf16[32,32,768]{2,1,0:T(8,128)(2,1)S(1)} %copy-done.2), channel_id=1, source_target_pairs={{0,4},{4,0},{8,12},{12,8},{1,5},{5,1},{9,13},{13,9},{2,6},{6,2},{1... | collective-permute-start | bytes 4718600 | tf_op jit(solution)/shard_map/ppermute | solution.py:247
  312.0 8.6 %collective-permute-start.20 = (bf16[32,32,768]{2,1,0:T(8,128)(2,1)}, bf16[32,32,768]{2,1,0:T(8,128)(2,1)}, u32[]{:S(2)}, u32[]{:S(2)}) collective-permute-start(bf16[32,32,768]{2,1,0:T(8,128)(2,1)} %collective-permute-done.16.refs_5_), channel_id=1, source_target_pairs={{0,4},{4,0},{8,12},{12,8},{1,5},{5,1},{9,13},{13,9},{2,6},{6,2},{1... | collective-permute-start | bytes 4718600 | tf_op jit(solution)/shard_map/ppermute | solution.py:247
Sparse Core Ops, SparseCore 0:
  11.6 118.0 all-gather.3
  131.3 61.7 all-gather.5
  194.6 62.1 all-gather.7

commit v4 on v3

--- a/solution.py
+++ b/solution.py
@@ -219,25 +219,24 @@
 def split_kernel(in_ref, *refs, pieces, span):
     wide_ref = refs[-1]
     rows, count_a, _ = in_ref.shape
-    for half in sorted({half for _, _, half in pieces}):
-        lanes = slice(half * span, (half + 1) * span)
-        wide_ref[half] = in_ref[:, :, lanes].astype(jnp.float32).reshape(rows * count_a, span)
-    for (first, count, half), out_ref in zip(pieces, refs):
+    wide_ref[...] = in_ref[...].astype(jnp.float32).reshape(rows * count_a, span)
+    for (first, count, _), out_ref in zip(pieces, refs):
         for a in range(count):
-            picked = wide_ref[half, pl.ds(first + a, rows, stride=count_a), :]
+            picked = wide_ref[pl.ds(first + a, rows, stride=count_a), :]
             out_ref[:, a * span : (a + 1) * span] = picked.astype(out_ref.dtype)
 
 
 def split_left(array, pieces, span):
-    rows, count_a, span_c = array.shape
+    rows, count_a, _ = array.shape
+    half = pieces[0][2]
     block = math.gcd(rows, 256)
     return pl.pallas_call(
         functools.partial(split_kernel, pieces=pieces, span=span),
         out_shape=[jax.ShapeDtypeStruct((rows, count * span), array.dtype) for _, count, _ in pieces],
         grid=(rows // block,),
-        in_specs=[pl.BlockSpec((block, count_a, span_c), lambda i: (i, 0, 0))],
+        in_specs=[pl.BlockSpec((block, count_a, span), lambda i: (i, 0, half))],
         out_specs=[pl.BlockSpec((block, count * span), lambda i: (i, 0)) for _, count, _ in pieces],
-        scratch_shapes=[pltpu.VMEM((span_c // span, block * count_a, span), jnp.float32)],
+        scratch_shapes=[pltpu.VMEM((block * count_a, span), jnp.float32)],
         compiler_params=pltpu.CompilerParams(vmem_limit_bytes=VMEM_BYTES),
         cost_estimate=SMALL_COST,
     )(array)
@@ -270,13 +269,15 @@
             held = held | {m ^ bit: swap(x, "row", bit, row_size) for m, x in held.items()}
         return held
 
-    parts = split_left(left_factor, pieces, span)
-    parts, right_factor = together((parts, right_factor))
+    parts = split_left(left_factor, pieces[:1], span)
+    parts, right_factor, left_factor = together((parts, right_factor, left_factor))
     owns = [turn(right_factor, starts[0], chunks[0])]
-    owns[0], right_factor = together((owns[0], right_factor))
-
-    lefts = [lax.all_gather(part, "col", axis=0, tiled=True) for part in parts]
-
+    owns[0], right_factor, left_factor = together((owns[0], right_factor, left_factor))
+
+    def gathered(parts):
+        return [lax.all_gather(part, "col", axis=0, tiled=True) for part in parts]
+
+    lefts = gathered(parts)
     total = jnp.zeros((width_a * width_b, pair_count), jnp.float32)
     rights = [spread({0: owns[0]})]
     for j, calls in enumerate(STAGES):
@@ -286,6 +287,9 @@
         if j == 0:
             owns.append(turn(right_factor, starts[1], chunks[1]))
         if j == 1:
+            parts = split_left(left_factor, pieces[1:], span)
+            lefts += gathered(parts)
+            parts, right_factor = together((parts, right_factor))
             owns += [turn(right_factor, s, n) for s, n in zip(starts[2:], chunks[2:])]
             owns, amplitudes = together((owns, amplitudes))
             amp = jnp.transpose(amplitudes, (1, 0, 2))
@@ -298,11 +302,11 @@
             )
         if moving:
             if j == 0:
-                far, total, owns, right_factor, amplitudes = together(
-                    (far, total, owns, right_factor, amplitudes)
+                far, total, right_factor, left_factor, amplitudes = together(
+                    (far, total, right_factor, left_factor, amplitudes)
                 )
             elif j == 1:
-                far, total, owns, amp, rights = together((far, total, owns, amp, rights))
+                far, total, amp, rights = together((far, total, amp, rights))
             else:
                 far, total, owns = together((far, total, owns))
             rights[j] |= spread({far_bit: far})

time: 369 us -> 364 us (0.986)
  waiting for transfers between devices: 94.1 us -> 89.1 us
    ppermute x21, waiting for transfers between devices: 75.8 us -> 64.4 us  [swap(): return lax.ppermute(block, axis, [(i, i ^ bit) for i in range(size)])]
    all_gather x3, waiting for transfers between devices: 18.3 us -> 24.6 us  [gathered(): return [lax.all_gather(part, 'col', axis=0, tiled=True) for part in parts]]
  transfers between devices with their start and end apart: 24 -> 24, of which waited for: 10 -> 9; matrix products, arithmetic and copies ran while one was open for 7% -> 7% of each run, Pallas kernels for 49% -> 50%
where the time goes in v4:
time: 364 us; the launch traced here: 361 us
  Pallas kernels  206 us (57%)
  waiting for transfers between devices  89.1 us (24%)
  local copies, waits for them, and re-layouts  24.8 us (7%)
  blocking collectives  14.2 us (4%)
  between operations  13.8 us (4%)
  starting transfers between devices  12.4 us (3%)
    pallas_call x10, Pallas kernels, add_ladder(): pl.pallas_call(functools.partial(ladder_kernel, pieces=pieces, chunk_step...  173 us
    ppermute x21, waiting for transfers between devices, swap(): return lax.ppermute(block, axis, [(i, i ^ bit) for i in range(size)])  64.4 us
    pallas_call x7, Pallas kernels, turn(): pl.pallas_call(turn_kernel, out_shape=jax.ShapeDtypeStruct((size, outer,...  25.8 us
    all_gather x3, waiting for transfers between devices, gathered(): return [lax.all_gather(part, 'col', axis=0, tiled=True) for part in parts]  24.6 us
    optimization_barrier x1, local copies, waits for them, and re-layouts, on_device(): owns, amplitudes = together((owns, amplitudes))  23 us
    all_to_all x1, blocking collectives, on_device(): return lax.all_to_all(shares, ('row', 'col'), 0, 0, tiled=True).sum(axis=0)  14.2 us
    ppermute x21, starting transfers between devices, swap(): return lax.ppermute(block, axis, [(i, i ^ bit) for i in range(size)])  12.1 us
    pallas_call x2, Pallas kernels, split_left(): pl.pallas_call(functools.partial(split_kernel, pieces=pieces, span=span),...  7.35 us
  transfers between devices with their start and end apart: 24, of which 9 were waited for; matrix products, arithmetic and copies ran while one was open for 7% of the time, Pallas kernels for 50%

profile of v4, /device:TPU:0, one launch (start us, length us, event | category | flops | bytes accessed | tf_op | source)
XLA Modules:
  0.0 360.6 jit_solution(18372823437071424746)
XLA Ops:
  6.5 3.7 %shard_map.37 = bf16[768,1024]{1,0:T(8,128)(2,1)} custom-call(bf16[768,8,256]{2,1,0:T(8,128)(2,1)} %in_ref.4), custom_call_target="tpu_custom_call" | custom-call | bytes 65536 | tf_op jit(solution)/shard_map/pallas_call | solution.py:233
  10.4 3.3 shard_map.38.refs_1_
  13.6 2.9 collective-permute-start
  16.6 4.7 %shard_map.39.refs_5_ = bf16[48,32,768]{2,1,0:T(8,128)(2,1)} custom-call(bf16[32,256,768]{2,1,0:T(8,128)(2,1)} %in_ref.9), custom_call_target="tpu_custom_call" | custom-call | bytes 65536 | tf_op jit(solution)/shard_map/pallas_call | solution.py:207
  21.3 0.1 collective-permute-start.2
  21.4 0.4 collective-permute-start.3
  21.8 30.4 %collective-permute-done.refs_3_ = bf16[32,32,768]{2,1,0:T(8,128)(2,1)} collective-permute-done((bf16[32,32,768]{2,1,0:T(8,128)(2,1)}, bf16[32,32,768]{2,1,0:T(8,128)(2,1)}, u32[]{:S(2)}, u32[]{:S(2)}) %collective-permute-start) | collective-permute-done | bytes 1572896 | tf_op jit(solution)/shard_map/ppermute | solution.py:246
  52.2 3.6 shard_map.40
  55.8 0.3 all-gather.8.cloned.1.call-start
  56.1 3.3 shard_map.45.refs_3_
  59.3 3.3 shard_map.44.refs_3_
  62.6 3.3 shard_map.43.refs_2_.refs_1_
  65.9 3.3 shard_map.42.refs_2_.refs_5_
  69.1 4.7 %shard_map.41.refs_1_.refs_9_ = bf16[48,32,768]{2,1,0:T(8,128)(2,1)} custom-call(bf16[32,256,768]{2,1,0:T(8,128)(2,1)} %in_ref.9), custom_call_target="tpu_custom_call" | custom-call | bytes 65536 | tf_op jit(solution)/shard_map/pallas_call | solution.py:207
  73.8 23.0 %copy.18 = bf16[256,256,256]{2,0,1:T(8,128)(2,1)} copy(bf16[256,256,256]{2,1,0:T(8,128)(2,1)} %param.5) | data formatting | bytes 67108864 | tf_op jit(solution)/shard_map/optimization_barrier | solution.py:294
  96.8 5.1 %collective-permute-done.2.refs_7_ = bf16[48,32,768]{2,1,0:T(8,128)(2,1)} collective-permute-done((bf16[48,32,768]{2,1,0:T(8,128)(2,1)}, bf16[48,32,768]{2,1,0:T(8,128)(2,1)}, u32[]{:S(2)}, u32[]{:S(2)}) %collective-permute-start.2) | collective-permute-done | bytes 2359328 | tf_op jit(solution)/shard_map/ppermute | solution.py:246
  101.9 1.7 collective-permute-start.1
  103.6 0.2 collective-permute-start.8
  103.8 3.0 collective-permute-done.6.refs_8_
  106.8 21.7 %all-gather.4.cloned.1.call-done.refs_0_ = bf16[3072,1024]{1,0:T(8,128)(2,1)} async-done(((bf16[768,1024]{1,0:T(8,128)(2,1)}), bf16[3072,1024]{1,0:T(8,128)(2,1)}) %all-gather.4.cloned.1.call-update) | async-done | bytes 6291472 | tf_op jit(solution)/shard_map/all_gather | solution.py:278
  128.5 0.7 broadcast_in_dim.3.total_ref
  129.2 23.4 %shard_map.46.total_ref = f32[256,256]{1,0:T(8,128)} custom-call(s32[1]{0:T(128)} %bitcast.place_ref, f32[256,256]{1,0:T(8,128)} %broadcast_in_dim.3.total_ref, bf16[256,256,256]{2,1,0:T(8,128)(2,1)} %bitcast.6, bf16[3072,1024]{1,0:T(8,128)(2,1)} %all-gather.4.cloned.1.call-done.refs_0_, ...), custom_call_target="tpu_custom_call", output_to_operand_aliasing={{}: (1, {})} | custom-call | flops 872415232 | bytes 22020096 | tf_op jit(solution)/shard_map/pallas_call | solution.py:152
  152.7 3.2 collective-permute-done.1.refs_3_.refs_11_
  155.9 1.7 collective-permute-start.7
  157.6 0.3 collective-permute-start.11
  157.9 2.9 collective-permute-done.9.refs_4_.refs_12_
  160.7 15.4 %shard_map.47.total_ref = f32[256,256]{1,0:T(8,128)} custom-call(s32[1]{0:T(128)} %bitcast.place_ref, f32[256,256]{1,0:T(8,128)} %shard_map.46.total_ref, bf16[256,256,256]{2,1,0:T(8,128)(2,1)} %bitcast.7, bf16[3072,1024]{1,0:T(8,128)(2,1)} %all-gather.4.cloned.1.call-done.refs_0_, ...), custom_call_target="tpu_custom_call", output_to_operand_aliasing={{}: (1, {})} | custom-call | flops 523449152 | bytes 15728640 | tf_op jit(solution)/shard_map/pallas_call | solution.py:152
  176.2 16.8 %collective-permute-done.7.refs_4_.refs_7_ = bf16[32,32,768]{2,1,0:T(8,128)(2,1)} collective-permute-done((bf16[32,32,768]{2,1,0:T(8,128)(2,1)}, bf16[32,32,768]{2,1,0:T(8,128)(2,1)}, u32[]{:S(2)}, u32[]{:S(2)}) %collective-permute-start.7) | collective-permute-done | bytes 1572896 | tf_op jit(solution)/shard_map/ppermute | solution.py:246
  193.0 1.7 collective-permute-start.10
  194.7 0.2 collective-permute-start.14
  194.9 21.4 %shard_map.48.total_ref = f32[256,256]{1,0:T(8,128)} custom-call(s32[1]{0:T(128)} %bitcast.place_ref, f32[256,256]{1,0:T(8,128)} %shard_map.47.total_ref, bf16[256,256,256]{2,1,0:T(8,128)(2,1)} %bitcast.8, bf16[3072,512]{1,0:T(8,128)(2,1)} %all-gather.6.cloned.1.call-done.refs_0_.refs_1_, ...), custom_call_target="tpu_custom_call", output_to_operand_aliasing={{}: (1, {})} | custom-call | flops 697932160 | bytes 28311552 | tf_op jit(solution)/shard_map/pallas_call | solution.py:152
  216.4 16.4 %shard_map.49.total_ref = f32[256,256]{1,0:T(8,128)} custom-call(s32[1]{0:T(128)} %bitcast.place_ref, f32[256,256]{1,0:T(8,128)} %shard_map.48.total_ref, bf16[256,256,256]{2,1,0:T(8,128)(2,1)} %bitcast.9, bf16[3072,1024]{1,0:T(8,128)(2,1)} %all-gather.4.cloned.1.call-done.refs_0_, ...), custom_call_target="tpu_custom_call", output_to_operand_aliasing={{}: (1, {})} | custom-call | flops 523449152 | bytes 15728640 | tf_op jit(solution)/shard_map/pallas_call | solution.py:152
  232.8 0.4 collective-permute-start.15
  233.2 0.4 collective-permute-start.13
  233.6 3.1 collective-permute-done.15.refs_5_.refs_4_
  236.7 16.1 %shard_map.50.total_ref = f32[256,256]{1,0:T(8,128)} custom-call(s32[1]{0:T(128)} %bitcast.place_ref, f32[256,256]{1,0:T(8,128)} %shard_map.49.total_ref, bf16[256,256,256]{2,1,0:T(8,128)(2,1)} %bitcast.10, bf16[3072,1024]{1,0:T(8,128)(2,1)} %all-gather.4.cloned.1.call-done.refs_0_, ...), custom_call_target="tpu_custom_call", output_to_operand_aliasing={{}: (1, {})} | custom-call | flops 523449152 | bytes 15728640 | tf_op jit(solution)/shard_map/pallas_call | solution.py:152
  252.8 2.9 all-gather.8.cloned.1.call-done.refs_0_.refs_2_
  255.6 14.9 %shard_map.51.total_ref = f32[256,256]{1,0:T(8,128)} custom-call(s32[1]{0:T(128)} %bitcast.place_ref, f32[256,256]{1,0:T(8,128)} %shard_map.50.total_ref, bf16[256,256,256]{2,1,0:T(8,128)(2,1)} %bitcast.11, bf16[3072,512]{1,0:T(8,128)(2,1)} %all-gather.8.cloned.1.call-done.refs_0_.refs_2_, ...), custom_call_target="tpu_custom_call", output_to_operand_aliasing={{}: (1, {})} | custom-call | flops 436207616 | bytes 18874368 | tf_op jit(solution)/shard_map/pallas_call | solution.py:152
  270.6 1.5 collective-permute-start.16
  272.1 0.2 collective-permute-start.19
  272.3 15.1 %shard_map.52.total_ref = f32[256,256]{1,0:T(8,128)} custom-call(s32[1]{0:T(128)} %bitcast.place_ref, f32[256,256]{1,0:T(8,128)} %shard_map.51.total_ref, bf16[256,256,256]{2,1,0:T(8,128)(2,1)} %bitcast.12, bf16[3072,512]{1,0:T(8,128)(2,1)} %all-gather.8.cloned.1.call-done.refs_0_.refs_2_, ...), custom_call_target="tpu_custom_call", output_to_operand_aliasing={{}: (1, {})} | custom-call | flops 436207616 | bytes 18874368 | tf_op jit(solution)/shard_map/pallas_call | solution.py:152
  287.4 20.6 %shard_map.53.total_ref = f32[256,256]{1,0:T(8,128)} custom-call(s32[1]{0:T(128)} %bitcast.place_ref, f32[256,256]{1,0:T(8,128)} %shard_map.52.total_ref, bf16[256,256,256]{2,1,0:T(8,128)(2,1)} %bitcast.13, bf16[3072,1024]{1,0:T(8,128)(2,1)} %all-gather.4.cloned.1.call-done.refs_0_, ...), custom_call_target="tpu_custom_call", output_to_operand_aliasing={{}: (1, {})} | custom-call | flops 697932160 | bytes 18874368 | tf_op jit(solution)/shard_map/pallas_call | solution.py:152
  308.0 0.4 collective-permute-start.20
  308.4 8.6 %shard_map.54.total_ref = f32[256,256]{1,0:T(8,128)} custom-call(s32[1]{0:T(128)} %bitcast.place_ref, f32[256,256]{1,0:T(8,128)} %shard_map.53.total_ref, bf16[256,256,256]{2,1,0:T(8,128)(2,1)} %bitcast.14, bf16[3072,512]{1,0:T(8,128)(2,1)} %all-gather.8.cloned.1.call-done.refs_0_.refs_2_, ...), custom_call_target="tpu_custom_call", output_to_operand_aliasing={{}: (1, {})} | custom-call | flops 174483040 | bytes 9437184 | tf_op jit(solution)/shard_map/pallas_call | solution.py:152
  317.1 20.6 %shard_map.55 = f32[256,256]{1,0:T(8,128)} custom-call(s32[1]{0:T(128)} %bitcast.place_ref, f32[256,256]{1,0:T(8,128)} %shard_map.54.total_ref, bf16[256,256,256]{2,1,0:T(8,128)(2,1)} %bitcast.15, bf16[3072,1024]{1,0:T(8,128)(2,1)} %all-gather.4.cloned.1.call-done.refs_0_, ...), custom_call_target="tpu_custom_call", output_to_operand_aliasing={{}: (1, {})} | custom-call | flops 697932160 | bytes 18874368 | tf_op jit(solution)/shard_map/pallas_call | solution.py:152
  337.7 1.1 copy.16
  338.8 14.2 %all_to_all.5 = f32[16,16,256]{2,1,0:T(8,128)S(1)} all-to-all(f32[16,16,256]{2,1,0:T(8,128)S(1)} %bitcast.17), channel_id=1, replica_groups=mesh['parts'=2,'row'=4,'col'=4] {'row','col'}, dimensions={0} | all-to-all | bytes 524288 | tf_op jit(solution)/shard_map/all_to_all | solution.py:317
  353.0 0.6 reduce_sum.9
  (33 shorter events, 0.2 us)
Async XLA Ops:
  6.5 122.0 %all-gather.4.cloned.1.call-start = ((), (), s32[]{:S(2)}) async-start(), calls=%async_computation.1 | async-start | bytes 7864320 | tf_op jit(solution)/shard_map/all_gather | solution.py:278
  10.3 184.6 %all-gather.6.cloned.1.call-start = ((), (), s32[]{:S(2)}) async-start(), calls=%async_computation.2 | async-start | bytes 3932160 | tf_op jit(solution)/shard_map/all_gather | solution.py:278
  13.6 7.7 %copy-start = (bf16[32,32,768]{2,1,0:T(8,128)(2,1)S(1)}, bf16[32,32,768]{2,1,0:T(8,128)(2,1)}, u32[]{:S(2)}) copy-start(bf16[32,32,768]{2,1,0:T(8,128)(2,1)} %shard_map.38.refs_1_) | copy-start | bytes 4718596
  13.6 38.5 %collective-permute-start = (bf16[32,32,768]{2,1,0:T(8,128)(2,1)}, bf16[32,32,768]{2,1,0:T(8,128)(2,1)}, u32[]{:S(2)}, u32[]{:S(2)}) collective-permute-start(bf16[32,32,768]{2,1,0:T(8,128)(2,1)} %shard_map.38.refs_1_), channel_id=1, source_target_pairs={{0,8},{4,12},{8,0},{12,4},{1,9},{5,13},{9,1},{13,5},{2,10},{6,14},... | collective-permute-start | bytes 4718600 | tf_op jit(solution)/shard_map/ppermute | solution.py:246
  21.3 75.6 %collective-permute-start.5 = (bf16[48,32,768]{2,1,0:T(8,128)(2,1)}, bf16[48,32,768]{2,1,0:T(8,128)(2,1)}, u32[]{:S(2)}, u32[]{:S(2)}) collective-permute-start(bf16[48,32,768]{2,1,0:T(8,128)(2,1)} %shard_map.39.refs_5_), channel_id=1, source_target_pairs={{0,4},{4,0},{8,12},{12,8},{1,5},{5,1},{9,13},{13,9},{2,6},{6,2},{1... | collective-permute-start | bytes 7077896 | tf_op jit(solution)/shard_map/ppermute | solution.py:246
  21.3 80.6 %collective-permute-start.2 = (bf16[48,32,768]{2,1,0:T(8,128)(2,1)}, bf16[48,32,768]{2,1,0:T(8,128)(2,1)}, u32[]{:S(2)}, u32[]{:S(2)}) collective-permute-start(bf16[48,32,768]{2,1,0:T(8,128)(2,1)} %shard_map.39.refs_5_), channel_id=1, source_target_pairs={{0,8},{4,12},{8,0},{12,4},{1,9},{5,13},{9,1},{13,5},{2,10},{6,14},... | collective-permute-start | bytes 7077896 | tf_op jit(solution)/shard_map/ppermute | solution.py:246
  21.4 75.5 %collective-permute-start.3 = (bf16[32,32,768]{2,1,0:T(8,128)(2,1)S(1)}, bf16[32,32,768]{2,1,0:T(8,128)(2,1)}, u32[]{:S(2)}, u32[]{:S(2)}) collective-permute-start(bf16[32,32,768]{2,1,0:T(8,128)(2,1)S(1)} %copy-done), channel_id=1, source_target_pairs={{0,4},{4,0},{8,12},{12,8},{1,5},{5,1},{9,13},{13,9},{2,6},{6,2},{1... | collective-permute-start | bytes 4718600 | tf_op jit(solution)/shard_map/ppermute | solution.py:246
  52.2 49.7 %collective-permute-start.4 = (bf16[32,32,768]{2,1,0:T(8,128)(2,1)}, bf16[32,32,768]{2,1,0:T(8,128)(2,1)}, u32[]{:S(2)}, u32[]{:S(2)}) collective-permute-start(bf16[32,32,768]{2,1,0:T(8,128)(2,1)} %collective-permute-done.refs_3_), channel_id=1, source_target_pairs={{0,4},{4,0},{8,12},{12,8},{1,5},{5,1},{9,13},{13,9},{2,6},{6,2},{1... | collective-permute-start | bytes 4718600 | tf_op jit(solution)/shard_map/ppermute | solution.py:246
  55.8 199.8 %all-gather.8.cloned.1.call-start = ((), (), s32[]{:S(2)}) async-start(), calls=%async_computation.3 | async-start | bytes 3932160 | tf_op jit(solution)/shard_map/all_gather | solution.py:278
  101.9 4.9 %collective-permute-start.6 = (bf16[48,32,768]{2,1,0:T(8,128)(2,1)}, bf16[48,32,768]{2,1,0:T(8,128)(2,1)}, u32[]{:S(2)}, u32[]{:S(2)}) collective-permute-start(bf16[48,32,768]{2,1,0:T(8,128)(2,1)} %collective-permute-done.2.refs_7_), channel_id=1, source_target_pairs={{0,4},{4,0},{8,12},{12,8},{1,5},{5,1},{9,13},{13,9},{2,6},{6,2},{1... | collective-permute-start | bytes 7077896 | tf_op jit(solution)/shard_map/ppermute | solution.py:246
  101.9 54.0 %collective-permute-start.1 = (bf16[48,32,768]{2,1,0:T(8,128)(2,1)}, bf16[48,32,768]{2,1,0:T(8,128)(2,1)}, u32[]{:S(2)}, u32[]{:S(2)}) collective-permute-start(bf16[48,32,768]{2,1,0:T(8,128)(2,1)} %shard_map.41.refs_1_.refs_9_), channel_id=1, source_target_pairs={{0,8},{4,12},{8,0},{12,4},{1,9},{5,13},{9,1},{13,5},{2,10},{6,14},... | collective-permute-start | bytes 7077896 | tf_op jit(solution)/shard_map/ppermute | solution.py:246
  103.6 54.3 %collective-permute-start.8 = (bf16[48,32,768]{2,1,0:T(8,128)(2,1)}, bf16[48,32,768]{2,1,0:T(8,128)(2,1)}, u32[]{:S(2)}, u32[]{:S(2)}) collective-permute-start(bf16[48,32,768]{2,1,0:T(8,128)(2,1)} %shard_map.41.refs_1_.refs_9_), channel_id=1, source_target_pairs={{0,4},{4,0},{8,12},{12,8},{1,5},{5,1},{9,13},{13,9},{2,6},{6,2},{1... | collective-permute-start | bytes 7077896 | tf_op jit(solution)/shard_map/ppermute | solution.py:246
  155.9 4.9 %collective-permute-start.9 = (bf16[48,32,768]{2,1,0:T(8,128)(2,1)}, bf16[48,32,768]{2,1,0:T(8,128)(2,1)}, u32[]{:S(2)}, u32[]{:S(2)}) collective-permute-start(bf16[48,32,768]{2,1,0:T(8,128)(2,1)} %collective-permute-done.1.refs_3_.refs_11_), channel_id=1, source_target_pairs={{0,4},{4,0},{8,12},{12,8},{1,5},{5,1},{9,13},{13,9},{2,6},{6,2},{1... | collective-permute-start | bytes 7077896 | tf_op jit(solution)/shard_map/ppermute | solution.py:246
  155.9 37.1 %collective-permute-start.7 = (bf16[32,32,768]{2,1,0:T(8,128)(2,1)}, bf16[32,32,768]{2,1,0:T(8,128)(2,1)}, u32[]{:S(2)}, u32[]{:S(2)}) collective-permute-start(bf16[32,32,768]{2,1,0:T(8,128)(2,1)} %shard_map.42.refs_2_.refs_5_), channel_id=1, source_target_pairs={{0,8},{4,12},{8,0},{12,4},{1,9},{5,13},{9,1},{13,5},{2,10},{6,14},... | collective-permute-start | bytes 4718600 | tf_op jit(solution)/shard_map/ppermute | solution.py:246
  157.6 35.4 %copy-start.1 = (bf16[32,32,768]{2,1,0:T(8,128)(2,1)S(1)}, bf16[32,32,768]{2,1,0:T(8,128)(2,1)}, u32[]{:S(2)}) copy-start(bf16[32,32,768]{2,1,0:T(8,128)(2,1)} %shard_map.43.refs_2_.refs_1_) | copy-start | bytes 4718596
  157.6 58.8 %collective-permute-start.11 = (bf16[32,32,768]{2,1,0:T(8,128)(2,1)}, bf16[32,32,768]{2,1,0:T(8,128)(2,1)}, u32[]{:S(2)}, u32[]{:S(2)}) collective-permute-start(bf16[32,32,768]{2,1,0:T(8,128)(2,1)} %shard_map.42.refs_2_.refs_5_), channel_id=1, source_target_pairs={{0,4},{4,0},{8,12},{12,8},{1,5},{5,1},{9,13},{13,9},{2,6},{6,2},{1... | collective-permute-start | bytes 4718600 | tf_op jit(solution)/shard_map/ppermute | solution.py:246
  193.0 23.4 %collective-permute-start.12 = (bf16[32,32,768]{2,1,0:T(8,128)(2,1)}, bf16[32,32,768]{2,1,0:T(8,128)(2,1)}, u32[]{:S(2)}, u32[]{:S(2)}) collective-permute-start(bf16[32,32,768]{2,1,0:T(8,128)(2,1)} %collective-permute-done.7.refs_4_.refs_7_), channel_id=1, source_target_pairs={{0,4},{4,0},{8,12},{12,8},{1,5},{5,1},{9,13},{13,9},{2,6},{6,2},{1... | collective-permute-start | bytes 4718600 | tf_op jit(solution)/shard_map/ppermute | solution.py:246
  193.0 39.8 %collective-permute-start.10 = (bf16[32,32,768]{2,1,0:T(8,128)(2,1)S(1)}, bf16[32,32,768]{2,1,0:T(8,128)(2,1)}, u32[]{:S(2)}, u32[]{:S(2)}) collective-permute-start(bf16[32,32,768]{2,1,0:T(8,128)(2,1)S(1)} %copy-done.1), channel_id=1, source_target_pairs={{0,8},{4,12},{8,0},{12,4},{1,9},{5,13},{9,1},{13,5},{2,10},{6,14},... | collective-permute-start | bytes 4718600 | tf_op jit(solution)/shard_map/ppermute | solution.py:246
  194.7 38.9 %collective-permute-start.14 = (bf16[32,32,768]{2,1,0:T(8,128)(2,1)S(1)}, bf16[32,32,768]{2,1,0:T(8,128)(2,1)}, u32[]{:S(2)}, u32[]{:S(2)}) collective-permute-start(bf16[32,32,768]{2,1,0:T(8,128)(2,1)S(1)} %copy-done.1), channel_id=1, source_target_pairs={{0,4},{4,0},{8,12},{12,8},{1,5},{5,1},{9,13},{13,9},{2,6},{6,2},{1... | collective-permute-start | bytes 4718600 | tf_op jit(solution)/shard_map/ppermute | solution.py:246
  232.8 3.8 %collective-permute-start.15 = (bf16[32,32,768]{2,1,0:T(8,128)(2,1)}, bf16[32,32,768]{2,1,0:T(8,128)(2,1)}, u32[]{:S(2)}, u32[]{:S(2)}) collective-permute-start(bf16[32,32,768]{2,1,0:T(8,128)(2,1)} %collective-permute-done.10.refs_4_.refs_3_), channel_id=1, source_target_pairs={{0,4},{4,0},{8,12},{12,8},{1,5},{5,1},{9,13},{13,9},{2,6},{6,2},{1... | collective-permute-start | bytes 4718600 | tf_op jit(solution)/shard_map/ppermute | solution.py:246
  233.2 37.3 %collective-permute-start.13 = (bf16[32,32,768]{2,1,0:T(8,128)(2,1)}, bf16[32,32,768]{2,1,0:T(8,128)(2,1)}, u32[]{:S(2)}, u32[]{:S(2)}) collective-permute-start(bf16[32,32,768]{2,1,0:T(8,128)(2,1)} %shard_map.44.refs_3_), channel_id=1, source_target_pairs={{0,8},{4,12},{8,0},{12,4},{1,9},{5,13},{9,1},{13,5},{2,10},{6,14},... | collective-permute-start | bytes 4718600 | tf_op jit(solution)/shard_map/ppermute | solution.py:246
  233.5 53.9 %collective-permute-start.17 = (bf16[32,32,768]{2,1,0:T(8,128)(2,1)}, bf16[32,32,768]{2,1,0:T(8,128)(2,1)}, u32[]{:S(2)}, u32[]{:S(2)}) collective-permute-start(bf16[32,32,768]{2,1,0:T(8,128)(2,1)} %shard_map.44.refs_3_), channel_id=1, source_target_pairs={{0,4},{4,0},{8,12},{12,8},{1,5},{5,1},{9,13},{13,9},{2,6},{6,2},{1... | collective-permute-start | bytes 4718600 | tf_op jit(solution)/shard_map/ppermute | solution.py:246
  252.7 17.9 %copy-start.2 = (bf16[32,32,768]{2,1,0:T(8,128)(2,1)S(1)}, bf16[32,32,768]{2,1,0:T(8,128)(2,1)}, u32[]{:S(2)}) copy-start(bf16[32,32,768]{2,1,0:T(8,128)(2,1)} %shard_map.45.refs_3_) | copy-start | bytes 4718596
  270.5 16.9 %collective-permute-start.18 = (bf16[32,32,768]{2,1,0:T(8,128)(2,1)}, bf16[32,32,768]{2,1,0:T(8,128)(2,1)}, u32[]{:S(2)}, u32[]{:S(2)}) collective-permute-start(bf16[32,32,768]{2,1,0:T(8,128)(2,1)} %collective-permute-done.13.refs_5_), channel_id=1, source_target_pairs={{0,4},{4,0},{8,12},{12,8},{1,5},{5,1},{9,13},{13,9},{2,6},{6,2},{1... | collective-permute-start | bytes 4718600 | tf_op jit(solution)/shard_map/ppermute | solution.py:246
  270.6 37.4 %collective-permute-start.16 = (bf16[32,32,768]{2,1,0:T(8,128)(2,1)S(1)}, bf16[32,32,768]{2,1,0:T(8,128)(2,1)}, u32[]{:S(2)}, u32[]{:S(2)}) collective-permute-start(bf16[32,32,768]{2,1,0:T(8,128)(2,1)S(1)} %copy-done.2), channel_id=1, source_target_pairs={{0,8},{4,12},{8,0},{12,4},{1,9},{5,13},{9,1},{13,5},{2,10},{6,14},... | collective-permute-start | bytes 4718600 | tf_op jit(solution)/shard_map/ppermute | solution.py:246
  272.1 44.9 %collective-permute-start.19 = (bf16[32,32,768]{2,1,0:T(8,128)(2,1)S(1)}, bf16[32,32,768]{2,1,0:T(8,128)(2,1)}, u32[]{:S(2)}, u32[]{:S(2)}) collective-permute-start(bf16[32,32,768]{2,1,0:T(8,128)(2,1)S(1)} %copy-done.2), channel_id=1, source_target_pairs={{0,4},{4,0},{8,12},{12,8},{1,5},{5,1},{9,13},{13,9},{2,6},{6,2},{1... | collective-permute-start | bytes 4718600 | tf_op jit(solution)/shard_map/ppermute | solution.py:246
  308.0 9.1 %collective-permute-start.20 = (bf16[32,32,768]{2,1,0:T(8,128)(2,1)}, bf16[32,32,768]{2,1,0:T(8,128)(2,1)}, u32[]{:S(2)}, u32[]{:S(2)}) collective-permute-start(bf16[32,32,768]{2,1,0:T(8,128)(2,1)} %collective-permute-done.16.refs_5_), channel_id=1, source_target_pairs={{0,4},{4,0},{8,12},{12,8},{1,5},{5,1},{9,13},{13,9},{2,6},{6,2},{1... | collective-permute-start | bytes 4718600 | tf_op jit(solution)/shard_map/ppermute | solution.py:246
Sparse Core Ops, SparseCore 0:
  10.4 118.0 all-gather.3
  130.1 61.7 all-gather.5
  193.4 62.1 all-gather.7

commit v5 on v4

--- a/solution.py
+++ b/solution.py
@@ -62,6 +62,12 @@
 
             begin += n
 
+    def fetch_rest():
+        total_copy().start()
+        amp_copy(0, 0).start()
+        if steps > 1:
+            fetch_right(1, 1)
+
     def integrals(to, first):
         row = 0
         for k, (_, count, _) in enumerate(pieces):
@@ -70,6 +76,8 @@
                 if first:
                     for copy in left_copies(k, a):
                         copy.wait()
+                    if k == 0 and a == 0:
+                        fetch_rest()
                 product = None
                 for m in range(ranks):
                     start = pl.multiple_of((place ^ m) * depth, depth)
@@ -106,12 +114,14 @@
             for a in range(0, count, 4):
                 for copy in left_copies(k, a):
                     copy.start()
-        total_copy().start()
-
-    amp_copy(step, slot).start()
+
     if steps > 1:
 
-        @pl.when(step + 1 < steps)
+        @pl.when(step > 0)
+        def _():
+            amp_copy(step, slot).start()
+
+        @pl.when((step > 0) & (step + 1 < steps))
         def _():
             fetch_right(step + 1, 1 - slot)
 

time: 364 us -> 363 us (level)
  no operation moved by 1% of the time
where the time goes in v5:
time: 363 us; the launch traced here: 360 us
  Pallas kernels  204 us (56%)
  waiting for transfers between devices  89.9 us (25%)
  local copies, waits for them, and re-layouts  24.8 us (7%)
  blocking collectives  14.6 us (4%)
  between operations  13.8 us (4%)
  starting transfers between devices  12.3 us (3%)
    pallas_call x10, Pallas kernels, add_ladder(): pl.pallas_call(functools.partial(ladder_kernel, pieces=pieces, chunk_step...  171 us
    ppermute x21, waiting for transfers between devices, swap(): return lax.ppermute(block, axis, [(i, i ^ bit) for i in range(size)])  65.2 us
    pallas_call x7, Pallas kernels, turn(): pl.pallas_call(turn_kernel, out_shape=jax.ShapeDtypeStruct((size, outer,...  25.8 us
    all_gather x3, waiting for transfers between devices, gathered(): return [lax.all_gather(part, 'col', axis=0, tiled=True) for part in parts]  24.7 us
    optimization_barrier x1, local copies, waits for them, and re-layouts, on_device(): owns, amplitudes = together((owns, amplitudes))  23 us
    all_to_all x1, blocking collectives, on_device(): return lax.all_to_all(shares, ('row', 'col'), 0, 0, tiled=True).sum(axis=0)  14.6 us
    ppermute x21, starting transfers between devices, swap(): return lax.ppermute(block, axis, [(i, i ^ bit) for i in range(size)])  12 us
    pallas_call x2, Pallas kernels, split_left(): pl.pallas_call(functools.partial(split_kernel, pieces=pieces, span=span),...  7.35 us
  transfers between devices with their start and end apart: 24, of which 9 were waited for; matrix products, arithmetic and copies ran while one was open for 7% of the time, Pallas kernels for 50%

profile of v5, /device:TPU:0, one launch (start us, length us, event | category | flops | bytes accessed | tf_op | source)
XLA Modules:
  0.0 360.0 jit_solution(10519490203836616792)
XLA Ops:
  6.5 3.7 %shard_map.37 = bf16[768,1024]{1,0:T(8,128)(2,1)} custom-call(bf16[768,8,256]{2,1,0:T(8,128)(2,1)} %in_ref.4), custom_call_target="tpu_custom_call" | custom-call | bytes 65536 | tf_op jit(solution)/shard_map/pallas_call | solution.py:243
  10.4 3.3 shard_map.38.refs_1_
  13.6 2.9 collective-permute-start
  16.6 4.7 %shard_map.39.refs_5_ = bf16[48,32,768]{2,1,0:T(8,128)(2,1)} custom-call(bf16[32,256,768]{2,1,0:T(8,128)(2,1)} %in_ref.9), custom_call_target="tpu_custom_call" | custom-call | bytes 65536 | tf_op jit(solution)/shard_map/pallas_call | solution.py:217
  21.4 0.4 collective-permute-start.3
  21.8 30.4 %collective-permute-done.refs_3_ = bf16[32,32,768]{2,1,0:T(8,128)(2,1)} collective-permute-done((bf16[32,32,768]{2,1,0:T(8,128)(2,1)}, bf16[32,32,768]{2,1,0:T(8,128)(2,1)}, u32[]{:S(2)}, u32[]{:S(2)}) %collective-permute-start) | collective-permute-done | bytes 1572896 | tf_op jit(solution)/shard_map/ppermute | solution.py:256
  52.2 3.6 %shard_map.40 = (bf16[768,512]{1,0:T(8,128)(2,1)}, bf16[768,512]{1,0:T(8,128)(2,1)}) custom-call(bf16[768,8,256]{2,1,0:T(8,128)(2,1)} %in_ref.4), custom_call_target="tpu_custom_call" | custom-call | bytes 65536 | tf_op jit(solution)/shard_map/pallas_call | solution.py:243
  55.8 0.3 all-gather.8.cloned.1.call-start
  56.1 3.3 shard_map.45.refs_3_
  59.3 3.3 shard_map.44.refs_3_
  62.6 3.3 shard_map.43.refs_2_.refs_1_
  65.9 3.3 shard_map.42.refs_2_.refs_5_
  69.1 4.7 %shard_map.41.refs_1_.refs_9_ = bf16[48,32,768]{2,1,0:T(8,128)(2,1)} custom-call(bf16[32,256,768]{2,1,0:T(8,128)(2,1)} %in_ref.9), custom_call_target="tpu_custom_call" | custom-call | bytes 65536 | tf_op jit(solution)/shard_map/pallas_call | solution.py:217
  73.8 23.0 %copy.18 = bf16[256,256,256]{2,0,1:T(8,128)(2,1)} copy(bf16[256,256,256]{2,1,0:T(8,128)(2,1)} %param.5) | data formatting | bytes 67108864 | tf_op jit(solution)/shard_map/optimization_barrier | solution.py:304
  96.8 5.1 %collective-permute-done.2.refs_7_ = bf16[48,32,768]{2,1,0:T(8,128)(2,1)} collective-permute-done((bf16[48,32,768]{2,1,0:T(8,128)(2,1)}, bf16[48,32,768]{2,1,0:T(8,128)(2,1)}, u32[]{:S(2)}, u32[]{:S(2)}) %collective-permute-start.2) | collective-permute-done | bytes 2359328 | tf_op jit(solution)/shard_map/ppermute | solution.py:256
  101.9 1.7 collective-permute-start.1
  103.6 0.2 collective-permute-start.8
  103.8 3.0 collective-permute-done.6.refs_8_
  106.8 21.7 %all-gather.4.cloned.1.call-done.refs_0_ = bf16[3072,1024]{1,0:T(8,128)(2,1)} async-done(((bf16[768,1024]{1,0:T(8,128)(2,1)}), bf16[3072,1024]{1,0:T(8,128)(2,1)}) %all-gather.4.cloned.1.call-update) | async-done | bytes 6291472 | tf_op jit(solution)/shard_map/all_gather | solution.py:288
  128.5 0.7 broadcast_in_dim.3.total_ref
  129.2 22.7 %shard_map.46.total_ref = f32[256,256]{1,0:T(8,128)} custom-call(s32[1]{0:T(128)} %bitcast.place_ref, f32[256,256]{1,0:T(8,128)} %broadcast_in_dim.3.total_ref, bf16[256,256,256]{2,1,0:T(8,128)(2,1)} %bitcast.6, bf16[3072,1024]{1,0:T(8,128)(2,1)} %all-gather.4.cloned.1.call-done.refs_0_, ...), custom_call_target="tpu_custom_call", output_to_operand_aliasing={{}: (1, {})} | custom-call | flops 872415232 | bytes 22020096 | tf_op jit(solution)/shard_map/pallas_call | solution.py:162
  152.0 3.9 %collective-permute-done.1.refs_3_.refs_11_ = bf16[48,32,768]{2,1,0:T(8,128)(2,1)} collective-permute-done((bf16[48,32,768]{2,1,0:T(8,128)(2,1)}, bf16[48,32,768]{2,1,0:T(8,128)(2,1)}, u32[]{:S(2)}, u32[]{:S(2)}) %collective-permute-start.1) | collective-permute-done | bytes 2359328 | tf_op jit(solution)/shard_map/ppermute | solution.py:256
  155.9 1.7 collective-permute-start.7
  157.6 0.3 collective-permute-start.11
  157.9 2.9 collective-permute-done.9.refs_4_.refs_12_
  160.7 15.4 %shard_map.47.total_ref = f32[256,256]{1,0:T(8,128)} custom-call(s32[1]{0:T(128)} %bitcast.place_ref, f32[256,256]{1,0:T(8,128)} %shard_map.46.total_ref, bf16[256,256,256]{2,1,0:T(8,128)(2,1)} %bitcast.7, bf16[3072,1024]{1,0:T(8,128)(2,1)} %all-gather.4.cloned.1.call-done.refs_0_, ...), custom_call_target="tpu_custom_call", output_to_operand_aliasing={{}: (1, {})} | custom-call | flops 523449152 | bytes 15728640 | tf_op jit(solution)/shard_map/pallas_call | solution.py:162
  176.2 16.8 %collective-permute-done.7.refs_4_.refs_7_ = bf16[32,32,768]{2,1,0:T(8,128)(2,1)} collective-permute-done((bf16[32,32,768]{2,1,0:T(8,128)(2,1)}, bf16[32,32,768]{2,1,0:T(8,128)(2,1)}, u32[]{:S(2)}, u32[]{:S(2)}) %collective-permute-start.7) | collective-permute-done | bytes 1572896 | tf_op jit(solution)/shard_map/ppermute | solution.py:256
  193.0 1.7 collective-permute-start.10
  194.7 0.2 collective-permute-start.14
  194.9 21.4 %shard_map.48.total_ref = f32[256,256]{1,0:T(8,128)} custom-call(s32[1]{0:T(128)} %bitcast.place_ref, f32[256,256]{1,0:T(8,128)} %shard_map.47.total_ref, bf16[256,256,256]{2,1,0:T(8,128)(2,1)} %bitcast.8, bf16[3072,512]{1,0:T(8,128)(2,1)} %all-gather.6.cloned.1.call-done.refs_0_.refs_1_, ...), custom_call_target="tpu_custom_call", output_to_operand_aliasing={{}: (1, {})} | custom-call | flops 697932160 | bytes 28311552 | tf_op jit(solution)/shard_map/pallas_call | solution.py:162
  216.3 16.4 %shard_map.49.total_ref = f32[256,256]{1,0:T(8,128)} custom-call(s32[1]{0:T(128)} %bitcast.place_ref, f32[256,256]{1,0:T(8,128)} %shard_map.48.total_ref, bf16[256,256,256]{2,1,0:T(8,128)(2,1)} %bitcast.9, bf16[3072,1024]{1,0:T(8,128)(2,1)} %all-gather.4.cloned.1.call-done.refs_0_, ...), custom_call_target="tpu_custom_call", output_to_operand_aliasing={{}: (1, {})} | custom-call | flops 523449152 | bytes 15728640 | tf_op jit(solution)/shard_map/pallas_call | solution.py:162
  232.8 0.4 collective-permute-start.15
  233.1 0.1 collective-permute-start.13
  233.2 0.1 collective-permute-start.17
  233.3 3.2 collective-permute-done.15.refs_5_.refs_4_
  236.6 16.1 %shard_map.50.total_ref = f32[256,256]{1,0:T(8,128)} custom-call(s32[1]{0:T(128)} %bitcast.place_ref, f32[256,256]{1,0:T(8,128)} %shard_map.49.total_ref, bf16[256,256,256]{2,1,0:T(8,128)(2,1)} %bitcast.10, bf16[3072,1024]{1,0:T(8,128)(2,1)} %all-gather.4.cloned.1.call-done.refs_0_, ...), custom_call_target="tpu_custom_call", output_to_operand_aliasing={{}: (1, {})} | custom-call | flops 523449152 | bytes 15728640 | tf_op jit(solution)/shard_map/pallas_call | solution.py:162
  252.7 2.9 all-gather.8.cloned.1.call-done.refs_0_.refs_2_
  255.6 14.5 %shard_map.51.total_ref = f32[256,256]{1,0:T(8,128)} custom-call(s32[1]{0:T(128)} %bitcast.place_ref, f32[256,256]{1,0:T(8,128)} %shard_map.50.total_ref, bf16[256,256,256]{2,1,0:T(8,128)(2,1)} %bitcast.11, bf16[3072,512]{1,0:T(8,128)(2,1)} %all-gather.8.cloned.1.call-done.refs_0_.refs_2_, ...), custom_call_target="tpu_custom_call", output_to_operand_aliasing={{}: (1, {})} | custom-call | flops 436207616 | bytes 18874368 | tf_op jit(solution)/shard_map/pallas_call | solution.py:162
  270.2 1.5 collective-permute-start.16
  271.7 0.2 collective-permute-start.19
  271.9 14.7 %shard_map.52.total_ref = f32[256,256]{1,0:T(8,128)} custom-call(s32[1]{0:T(128)} %bitcast.place_ref, f32[256,256]{1,0:T(8,128)} %shard_map.51.total_ref, bf16[256,256,256]{2,1,0:T(8,128)(2,1)} %bitcast.12, bf16[3072,512]{1,0:T(8,128)(2,1)} %all-gather.8.cloned.1.call-done.refs_0_.refs_2_, ...), custom_call_target="tpu_custom_call", output_to_operand_aliasing={{}: (1, {})} | custom-call | flops 436207616 | bytes 18874368 | tf_op jit(solution)/shard_map/pallas_call | solution.py:162
  286.6 20.6 %shard_map.53.total_ref = f32[256,256]{1,0:T(8,128)} custom-call(s32[1]{0:T(128)} %bitcast.place_ref, f32[256,256]{1,0:T(8,128)} %shard_map.52.total_ref, bf16[256,256,256]{2,1,0:T(8,128)(2,1)} %bitcast.13, bf16[3072,1024]{1,0:T(8,128)(2,1)} %all-gather.4.cloned.1.call-done.refs_0_, ...), custom_call_target="tpu_custom_call", output_to_operand_aliasing={{}: (1, {})} | custom-call | flops 697932160 | bytes 18874368 | tf_op jit(solution)/shard_map/pallas_call | solution.py:162
  307.2 0.4 collective-permute-start.20
  307.6 8.5 %shard_map.54.total_ref = f32[256,256]{1,0:T(8,128)} custom-call(s32[1]{0:T(128)} %bitcast.place_ref, f32[256,256]{1,0:T(8,128)} %shard_map.53.total_ref, bf16[256,256,256]{2,1,0:T(8,128)(2,1)} %bitcast.14, bf16[3072,512]{1,0:T(8,128)(2,1)} %all-gather.8.cloned.1.call-done.refs_0_.refs_2_, ...), custom_call_target="tpu_custom_call", output_to_operand_aliasing={{}: (1, {})} | custom-call | flops 174483040 | bytes 9437184 | tf_op jit(solution)/shard_map/pallas_call | solution.py:162
  316.2 20.6 %shard_map.55 = f32[256,256]{1,0:T(8,128)} custom-call(s32[1]{0:T(128)} %bitcast.place_ref, f32[256,256]{1,0:T(8,128)} %shard_map.54.total_ref, bf16[256,256,256]{2,1,0:T(8,128)(2,1)} %bitcast.15, bf16[3072,1024]{1,0:T(8,128)(2,1)} %all-gather.4.cloned.1.call-done.refs_0_, ...), custom_call_target="tpu_custom_call", output_to_operand_aliasing={{}: (1, {})} | custom-call | flops 697932160 | bytes 18874368 | tf_op jit(solution)/shard_map/pallas_call | solution.py:162
  336.8 1.1 copy.16
  337.8 14.6 %all_to_all.5 = f32[16,16,256]{2,1,0:T(8,128)S(1)} all-to-all(f32[16,16,256]{2,1,0:T(8,128)S(1)} %bitcast.17), channel_id=1, replica_groups=mesh['parts'=2,'row'=4,'col'=4] {'row','col'}, dimensions={0} | all-to-all | bytes 524288 | tf_op jit(solution)/shard_map/all_to_all | solution.py:327
  352.4 0.6 reduce_sum.9
  (33 shorter events, 0.3 us)
Async XLA Ops:
  6.5 122.0 %all-gather.4.cloned.1.call-start = ((), (), s32[]{:S(2)}) async-start(), calls=%async_computation.1 | async-start | bytes 7864320 | tf_op jit(solution)/shard_map/all_gather | solution.py:288
  10.3 184.6 %all-gather.6.cloned.1.call-start = ((), (), s32[]{:S(2)}) async-start(), calls=%async_computation.2 | async-start | bytes 3932160 | tf_op jit(solution)/shard_map/all_gather | solution.py:288
  13.6 7.7 %copy-start = (bf16[32,32,768]{2,1,0:T(8,128)(2,1)S(1)}, bf16[32,32,768]{2,1,0:T(8,128)(2,1)}, u32[]{:S(2)}) copy-start(bf16[32,32,768]{2,1,0:T(8,128)(2,1)} %shard_map.38.refs_1_) | copy-start | bytes 4718596
  13.6 38.5 %collective-permute-start = (bf16[32,32,768]{2,1,0:T(8,128)(2,1)}, bf16[32,32,768]{2,1,0:T(8,128)(2,1)}, u32[]{:S(2)}, u32[]{:S(2)}) collective-permute-start(bf16[32,32,768]{2,1,0:T(8,128)(2,1)} %shard_map.38.refs_1_), channel_id=1, source_target_pairs={{0,8},{4,12},{8,0},{12,4},{1,9},{5,13},{9,1},{13,5},{2,10},{6,14},... | collective-permute-start | bytes 4718600 | tf_op jit(solution)/shard_map/ppermute | solution.py:256
  21.3 75.6 %collective-permute-start.5 = (bf16[48,32,768]{2,1,0:T(8,128)(2,1)}, bf16[48,32,768]{2,1,0:T(8,128)(2,1)}, u32[]{:S(2)}, u32[]{:S(2)}) collective-permute-start(bf16[48,32,768]{2,1,0:T(8,128)(2,1)} %shard_map.39.refs_5_), channel_id=1, source_target_pairs={{0,4},{4,0},{8,12},{12,8},{1,5},{5,1},{9,13},{13,9},{2,6},{6,2},{1... | collective-permute-start | bytes 7077896 | tf_op jit(solution)/shard_map/ppermute | solution.py:256
  21.3 80.6 %collective-permute-start.2 = (bf16[48,32,768]{2,1,0:T(8,128)(2,1)}, bf16[48,32,768]{2,1,0:T(8,128)(2,1)}, u32[]{:S(2)}, u32[]{:S(2)}) collective-permute-start(bf16[48,32,768]{2,1,0:T(8,128)(2,1)} %shard_map.39.refs_5_), channel_id=1, source_target_pairs={{0,8},{4,12},{8,0},{12,4},{1,9},{5,13},{9,1},{13,5},{2,10},{6,14},... | collective-permute-start | bytes 7077896 | tf_op jit(solution)/shard_map/ppermute | solution.py:256
  21.4 75.5 %collective-permute-start.3 = (bf16[32,32,768]{2,1,0:T(8,128)(2,1)S(1)}, bf16[32,32,768]{2,1,0:T(8,128)(2,1)}, u32[]{:S(2)}, u32[]{:S(2)}) collective-permute-start(bf16[32,32,768]{2,1,0:T(8,128)(2,1)S(1)} %copy-done), channel_id=1, source_target_pairs={{0,4},{4,0},{8,12},{12,8},{1,5},{5,1},{9,13},{13,9},{2,6},{6,2},{1... | collective-permute-start | bytes 4718600 | tf_op jit(solution)/shard_map/ppermute | solution.py:256
  52.2 49.7 %collective-permute-start.4 = (bf16[32,32,768]{2,1,0:T(8,128)(2,1)}, bf16[32,32,768]{2,1,0:T(8,128)(2,1)}, u32[]{:S(2)}, u32[]{:S(2)}) collective-permute-start(bf16[32,32,768]{2,1,0:T(8,128)(2,1)} %collective-permute-done.refs_3_), channel_id=1, source_target_pairs={{0,4},{4,0},{8,12},{12,8},{1,5},{5,1},{9,13},{13,9},{2,6},{6,2},{1... | collective-permute-start | bytes 4718600 | tf_op jit(solution)/shard_map/ppermute | solution.py:256
  55.8 199.8 %all-gather.8.cloned.1.call-start = ((), (), s32[]{:S(2)}) async-start(), calls=%async_computation.3 | async-start | bytes 3932160 | tf_op jit(solution)/shard_map/all_gather | solution.py:288
  101.9 4.9 %collective-permute-start.6 = (bf16[48,32,768]{2,1,0:T(8,128)(2,1)}, bf16[48,32,768]{2,1,0:T(8,128)(2,1)}, u32[]{:S(2)}, u32[]{:S(2)}) collective-permute-start(bf16[48,32,768]{2,1,0:T(8,128)(2,1)} %collective-permute-done.2.refs_7_), channel_id=1, source_target_pairs={{0,4},{4,0},{8,12},{12,8},{1,5},{5,1},{9,13},{13,9},{2,6},{6,2},{1... | collective-permute-start | bytes 7077896 | tf_op jit(solution)/shard_map/ppermute | solution.py:256
  101.9 54.0 %collective-permute-start.1 = (bf16[48,32,768]{2,1,0:T(8,128)(2,1)}, bf16[48,32,768]{2,1,0:T(8,128)(2,1)}, u32[]{:S(2)}, u32[]{:S(2)}) collective-permute-start(bf16[48,32,768]{2,1,0:T(8,128)(2,1)} %shard_map.41.refs_1_.refs_9_), channel_id=1, source_target_pairs={{0,8},{4,12},{8,0},{12,4},{1,9},{5,13},{9,1},{13,5},{2,10},{6,14},... | collective-permute-start | bytes 7077896 | tf_op jit(solution)/shard_map/ppermute | solution.py:256
  103.6 54.3 %collective-permute-start.8 = (bf16[48,32,768]{2,1,0:T(8,128)(2,1)}, bf16[48,32,768]{2,1,0:T(8,128)(2,1)}, u32[]{:S(2)}, u32[]{:S(2)}) collective-permute-start(bf16[48,32,768]{2,1,0:T(8,128)(2,1)} %shard_map.41.refs_1_.refs_9_), channel_id=1, source_target_pairs={{0,4},{4,0},{8,12},{12,8},{1,5},{5,1},{9,13},{13,9},{2,6},{6,2},{1... | collective-permute-start | bytes 7077896 | tf_op jit(solution)/shard_map/ppermute | solution.py:256
  155.9 4.9 %collective-permute-start.9 = (bf16[48,32,768]{2,1,0:T(8,128)(2,1)}, bf16[48,32,768]{2,1,0:T(8,128)(2,1)}, u32[]{:S(2)}, u32[]{:S(2)}) collective-permute-start(bf16[48,32,768]{2,1,0:T(8,128)(2,1)} %collective-permute-done.1.refs_3_.refs_11_), channel_id=1, source_target_pairs={{0,4},{4,0},{8,12},{12,8},{1,5},{5,1},{9,13},{13,9},{2,6},{6,2},{1... | collective-permute-start | bytes 7077896 | tf_op jit(solution)/shard_map/ppermute | solution.py:256
  155.9 37.1 %collective-permute-start.7 = (bf16[32,32,768]{2,1,0:T(8,128)(2,1)}, bf16[32,32,768]{2,1,0:T(8,128)(2,1)}, u32[]{:S(2)}, u32[]{:S(2)}) collective-permute-start(bf16[32,32,768]{2,1,0:T(8,128)(2,1)} %shard_map.42.refs_2_.refs_5_), channel_id=1, source_target_pairs={{0,8},{4,12},{8,0},{12,4},{1,9},{5,13},{9,1},{13,5},{2,10},{6,14},... | collective-permute-start | bytes 4718600 | tf_op jit(solution)/shard_map/ppermute | solution.py:256
  157.6 35.4 %copy-start.1 = (bf16[32,32,768]{2,1,0:T(8,128)(2,1)S(1)}, bf16[32,32,768]{2,1,0:T(8,128)(2,1)}, u32[]{:S(2)}) copy-start(bf16[32,32,768]{2,1,0:T(8,128)(2,1)} %shard_map.43.refs_2_.refs_1_) | copy-start | bytes 4718596
  157.6 58.7 %collective-permute-start.11 = (bf16[32,32,768]{2,1,0:T(8,128)(2,1)}, bf16[32,32,768]{2,1,0:T(8,128)(2,1)}, u32[]{:S(2)}, u32[]{:S(2)}) collective-permute-start(bf16[32,32,768]{2,1,0:T(8,128)(2,1)} %shard_map.42.refs_2_.refs_5_), channel_id=1, source_target_pairs={{0,4},{4,0},{8,12},{12,8},{1,5},{5,1},{9,13},{13,9},{2,6},{6,2},{1... | collective-permute-start | bytes 4718600 | tf_op jit(solution)/shard_map/ppermute | solution.py:256
  193.0 23.3 %collective-permute-start.12 = (bf16[32,32,768]{2,1,0:T(8,128)(2,1)}, bf16[32,32,768]{2,1,0:T(8,128)(2,1)}, u32[]{:S(2)}, u32[]{:S(2)}) collective-permute-start(bf16[32,32,768]{2,1,0:T(8,128)(2,1)} %collective-permute-done.7.refs_4_.refs_7_), channel_id=1, source_target_pairs={{0,4},{4,0},{8,12},{12,8},{1,5},{5,1},{9,13},{13,9},{2,6},{6,2},{1... | collective-permute-start | bytes 4718600 | tf_op jit(solution)/shard_map/ppermute | solution.py:256
  193.0 39.7 %collective-permute-start.10 = (bf16[32,32,768]{2,1,0:T(8,128)(2,1)S(1)}, bf16[32,32,768]{2,1,0:T(8,128)(2,1)}, u32[]{:S(2)}, u32[]{:S(2)}) collective-permute-start(bf16[32,32,768]{2,1,0:T(8,128)(2,1)S(1)} %copy-done.1), channel_id=1, source_target_pairs={{0,8},{4,12},{8,0},{12,4},{1,9},{5,13},{9,1},{13,5},{2,10},{6,14},... | collective-permute-start | bytes 4718600 | tf_op jit(solution)/shard_map/ppermute | solution.py:256
  194.7 38.7 %collective-permute-start.14 = (bf16[32,32,768]{2,1,0:T(8,128)(2,1)S(1)}, bf16[32,32,768]{2,1,0:T(8,128)(2,1)}, u32[]{:S(2)}, u32[]{:S(2)}) collective-permute-start(bf16[32,32,768]{2,1,0:T(8,128)(2,1)S(1)} %copy-done.1), channel_id=1, source_target_pairs={{0,4},{4,0},{8,12},{12,8},{1,5},{5,1},{9,13},{13,9},{2,6},{6,2},{1... | collective-permute-start | bytes 4718600 | tf_op jit(solution)/shard_map/ppermute | solution.py:256
  232.8 3.8 %collective-permute-start.15 = (bf16[32,32,768]{2,1,0:T(8,128)(2,1)}, bf16[32,32,768]{2,1,0:T(8,128)(2,1)}, u32[]{:S(2)}, u32[]{:S(2)}) collective-permute-start(bf16[32,32,768]{2,1,0:T(8,128)(2,1)} %collective-permute-done.10.refs_4_.refs_3_), channel_id=1, source_target_pairs={{0,4},{4,0},{8,12},{12,8},{1,5},{5,1},{9,13},{13,9},{2,6},{6,2},{1... | collective-permute-start | bytes 4718600 | tf_op jit(solution)/shard_map/ppermute | solution.py:256
  233.1 37.0 %collective-permute-start.13 = (bf16[32,32,768]{2,1,0:T(8,128)(2,1)}, bf16[32,32,768]{2,1,0:T(8,128)(2,1)}, u32[]{:S(2)}, u32[]{:S(2)}) collective-permute-start(bf16[32,32,768]{2,1,0:T(8,128)(2,1)} %shard_map.44.refs_3_), channel_id=1, source_target_pairs={{0,8},{4,12},{8,0},{12,4},{1,9},{5,13},{9,1},{13,5},{2,10},{6,14},... | collective-permute-start | bytes 4718600 | tf_op jit(solution)/shard_map/ppermute | solution.py:256
  233.2 53.4 %collective-permute-start.17 = (bf16[32,32,768]{2,1,0:T(8,128)(2,1)}, bf16[32,32,768]{2,1,0:T(8,128)(2,1)}, u32[]{:S(2)}, u32[]{:S(2)}) collective-permute-start(bf16[32,32,768]{2,1,0:T(8,128)(2,1)} %shard_map.44.refs_3_), channel_id=1, source_target_pairs={{0,4},{4,0},{8,12},{12,8},{1,5},{5,1},{9,13},{13,9},{2,6},{6,2},{1... | collective-permute-start | bytes 4718600 | tf_op jit(solution)/shard_map/ppermute | solution.py:256
  252.7 17.5 %copy-start.2 = (bf16[32,32,768]{2,1,0:T(8,128)(2,1)S(1)}, bf16[32,32,768]{2,1,0:T(8,128)(2,1)}, u32[]{:S(2)}) copy-start(bf16[32,32,768]{2,1,0:T(8,128)(2,1)} %shard_map.45.refs_3_) | copy-start | bytes 4718596
  270.1 16.5 %collective-permute-start.18 = (bf16[32,32,768]{2,1,0:T(8,128)(2,1)}, bf16[32,32,768]{2,1,0:T(8,128)(2,1)}, u32[]{:S(2)}, u32[]{:S(2)}) collective-permute-start(bf16[32,32,768]{2,1,0:T(8,128)(2,1)} %collective-permute-done.13.refs_5_), channel_id=1, source_target_pairs={{0,4},{4,0},{8,12},{12,8},{1,5},{5,1},{9,13},{13,9},{2,6},{6,2},{1... | collective-permute-start | bytes 4718600 | tf_op jit(solution)/shard_map/ppermute | solution.py:256
  270.2 37.0 %collective-permute-start.16 = (bf16[32,32,768]{2,1,0:T(8,128)(2,1)S(1)}, bf16[32,32,768]{2,1,0:T(8,128)(2,1)}, u32[]{:S(2)}, u32[]{:S(2)}) collective-permute-start(bf16[32,32,768]{2,1,0:T(8,128)(2,1)S(1)} %copy-done.2), channel_id=1, source_target_pairs={{0,8},{4,12},{8,0},{12,4},{1,9},{5,13},{9,1},{13,5},{2,10},{6,14},... | collective-permute-start | bytes 4718600 | tf_op jit(solution)/shard_map/ppermute | solution.py:256
  271.7 44.4 %collective-permute-start.19 = (bf16[32,32,768]{2,1,0:T(8,128)(2,1)S(1)}, bf16[32,32,768]{2,1,0:T(8,128)(2,1)}, u32[]{:S(2)}, u32[]{:S(2)}) collective-permute-start(bf16[32,32,768]{2,1,0:T(8,128)(2,1)S(1)} %copy-done.2), channel_id=1, source_target_pairs={{0,4},{4,0},{8,12},{12,8},{1,5},{5,1},{9,13},{13,9},{2,6},{6,2},{1... | collective-permute-start | bytes 4718600 | tf_op jit(solution)/shard_map/ppermute | solution.py:256
  307.2 8.9 %collective-permute-start.20 = (bf16[32,32,768]{2,1,0:T(8,128)(2,1)}, bf16[32,32,768]{2,1,0:T(8,128)(2,1)}, u32[]{:S(2)}, u32[]{:S(2)}) collective-permute-start(bf16[32,32,768]{2,1,0:T(8,128)(2,1)} %collective-permute-done.16.refs_5_), channel_id=1, source_target_pairs={{0,4},{4,0},{8,12},{12,8},{1,5},{5,1},{9,13},{13,9},{2,6},{6,2},{1... | collective-permute-start | bytes 4718600 | tf_op jit(solution)/shard_map/ppermute | solution.py:256
Sparse Core Ops, SparseCore 0:
  10.4 118.0 all-gather.3
  130.1 61.7 all-gather.5
  193.4 62.1 all-gather.7

commit v6 on v5

--- a/solution.py
+++ b/solution.py
@@ -8,7 +8,7 @@
 from jax.experimental.pallas import tpu as pltpu
 from jax.sharding import PartitionSpec as P
 
-CHUNK_SHARES = (2, 3, 3, 2, 2, 2, 2)
+CHUNK_SHARES = (1, 4, 3, 2, 2, 2, 2)
 PIECES = ((0, 8, 0), (0, 4, 1), (4, 4, 1))
 
 

time: 363 us -> 414 us (1.14)
  waiting for transfers between devices: 89.9 us -> 141 us
    ppermute x21, waiting for transfers between devices: 65.2 us -> 141 us  [swap(): return lax.ppermute(block, axis, [(i, i ^ bit) for i in range(size)])]
    all_gather x3, waiting for transfers between devices: 24.7 us -> 0.02 us  [gathered(): return [lax.all_gather(part, 'col', axis=0, tiled=True) for part in parts]]
  transfers between devices with their start and end apart: 24 -> 24, of which waited for: 9 -> 8; matrix products, arithmetic and copies ran while one was open for 7% -> 6% of each run, Pallas kernels for 50% -> 44%
where the time goes in v6:
time: 414 us; the launch traced here: 410 us
  Pallas kernels  204 us (49%)
  waiting for transfers between devices  141 us (34%)
  local copies, waits for them, and re-layouts  25.3 us (6%)
  blocking collectives  15.4 us (4%)
  between operations  13.8 us (3%)
  starting transfers between devices  10.8 us (3%)
    pallas_call x10, Pallas kernels, add_ladder(): pl.pallas_call(functools.partial(ladder_kernel, pieces=pieces, chunk_step...  170 us
    ppermute x21, waiting for transfers between devices, swap(): return lax.ppermute(block, axis, [(i, i ^ bit) for i in range(size)])  141 us
    pallas_call x7, Pallas kernels, turn(): pl.pallas_call(turn_kernel, out_shape=jax.ShapeDtypeStruct((size, outer,...  25.8 us
    optimization_barrier x1, local copies, waits for them, and re-layouts, on_device(): owns, amplitudes = together((owns, amplitudes))  23.5 us
    all_to_all x1, blocking collectives, on_device(): return lax.all_to_all(shares, ('row', 'col'), 0, 0, tiled=True).sum(axis=0)  15.4 us
    ppermute x21, starting transfers between devices, swap(): return lax.ppermute(block, axis, [(i, i ^ bit) for i in range(size)])  10.5 us
  transfers between devices with their start and end apart: 24, of which 8 were waited for; matrix products, arithmetic and copies ran while one was open for 6% of the time, Pallas kernels for 44%

profile of v6, /device:TPU:0, one launch (start us, length us, event | category | flops | bytes accessed | tf_op | source)
XLA Modules:
  0.0 410.4 jit_solution(7400363662741917198)
XLA Ops:
  6.5 3.8 shard_map.37
  10.3 0.0 all-gather.6.cloned.1.call-start
  10.4 2.6 shard_map.38.refs_1_
  13.0 5.4 %shard_map.39.refs_5_ = bf16[64,32,768]{2,1,0:T(8,128)(2,1)} custom-call(bf16[32,256,768]{2,1,0:T(8,128)(2,1)} %in_ref.9), custom_call_target="tpu_custom_call" | custom-call | bytes 65536 | tf_op jit(solution)/shard_map/pallas_call | solution.py:217
  18.4 0.5 collective-permute-start.5
  18.9 2.5 collective-permute-start.2
  21.4 0.1 collective-permute-start
  21.4 0.2 collective-permute-start.3
  21.6 85.6 %collective-permute-done.refs_3_ = bf16[16,32,768]{2,1,0:T(8,128)(2,1)S(1)} collective-permute-done((bf16[16,32,768]{2,1,0:T(8,128)(2,1)S(1)}, bf16[16,32,768]{2,1,0:T(8,128)(2,1)S(1)}, u32[]{:S(2)}, u32[]{:S(2)}) %collective-permute-start) | collective-permute-done | bytes 786464 | tf_op jit(solution)/shard_map/ppermute | solution.py:256
  107.2 3.9 shard_map.40
  111.1 0.3 all-gather.8.cloned.1.call-start
  111.4 3.3 shard_map.45.refs_3_
  114.7 3.3 shard_map.44.refs_3_
  118.0 3.3 shard_map.43.refs_2_.refs_1_
  121.2 3.3 shard_map.42.refs_2_.refs_5_
  124.5 4.7 %shard_map.41.refs_1_.refs_9_ = bf16[48,32,768]{2,1,0:T(8,128)(2,1)} custom-call(bf16[32,256,768]{2,1,0:T(8,128)(2,1)} %in_ref.9), custom_call_target="tpu_custom_call" | custom-call | bytes 65536 | tf_op jit(solution)/shard_map/pallas_call | solution.py:217
  129.2 23.5 %copy.18 = bf16[256,256,256]{2,0,1:T(8,128)(2,1)} copy(bf16[256,256,256]{2,1,0:T(8,128)(2,1)} %param.5) | data formatting | bytes 67108864 | tf_op jit(solution)/shard_map/optimization_barrier | solution.py:304
  152.7 0.2 collective-permute-start.6
  152.9 1.8 collective-permute-start.1
  154.8 4.0 collective-permute-done.6.refs_8_
  158.8 0.7 broadcast_in_dim.3.total_ref
  159.5 22.8 %shard_map.46.total_ref = f32[256,256]{1,0:T(8,128)} custom-call(s32[1]{0:T(128)} %bitcast.place_ref, f32[256,256]{1,0:T(8,128)} %broadcast_in_dim.3.total_ref, bf16[256,256,256]{2,1,0:T(8,128)(2,1)} %bitcast.6, bf16[3072,1024]{1,0:T(8,128)(2,1)} %all-gather.4.cloned.1.call-done.refs_0_, ...), custom_call_target="tpu_custom_call", output_to_operand_aliasing={{}: (1, {})} | custom-call | flops 872415232 | bytes 22020096 | tf_op jit(solution)/shard_map/pallas_call | solution.py:162
  182.3 24.5 %collective-permute-done.1.refs_3_.refs_11_ = bf16[48,32,768]{2,1,0:T(8,128)(2,1)} collective-permute-done((bf16[48,32,768]{2,1,0:T(8,128)(2,1)}, bf16[48,32,768]{2,1,0:T(8,128)(2,1)}, u32[]{:S(2)}, u32[]{:S(2)}) %collective-permute-start.1) | collective-permute-done | bytes 2359328 | tf_op jit(solution)/shard_map/ppermute | solution.py:256
  206.8 1.7 collective-permute-start.7
  208.5 0.3 collective-permute-start.11
  208.8 2.8 collective-permute-done.9.refs_4_.refs_12_
  211.6 15.4 %shard_map.47.total_ref = f32[256,256]{1,0:T(8,128)} custom-call(s32[1]{0:T(128)} %bitcast.place_ref, f32[256,256]{1,0:T(8,128)} %shard_map.46.total_ref, bf16[256,256,256]{2,1,0:T(8,128)(2,1)} %bitcast.7, bf16[3072,1024]{1,0:T(8,128)(2,1)} %all-gather.4.cloned.1.call-done.refs_0_, ...), custom_call_target="tpu_custom_call", output_to_operand_aliasing={{}: (1, {})} | custom-call | flops 523449152 | bytes 15728640 | tf_op jit(solution)/shard_map/pallas_call | solution.py:162
  227.1 16.8 %collective-permute-done.7.refs_4_.refs_7_ = bf16[32,32,768]{2,1,0:T(8,128)(2,1)} collective-permute-done((bf16[32,32,768]{2,1,0:T(8,128)(2,1)}, bf16[32,32,768]{2,1,0:T(8,128)(2,1)}, u32[]{:S(2)}, u32[]{:S(2)}) %collective-permute-start.7) | collective-permute-done | bytes 1572896 | tf_op jit(solution)/shard_map/ppermute | solution.py:256
  243.9 1.7 collective-permute-start.10
  245.6 0.2 collective-permute-start.14
  245.9 20.8 %shard_map.48.total_ref = f32[256,256]{1,0:T(8,128)} custom-call(s32[1]{0:T(128)} %bitcast.place_ref, f32[256,256]{1,0:T(8,128)} %shard_map.47.total_ref, bf16[256,256,256]{2,1,0:T(8,128)(2,1)} %bitcast.8, bf16[3072,512]{1,0:T(8,128)(2,1)} %all-gather.6.cloned.1.call-done.refs_0_.refs_1_, ...), custom_call_target="tpu_custom_call", output_to_operand_aliasing={{}: (1, {})} | custom-call | flops 697932160 | bytes 28311552 | tf_op jit(solution)/shard_map/pallas_call | solution.py:162
  266.7 16.4 %shard_map.49.total_ref = f32[256,256]{1,0:T(8,128)} custom-call(s32[1]{0:T(128)} %bitcast.place_ref, f32[256,256]{1,0:T(8,128)} %shard_map.48.total_ref, bf16[256,256,256]{2,1,0:T(8,128)(2,1)} %bitcast.9, bf16[3072,1024]{1,0:T(8,128)(2,1)} %all-gather.4.cloned.1.call-done.refs_0_, ...), custom_call_target="tpu_custom_call", output_to_operand_aliasing={{}: (1, {})} | custom-call | flops 523449152 | bytes 15728640 | tf_op jit(solution)/shard_map/pallas_call | solution.py:162
  283.1 0.4 collective-permute-start.15
  283.5 0.3 collective-permute-start.13
  283.7 3.2 collective-permute-done.15.refs_5_.refs_4_
  286.9 16.1 %shard_map.50.total_ref = f32[256,256]{1,0:T(8,128)} custom-call(s32[1]{0:T(128)} %bitcast.place_ref, f32[256,256]{1,0:T(8,128)} %shard_map.49.total_ref, bf16[256,256,256]{2,1,0:T(8,128)(2,1)} %bitcast.10, bf16[3072,1024]{1,0:T(8,128)(2,1)} %all-gather.4.cloned.1.call-done.refs_0_, ...), custom_call_target="tpu_custom_call", output_to_operand_aliasing={{}: (1, {})} | custom-call | flops 523449152 | bytes 15728640 | tf_op jit(solution)/shard_map/pallas_call | solution.py:162
  303.0 14.4 %shard_map.51.total_ref = f32[256,256]{1,0:T(8,128)} custom-call(s32[1]{0:T(128)} %bitcast.place_ref, f32[256,256]{1,0:T(8,128)} %shard_map.50.total_ref, bf16[256,256,256]{2,1,0:T(8,128)(2,1)} %bitcast.11, bf16[3072,512]{1,0:T(8,128)(2,1)} %all-gather.8.cloned.1.call-done.refs_0_.refs_2_, ...), custom_call_target="tpu_custom_call", output_to_operand_aliasing={{}: (1, {})} | custom-call | flops 436207616 | bytes 18874368 | tf_op jit(solution)/shard_map/pallas_call | solution.py:162
  317.4 2.8 collective-permute-done.13.refs_5_
  320.3 0.3 collective-permute-start.16
  320.6 0.2 collective-permute-start.19
  320.9 14.7 %shard_map.52.total_ref = f32[256,256]{1,0:T(8,128)} custom-call(s32[1]{0:T(128)} %bitcast.place_ref, f32[256,256]{1,0:T(8,128)} %shard_map.51.total_ref, bf16[256,256,256]{2,1,0:T(8,128)(2,1)} %bitcast.12, bf16[3072,512]{1,0:T(8,128)(2,1)} %all-gather.8.cloned.1.call-done.refs_0_.refs_2_, ...), custom_call_target="tpu_custom_call", output_to_operand_aliasing={{}: (1, {})} | custom-call | flops 436207616 | bytes 18874368 | tf_op jit(solution)/shard_map/pallas_call | solution.py:162
  335.6 20.6 %shard_map.53.total_ref = f32[256,256]{1,0:T(8,128)} custom-call(s32[1]{0:T(128)} %bitcast.place_ref, f32[256,256]{1,0:T(8,128)} %shard_map.52.total_ref, bf16[256,256,256]{2,1,0:T(8,128)(2,1)} %bitcast.13, bf16[3072,1024]{1,0:T(8,128)(2,1)} %all-gather.4.cloned.1.call-done.refs_0_, ...), custom_call_target="tpu_custom_call", output_to_operand_aliasing={{}: (1, {})} | custom-call | flops 697932160 | bytes 18874368 | tf_op jit(solution)/shard_map/pallas_call | solution.py:162
  356.2 1.0 collective-permute-done.16.refs_5_
  357.2 8.5 %shard_map.54.total_ref = f32[256,256]{1,0:T(8,128)} custom-call(s32[1]{0:T(128)} %bitcast.place_ref, f32[256,256]{1,0:T(8,128)} %shard_map.53.total_ref, bf16[256,256,256]{2,1,0:T(8,128)(2,1)} %bitcast.14, bf16[3072,512]{1,0:T(8,128)(2,1)} %all-gather.8.cloned.1.call-done.refs_0_.refs_2_, ...), custom_call_target="tpu_custom_call", output_to_operand_aliasing={{}: (1, {})} | custom-call | flops 174483040 | bytes 9437184 | tf_op jit(solution)/shard_map/pallas_call | solution.py:162
  365.7 20.6 %shard_map.55 = f32[256,256]{1,0:T(8,128)} custom-call(s32[1]{0:T(128)} %bitcast.place_ref, f32[256,256]{1,0:T(8,128)} %shard_map.54.total_ref, bf16[256,256,256]{2,1,0:T(8,128)(2,1)} %bitcast.15, bf16[3072,1024]{1,0:T(8,128)(2,1)} %all-gather.4.cloned.1.call-done.refs_0_, ...), custom_call_target="tpu_custom_call", output_to_operand_aliasing={{}: (1, {})} | custom-call | flops 697932160 | bytes 18874368 | tf_op jit(solution)/shard_map/pallas_call | solution.py:162
  386.3 1.1 copy.16
  387.4 15.4 %all_to_all.5 = f32[16,16,256]{2,1,0:T(8,128)S(1)} all-to-all(f32[16,16,256]{2,1,0:T(8,128)S(1)} %bitcast.17), channel_id=1, replica_groups=mesh['parts'=2,'row'=4,'col'=4] {'row','col'}, dimensions={0} | all-to-all | bytes 524288 | tf_op jit(solution)/shard_map/all_to_all | solution.py:327
  402.8 0.6 reduce_sum.9
  (35 shorter events, 0.2 us)
Async XLA Ops:
  6.5 152.3 %all-gather.4.cloned.1.call-start = ((), (), s32[]{:S(2)}) async-start(), calls=%async_computation.1 | async-start | bytes 7864320 | tf_op jit(solution)/shard_map/all_gather | solution.py:288
  10.3 235.6 %all-gather.6.cloned.1.call-start = ((), (), s32[]{:S(2)}) async-start(), calls=%async_computation.2 | async-start | bytes 3932160 | tf_op jit(solution)/shard_map/all_gather | solution.py:288
  13.0 8.4 %copy-start.1 = (bf16[16,32,768]{2,1,0:T(8,128)(2,1)S(1)}, bf16[16,32,768]{2,1,0:T(8,128)(2,1)}, u32[]{:S(2)}) copy-start(bf16[16,32,768]{2,1,0:T(8,128)(2,1)} %shard_map.38.refs_1_) | copy-start | bytes 2359300
  18.4 134.3 %collective-permute-start.5 = (bf16[64,32,768]{2,1,0:T(8,128)(2,1)}, bf16[64,32,768]{2,1,0:T(8,128)(2,1)}, u32[]{:S(2)}, u32[]{:S(2)}) collective-permute-start(bf16[64,32,768]{2,1,0:T(8,128)(2,1)} %shard_map.39.refs_5_), channel_id=1, source_target_pairs={{0,4},{4,0},{8,12},{12,8},{1,5},{5,1},{9,13},{13,9},{2,6},{6,2},{1... | collective-permute-start | bytes 9437192 | tf_op jit(solution)/shard_map/ppermute | solution.py:256
  18.9 133.8 %collective-permute-start.2 = (bf16[64,32,768]{2,1,0:T(8,128)(2,1)}, bf16[64,32,768]{2,1,0:T(8,128)(2,1)}, u32[]{:S(2)}, u32[]{:S(2)}) collective-permute-start(bf16[64,32,768]{2,1,0:T(8,128)(2,1)} %shard_map.39.refs_5_), channel_id=1, source_target_pairs={{0,8},{4,12},{8,0},{12,4},{1,9},{5,13},{9,1},{13,5},{2,10},{6,14},... | collective-permute-start | bytes 9437192 | tf_op jit(solution)/shard_map/ppermute | solution.py:256
  21.4 85.8 %collective-permute-start = (bf16[16,32,768]{2,1,0:T(8,128)(2,1)S(1)}, bf16[16,32,768]{2,1,0:T(8,128)(2,1)S(1)}, u32[]{:S(2)}, u32[]{:S(2)}) collective-permute-start(bf16[16,32,768]{2,1,0:T(8,128)(2,1)S(1)} %copy-done.1), channel_id=1, source_target_pairs={{0,8},{4,12},{8,0},{12,4},{1,9},{5,13},{9,1},{13,5},{2,10},{6,14},... | collective-permute-start | bytes 2359304 | tf_op jit(solution)/shard_map/ppermute | solution.py:256
  21.4 131.3 %collective-permute-start.3 = (bf16[16,32,768]{2,1,0:T(8,128)(2,1)S(1)}, bf16[16,32,768]{2,1,0:T(8,128)(2,1)}, u32[]{:S(2)}, u32[]{:S(2)}) collective-permute-start(bf16[16,32,768]{2,1,0:T(8,128)(2,1)S(1)} %copy-done.1), channel_id=1, source_target_pairs={{0,4},{4,0},{8,12},{12,8},{1,5},{5,1},{9,13},{13,9},{2,6},{6,2},{1... | collective-permute-start | bytes 2359304 | tf_op jit(solution)/shard_map/ppermute | solution.py:256
  107.2 3.9 copy-start.2
  107.2 45.5 %collective-permute-start.4 = (bf16[16,32,768]{2,1,0:T(8,128)(2,1)S(1)}, bf16[16,32,768]{2,1,0:T(8,128)(2,1)}, u32[]{:S(2)}, u32[]{:S(2)}) collective-permute-start(bf16[16,32,768]{2,1,0:T(8,128)(2,1)S(1)} %collective-permute-done.refs_3_), channel_id=1, source_target_pairs={{0,4},{4,0},{8,12},{12,8},{1,5},{5,1},{9,13},{13,9},{2,6},{6,2},{1... | collective-permute-start | bytes 2359304 | tf_op jit(solution)/shard_map/ppermute | solution.py:256
  111.1 191.9 %all-gather.8.cloned.1.call-start = ((), (), s32[]{:S(2)}) async-start(), calls=%async_computation.3 | async-start | bytes 3932160 | tf_op jit(solution)/shard_map/all_gather | solution.py:288
  152.7 6.1 %collective-permute-start.6 = (bf16[64,32,768]{2,1,0:T(8,128)(2,1)}, bf16[64,32,768]{2,1,0:T(8,128)(2,1)}, u32[]{:S(2)}, u32[]{:S(2)}) collective-permute-start(bf16[64,32,768]{2,1,0:T(8,128)(2,1)} %collective-permute-done.2.refs_7_), channel_id=1, source_target_pairs={{0,4},{4,0},{8,12},{12,8},{1,5},{5,1},{9,13},{13,9},{2,6},{6,2},{1... | collective-permute-start | bytes 9437192 | tf_op jit(solution)/shard_map/ppermute | solution.py:256
  152.9 53.8 %collective-permute-start.1 = (bf16[48,32,768]{2,1,0:T(8,128)(2,1)}, bf16[48,32,768]{2,1,0:T(8,128)(2,1)}, u32[]{:S(2)}, u32[]{:S(2)}) collective-permute-start(bf16[48,32,768]{2,1,0:T(8,128)(2,1)} %shard_map.41.refs_1_.refs_9_), channel_id=1, source_target_pairs={{0,8},{4,12},{8,0},{12,4},{1,9},{5,13},{9,1},{13,5},{2,10},{6,14},... | collective-permute-start | bytes 7077896 | tf_op jit(solution)/shard_map/ppermute | solution.py:256
  154.7 54.1 %collective-permute-start.8 = (bf16[48,32,768]{2,1,0:T(8,128)(2,1)}, bf16[48,32,768]{2,1,0:T(8,128)(2,1)}, u32[]{:S(2)}, u32[]{:S(2)}) collective-permute-start(bf16[48,32,768]{2,1,0:T(8,128)(2,1)} %shard_map.41.refs_1_.refs_9_), channel_id=1, source_target_pairs={{0,4},{4,0},{8,12},{12,8},{1,5},{5,1},{9,13},{13,9},{2,6},{6,2},{1... | collective-permute-start | bytes 7077896 | tf_op jit(solution)/shard_map/ppermute | solution.py:256
  206.8 4.9 %collective-permute-start.9 = (bf16[48,32,768]{2,1,0:T(8,128)(2,1)}, bf16[48,32,768]{2,1,0:T(8,128)(2,1)}, u32[]{:S(2)}, u32[]{:S(2)}) collective-permute-start(bf16[48,32,768]{2,1,0:T(8,128)(2,1)} %collective-permute-done.1.refs_3_.refs_11_), channel_id=1, source_target_pairs={{0,4},{4,0},{8,12},{12,8},{1,5},{5,1},{9,13},{13,9},{2,6},{6,2},{1... | collective-permute-start | bytes 7077896 | tf_op jit(solution)/shard_map/ppermute | solution.py:256
  206.8 37.1 %collective-permute-start.7 = (bf16[32,32,768]{2,1,0:T(8,128)(2,1)}, bf16[32,32,768]{2,1,0:T(8,128)(2,1)}, u32[]{:S(2)}, u32[]{:S(2)}) collective-permute-start(bf16[32,32,768]{2,1,0:T(8,128)(2,1)} %shard_map.42.refs_2_.refs_5_), channel_id=1, source_target_pairs={{0,8},{4,12},{8,0},{12,4},{1,9},{5,13},{9,1},{13,5},{2,10},{6,14},... | collective-permute-start | bytes 4718600 | tf_op jit(solution)/shard_map/ppermute | solution.py:256
  208.5 35.4 %copy-start = (bf16[32,32,768]{2,1,0:T(8,128)(2,1)S(1)}, bf16[32,32,768]{2,1,0:T(8,128)(2,1)}, u32[]{:S(2)}) copy-start(bf16[32,32,768]{2,1,0:T(8,128)(2,1)} %shard_map.43.refs_2_.refs_1_) | copy-start | bytes 4718596
  208.5 58.1 %collective-permute-start.11 = (bf16[32,32,768]{2,1,0:T(8,128)(2,1)}, bf16[32,32,768]{2,1,0:T(8,128)(2,1)}, u32[]{:S(2)}, u32[]{:S(2)}) collective-permute-start(bf16[32,32,768]{2,1,0:T(8,128)(2,1)} %shard_map.42.refs_2_.refs_5_), channel_id=1, source_target_pairs={{0,4},{4,0},{8,12},{12,8},{1,5},{5,1},{9,13},{13,9},{2,6},{6,2},{1... | collective-permute-start | bytes 4718600 | tf_op jit(solution)/shard_map/ppermute | solution.py:256
  243.9 22.8 %collective-permute-start.12 = (bf16[32,32,768]{2,1,0:T(8,128)(2,1)}, bf16[32,32,768]{2,1,0:T(8,128)(2,1)}, u32[]{:S(2)}, u32[]{:S(2)}) collective-permute-start(bf16[32,32,768]{2,1,0:T(8,128)(2,1)} %collective-permute-done.7.refs_4_.refs_7_), channel_id=1, source_target_pairs={{0,4},{4,0},{8,12},{12,8},{1,5},{5,1},{9,13},{13,9},{2,6},{6,2},{1... | collective-permute-start | bytes 4718600 | tf_op jit(solution)/shard_map/ppermute | solution.py:256
  243.9 39.2 %collective-permute-start.10 = (bf16[32,32,768]{2,1,0:T(8,128)(2,1)S(1)}, bf16[32,32,768]{2,1,0:T(8,128)(2,1)}, u32[]{:S(2)}, u32[]{:S(2)}) collective-permute-start(bf16[32,32,768]{2,1,0:T(8,128)(2,1)S(1)} %copy-done), channel_id=1, source_target_pairs={{0,8},{4,12},{8,0},{12,4},{1,9},{5,13},{9,1},{13,5},{2,10},{6,14},... | collective-permute-start | bytes 4718600 | tf_op jit(solution)/shard_map/ppermute | solution.py:256
  245.6 38.1 %collective-permute-start.14 = (bf16[32,32,768]{2,1,0:T(8,128)(2,1)S(1)}, bf16[32,32,768]{2,1,0:T(8,128)(2,1)}, u32[]{:S(2)}, u32[]{:S(2)}) collective-permute-start(bf16[32,32,768]{2,1,0:T(8,128)(2,1)S(1)} %copy-done), channel_id=1, source_target_pairs={{0,4},{4,0},{8,12},{12,8},{1,5},{5,1},{9,13},{13,9},{2,6},{6,2},{1... | collective-permute-start | bytes 4718600 | tf_op jit(solution)/shard_map/ppermute | solution.py:256
  283.1 3.8 collective-permute-start.15
  283.5 36.8 %collective-permute-start.13 = (bf16[32,32,768]{2,1,0:T(8,128)(2,1)}, bf16[32,32,768]{2,1,0:T(8,128)(2,1)}, u32[]{:S(2)}, u32[]{:S(2)}) collective-permute-start(bf16[32,32,768]{2,1,0:T(8,128)(2,1)} %shard_map.44.refs_3_), channel_id=1, source_target_pairs={{0,8},{4,12},{8,0},{12,4},{1,9},{5,13},{9,1},{13,5},{2,10},{6,14},... | collective-permute-start | bytes 4718600 | tf_op jit(solution)/shard_map/ppermute | solution.py:256
  283.7 51.8 %collective-permute-start.17 = (bf16[32,32,768]{2,1,0:T(8,128)(2,1)}, bf16[32,32,768]{2,1,0:T(8,128)(2,1)}, u32[]{:S(2)}, u32[]{:S(2)}) collective-permute-start(bf16[32,32,768]{2,1,0:T(8,128)(2,1)} %shard_map.44.refs_3_), channel_id=1, source_target_pairs={{0,4},{4,0},{8,12},{12,8},{1,5},{5,1},{9,13},{13,9},{2,6},{6,2},{1... | collective-permute-start | bytes 4718600 | tf_op jit(solution)/shard_map/ppermute | solution.py:256
  303.0 17.3 %copy-start.3 = (bf16[32,32,768]{2,1,0:T(8,128)(2,1)S(1)}, bf16[32,32,768]{2,1,0:T(8,128)(2,1)}, u32[]{:S(2)}) copy-start(bf16[32,32,768]{2,1,0:T(8,128)(2,1)} %shard_map.45.refs_3_) | copy-start | bytes 4718596
  320.3 15.3 %collective-permute-start.18 = (bf16[32,32,768]{2,1,0:T(8,128)(2,1)}, bf16[32,32,768]{2,1,0:T(8,128)(2,1)}, u32[]{:S(2)}, u32[]{:S(2)}) collective-permute-start(bf16[32,32,768]{2,1,0:T(8,128)(2,1)} %collective-permute-done.13.refs_5_), channel_id=1, source_target_pairs={{0,4},{4,0},{8,12},{12,8},{1,5},{5,1},{9,13},{13,9},{2,6},{6,2},{1... | collective-permute-start | bytes 4718600 | tf_op jit(solution)/shard_map/ppermute | solution.py:256
  320.3 36.9 %collective-permute-start.16 = (bf16[32,32,768]{2,1,0:T(8,128)(2,1)S(1)}, bf16[32,32,768]{2,1,0:T(8,128)(2,1)}, u32[]{:S(2)}, u32[]{:S(2)}) collective-permute-start(bf16[32,32,768]{2,1,0:T(8,128)(2,1)S(1)} %copy-done.3), channel_id=1, source_target_pairs={{0,8},{4,12},{8,0},{12,4},{1,9},{5,13},{9,1},{13,5},{2,10},{6,14},... | collective-permute-start | bytes 4718600 | tf_op jit(solution)/shard_map/ppermute | solution.py:256
  320.6 45.1 %collective-permute-start.19 = (bf16[32,32,768]{2,1,0:T(8,128)(2,1)S(1)}, bf16[32,32,768]{2,1,0:T(8,128)(2,1)}, u32[]{:S(2)}, u32[]{:S(2)}) collective-permute-start(bf16[32,32,768]{2,1,0:T(8,128)(2,1)S(1)} %copy-done.3), channel_id=1, source_target_pairs={{0,4},{4,0},{8,12},{12,8},{1,5},{5,1},{9,13},{13,9},{2,6},{6,2},{1... | collective-permute-start | bytes 4718600 | tf_op jit(solution)/shard_map/ppermute | solution.py:256
  357.2 8.5 %collective-permute-start.20 = (bf16[32,32,768]{2,1,0:T(8,128)(2,1)}, bf16[32,32,768]{2,1,0:T(8,128)(2,1)}, u32[]{:S(2)}, u32[]{:S(2)}) collective-permute-start(bf16[32,32,768]{2,1,0:T(8,128)(2,1)} %collective-permute-done.16.refs_5_), channel_id=1, source_target_pairs={{0,4},{4,0},{8,12},{12,8},{1,5},{5,1},{9,13},{13,9},{2,6},{6,2},{1... | collective-permute-start | bytes 4718600 | tf_op jit(solution)/shard_map/ppermute | solution.py:256
Sparse Core Ops, SparseCore 0:
  10.4 118.0 all-gather.3
  130.1 61.7 all-gather.5
  208.7 63.8 all-gather.7

commit v7 on v5

--- a/solution.py
+++ b/solution.py
@@ -332,8 +332,8 @@
     (),
     (((0,), (0, 1)),),
     (((0,), (2,)),),
-    (((1,), (0, 1, 2)), ((0, 1), (3,))),
-    (((0, 1), (4,)), ((2,), (0, 1))),
+    (((1,), (0, 1)), ((0, 1), (3,))),
+    (((1,), (2,)), ((0, 1), (4,)), ((2,), (0, 1))),
     (((2,), (2, 3)), ((0, 1, 2), (5,))),
     (((2,), (4,)), ((0, 1, 2), (6,))),
 )

time: 363 us -> 366 us (level)
  Pallas kernels: 204 us -> 208 us
    pallas_call x10 -> x11, Pallas kernels: 171 us -> 175 us  [add_ladder(): pl.pallas_call(functools.partial(ladder_kernel, pieces=pieces, chunk_step...]
  transfers between devices with their start and end apart: 24 -> 24, of which waited for: 9 -> 9; matrix products, arithmetic and copies ran while one was open for 7% -> 7% of each run, Pallas kernels for 50% -> 51%
where the time goes in v7:
time: 366 us; the launch traced here: 363 us
  Pallas kernels  208 us (57%)
  waiting for transfers between devices  88.5 us (24%)
  local copies, waits for them, and re-layouts  24.8 us (7%)
  blocking collectives  15.6 us (4%)
  between operations  13.8 us (4%)
  starting transfers between devices  12.1 us (3%)
    pallas_call x11, Pallas kernels, add_ladder(): pl.pallas_call(functools.partial(ladder_kernel, pieces=pieces, chunk_step...  175 us
    ppermute x21, waiting for transfers between devices, swap(): return lax.ppermute(block, axis, [(i, i ^ bit) for i in range(size)])  66.7 us
    pallas_call x7, Pallas kernels, turn(): pl.pallas_call(turn_kernel, out_shape=jax.ShapeDtypeStruct((size, outer,...  25.8 us
    optimization_barrier x1, local copies, waits for them, and re-layouts, on_device(): owns, amplitudes = together((owns, amplitudes))  23 us
    all_gather x3, waiting for transfers between devices, gathered(): return [lax.all_gather(part, 'col', axis=0, tiled=True) for part in parts]  21.8 us
    all_to_all x1, blocking collectives, on_device(): return lax.all_to_all(shares, ('row', 'col'), 0, 0, tiled=True).sum(axis=0)  15.6 us
    ppermute x21, starting transfers between devices, swap(): return lax.ppermute(block, axis, [(i, i ^ bit) for i in range(size)])  11.8 us
    pallas_call x2, Pallas kernels, split_left(): pl.pallas_call(functools.partial(split_kernel, pieces=pieces, span=span),...  7.35 us
  transfers between devices with their start and end apart: 24, of which 9 were waited for; matrix products, arithmetic and copies ran while one was open for 7% of the time, Pallas kernels for 51%

profile of v7, /device:TPU:0, one launch (start us, length us, event | category | flops | bytes accessed | tf_op | source)
XLA Modules:
  0.0 363.3 jit_solution(15636409580238388105)
XLA Ops:
  6.5 3.7 %shard_map.37 = bf16[768,1024]{1,0:T(8,128)(2,1)} custom-call(bf16[768,8,256]{2,1,0:T(8,128)(2,1)} %in_ref.4), custom_call_target="tpu_custom_call" | custom-call | bytes 65536 | tf_op jit(solution)/shard_map/pallas_call | solution.py:243
  10.4 3.3 shard_map.38.refs_1_
  13.6 2.9 collective-permute-start
  16.6 4.7 %shard_map.39.refs_5_ = bf16[48,32,768]{2,1,0:T(8,128)(2,1)} custom-call(bf16[32,256,768]{2,1,0:T(8,128)(2,1)} %in_ref.9), custom_call_target="tpu_custom_call" | custom-call | bytes 65536 | tf_op jit(solution)/shard_map/pallas_call | solution.py:217
  21.3 0.1 collective-permute-start.2
  21.4 0.4 collective-permute-start.3
  21.8 30.4 %collective-permute-done.refs_3_ = bf16[32,32,768]{2,1,0:T(8,128)(2,1)} collective-permute-done((bf16[32,32,768]{2,1,0:T(8,128)(2,1)}, bf16[32,32,768]{2,1,0:T(8,128)(2,1)}, u32[]{:S(2)}, u32[]{:S(2)}) %collective-permute-start) | collective-permute-done | bytes 1572896 | tf_op jit(solution)/shard_map/ppermute | solution.py:256
  52.2 3.6 shard_map.40
  55.8 0.3 all-gather.8.cloned.1.call-start
  56.1 3.3 shard_map.45.refs_3_
  59.3 3.3 shard_map.44.refs_3_
  62.6 3.3 shard_map.43.refs_2_.refs_1_
  65.9 3.3 shard_map.42.refs_2_.refs_5_
  69.1 4.7 %shard_map.41.refs_1_ = bf16[48,32,768]{2,1,0:T(8,128)(2,1)} custom-call(bf16[32,256,768]{2,1,0:T(8,128)(2,1)} %in_ref.9), custom_call_target="tpu_custom_call" | custom-call | bytes 65536 | tf_op jit(solution)/shard_map/pallas_call | solution.py:217
  73.8 23.0 %copy.19 = bf16[256,256,256]{2,0,1:T(8,128)(2,1)} copy(bf16[256,256,256]{2,1,0:T(8,128)(2,1)} %param.5) | data formatting | bytes 67108864 | tf_op jit(solution)/shard_map/optimization_barrier | solution.py:304
  96.8 5.1 %collective-permute-done.2.refs_7_ = bf16[48,32,768]{2,1,0:T(8,128)(2,1)} collective-permute-done((bf16[48,32,768]{2,1,0:T(8,128)(2,1)}, bf16[48,32,768]{2,1,0:T(8,128)(2,1)}, u32[]{:S(2)}, u32[]{:S(2)}) %collective-permute-start.2) | collective-permute-done | bytes 2359328 | tf_op jit(solution)/shard_map/ppermute | solution.py:256
  101.9 1.7 collective-permute-start.1
  103.6 0.2 collective-permute-start.8
  103.8 3.0 collective-permute-done.6.refs_8_
  106.8 21.7 %all-gather.4.cloned.1.call-done.refs_0_ = bf16[3072,1024]{1,0:T(8,128)(2,1)} async-done(((bf16[768,1024]{1,0:T(8,128)(2,1)}), bf16[3072,1024]{1,0:T(8,128)(2,1)}) %all-gather.4.cloned.1.call-update) | async-done | bytes 6291472 | tf_op jit(solution)/shard_map/all_gather | solution.py:288
  128.5 0.7 broadcast_in_dim.3.total_ref
  129.2 22.7 %shard_map.46.total_ref = f32[256,256]{1,0:T(8,128)} custom-call(s32[1]{0:T(128)} %bitcast.place_ref, f32[256,256]{1,0:T(8,128)} %broadcast_in_dim.3.total_ref, bf16[256,256,256]{2,1,0:T(8,128)(2,1)} %bitcast.6, bf16[3072,1024]{1,0:T(8,128)(2,1)} %all-gather.4.cloned.1.call-done.refs_0_, ...), custom_call_target="tpu_custom_call", output_to_operand_aliasing={{}: (1, {})} | custom-call | flops 872415232 | bytes 22020096 | tf_op jit(solution)/shard_map/pallas_call | solution.py:162
  152.0 3.9 %collective-permute-done.1.refs_3_ = bf16[48,32,768]{2,1,0:T(8,128)(2,1)} collective-permute-done((bf16[48,32,768]{2,1,0:T(8,128)(2,1)}, bf16[48,32,768]{2,1,0:T(8,128)(2,1)}, u32[]{:S(2)}, u32[]{:S(2)}) %collective-permute-start.1) | collective-permute-done | bytes 2359328 | tf_op jit(solution)/shard_map/ppermute | solution.py:256
  155.9 1.7 collective-permute-start.7
  157.6 0.3 collective-permute-start.11
  157.9 2.9 collective-permute-done.9.refs_4_
  160.7 15.4 %shard_map.47.total_ref = f32[256,256]{1,0:T(8,128)} custom-call(s32[1]{0:T(128)} %bitcast.place_ref, f32[256,256]{1,0:T(8,128)} %shard_map.46.total_ref, bf16[256,256,256]{2,1,0:T(8,128)(2,1)} %bitcast.7, bf16[3072,1024]{1,0:T(8,128)(2,1)} %all-gather.4.cloned.1.call-done.refs_0_, ...), custom_call_target="tpu_custom_call", output_to_operand_aliasing={{}: (1, {})} | custom-call | flops 523449152 | bytes 15728640 | tf_op jit(solution)/shard_map/pallas_call | solution.py:162
  176.2 16.8 %collective-permute-done.7.refs_4_.refs_7_ = bf16[32,32,768]{2,1,0:T(8,128)(2,1)} collective-permute-done((bf16[32,32,768]{2,1,0:T(8,128)(2,1)}, bf16[32,32,768]{2,1,0:T(8,128)(2,1)}, u32[]{:S(2)}, u32[]{:S(2)}) %collective-permute-start.7) | collective-permute-done | bytes 1572896 | tf_op jit(solution)/shard_map/ppermute | solution.py:256
  193.0 1.7 collective-permute-start.10
  194.7 0.2 collective-permute-start.14
  194.9 14.8 %shard_map.48.total_ref = f32[256,256]{1,0:T(8,128)} custom-call(s32[1]{0:T(128)} %bitcast.place_ref, f32[256,256]{1,0:T(8,128)} %shard_map.47.total_ref, bf16[256,256,256]{2,1,0:T(8,128)(2,1)} %bitcast.8, bf16[3072,512]{1,0:T(8,128)(2,1)} %all-gather.6.cloned.1.call-done.refs_0_.refs_1_, ...), custom_call_target="tpu_custom_call", output_to_operand_aliasing={{}: (1, {})} | custom-call | flops 436207616 | bytes 18874368 | tf_op jit(solution)/shard_map/pallas_call | solution.py:162
  209.8 16.4 %shard_map.49.total_ref = f32[256,256]{1,0:T(8,128)} custom-call(s32[1]{0:T(128)} %bitcast.place_ref, f32[256,256]{1,0:T(8,128)} %shard_map.48.total_ref, bf16[256,256,256]{2,1,0:T(8,128)(2,1)} %bitcast.9, bf16[3072,1024]{1,0:T(8,128)(2,1)} %all-gather.4.cloned.1.call-done.refs_0_, ...), custom_call_target="tpu_custom_call", output_to_operand_aliasing={{}: (1, {})} | custom-call | flops 523449152 | bytes 15728640 | tf_op jit(solution)/shard_map/pallas_call | solution.py:162
  226.2 3.7 %collective-permute-done.10.refs_4_.refs_3_ = bf16[32,32,768]{2,1,0:T(8,128)(2,1)} collective-permute-done((bf16[32,32,768]{2,1,0:T(8,128)(2,1)S(1)}, bf16[32,32,768]{2,1,0:T(8,128)(2,1)}, u32[]{:S(2)}, u32[]{:S(2)}) %collective-permute-start.10) | collective-permute-done | bytes 1572896 | tf_op jit(solution)/shard_map/ppermute | solution.py:256
  229.9 1.7 collective-permute-start.13
  231.6 0.2 collective-permute-start.17
  231.8 10.3 %shard_map.50.total_ref = f32[256,256]{1,0:T(8,128)} custom-call(s32[1]{0:T(128)} %bitcast.place_ref, f32[256,256]{1,0:T(8,128)} %shard_map.49.total_ref, bf16[256,256,256]{2,1,0:T(8,128)(2,1)} %bitcast.10, bf16[3072,512]{1,0:T(8,128)(2,1)} %all-gather.6.cloned.1.call-done.refs_0_.refs_1_, ...), custom_call_target="tpu_custom_call", output_to_operand_aliasing={{}: (1, {})} | custom-call | flops 261724576 | bytes 12582912 | tf_op jit(solution)/shard_map/pallas_call | solution.py:162
  242.2 16.1 %shard_map.51.total_ref = f32[256,256]{1,0:T(8,128)} custom-call(s32[1]{0:T(128)} %bitcast.place_ref, f32[256,256]{1,0:T(8,128)} %shard_map.50.total_ref, bf16[256,256,256]{2,1,0:T(8,128)(2,1)} %bitcast.11, bf16[3072,1024]{1,0:T(8,128)(2,1)} %all-gather.4.cloned.1.call-done.refs_0_, ...), custom_call_target="tpu_custom_call", output_to_operand_aliasing={{}: (1, {})} | custom-call | flops 523449152 | bytes 15728640 | tf_op jit(solution)/shard_map/pallas_call | solution.py:162
  258.3 14.6 %shard_map.52.total_ref = f32[256,256]{1,0:T(8,128)} custom-call(s32[1]{0:T(128)} %bitcast.place_ref, f32[256,256]{1,0:T(8,128)} %shard_map.51.total_ref, bf16[256,256,256]{2,1,0:T(8,128)(2,1)} %bitcast.12, bf16[3072,512]{1,0:T(8,128)(2,1)} %all-gather.8.cloned.1.call-done.refs_0_.refs_2_, ...), custom_call_target="tpu_custom_call", output_to_operand_aliasing={{}: (1, {})} | custom-call | flops 436207616 | bytes 18874368 | tf_op jit(solution)/shard_map/pallas_call | solution.py:162
  272.9 0.3 collective-permute-start.18
  273.3 0.4 collective-permute-start.16
  273.6 14.7 %shard_map.53.total_ref = f32[256,256]{1,0:T(8,128)} custom-call(s32[1]{0:T(128)} %bitcast.place_ref, f32[256,256]{1,0:T(8,128)} %shard_map.52.total_ref, bf16[256,256,256]{2,1,0:T(8,128)(2,1)} %bitcast.13, bf16[3072,512]{1,0:T(8,128)(2,1)} %all-gather.8.cloned.1.call-done.refs_0_.refs_2_, ...), custom_call_target="tpu_custom_call", output_to_operand_aliasing={{}: (1, {})} | custom-call | flops 436207616 | bytes 18874368 | tf_op jit(solution)/shard_map/pallas_call | solution.py:162
  288.4 20.6 %shard_map.54.total_ref = f32[256,256]{1,0:T(8,128)} custom-call(s32[1]{0:T(128)} %bitcast.place_ref, f32[256,256]{1,0:T(8,128)} %shard_map.53.total_ref, bf16[256,256,256]{2,1,0:T(8,128)(2,1)} %bitcast.14, bf16[3072,1024]{1,0:T(8,128)(2,1)} %all-gather.4.cloned.1.call-done.refs_0_, ...), custom_call_target="tpu_custom_call", output_to_operand_aliasing={{}: (1, {})} | custom-call | flops 697932160 | bytes 18874368 | tf_op jit(solution)/shard_map/pallas_call | solution.py:162
  308.9 1.0 collective-permute-done.16.refs_5_
  309.9 8.5 %shard_map.55.total_ref = f32[256,256]{1,0:T(8,128)} custom-call(s32[1]{0:T(128)} %bitcast.place_ref, f32[256,256]{1,0:T(8,128)} %shard_map.54.total_ref, bf16[256,256,256]{2,1,0:T(8,128)(2,1)} %bitcast.15, bf16[3072,512]{1,0:T(8,128)(2,1)} %all-gather.8.cloned.1.call-done.refs_0_.refs_2_, ...), custom_call_target="tpu_custom_call", output_to_operand_aliasing={{}: (1, {})} | custom-call | flops 174483040 | bytes 9437184 | tf_op jit(solution)/shard_map/pallas_call | solution.py:162
  318.4 20.6 %shard_map.56 = f32[256,256]{1,0:T(8,128)} custom-call(s32[1]{0:T(128)} %bitcast.place_ref, f32[256,256]{1,0:T(8,128)} %shard_map.55.total_ref, bf16[256,256,256]{2,1,0:T(8,128)(2,1)} %bitcast.16, bf16[3072,1024]{1,0:T(8,128)(2,1)} %all-gather.4.cloned.1.call-done.refs_0_, ...), custom_call_target="tpu_custom_call", output_to_operand_aliasing={{}: (1, {})} | custom-call | flops 697932160 | bytes 18874368 | tf_op jit(solution)/shard_map/pallas_call | solution.py:162
  339.0 1.1 copy.17
  340.1 15.6 %all_to_all.5 = f32[16,16,256]{2,1,0:T(8,128)S(1)} all-to-all(f32[16,16,256]{2,1,0:T(8,128)S(1)} %bitcast.18), channel_id=1, replica_groups=mesh['parts'=2,'row'=4,'col'=4] {'row','col'}, dimensions={0} | all-to-all | bytes 524288 | tf_op jit(solution)/shard_map/all_to_all | solution.py:327
  355.7 0.6 reduce_sum.9
  (34 shorter events, 0.2 us)
Async XLA Ops:
  6.5 122.0 %all-gather.4.cloned.1.call-start = ((), (), s32[]{:S(2)}) async-start(), calls=%async_computation.1 | async-start | bytes 7864320 | tf_op jit(solution)/shard_map/all_gather | solution.py:288
  10.3 184.6 %all-gather.6.cloned.1.call-start = ((), (), s32[]{:S(2)}) async-start(), calls=%async_computation.2 | async-start | bytes 3932160 | tf_op jit(solution)/shard_map/all_gather | solution.py:288
  13.6 7.7 %copy-start = (bf16[32,32,768]{2,1,0:T(8,128)(2,1)S(1)}, bf16[32,32,768]{2,1,0:T(8,128)(2,1)}, u32[]{:S(2)}) copy-start(bf16[32,32,768]{2,1,0:T(8,128)(2,1)} %shard_map.38.refs_1_) | copy-start | bytes 4718596
  13.6 38.5 %collective-permute-start = (bf16[32,32,768]{2,1,0:T(8,128)(2,1)}, bf16[32,32,768]{2,1,0:T(8,128)(2,1)}, u32[]{:S(2)}, u32[]{:S(2)}) collective-permute-start(bf16[32,32,768]{2,1,0:T(8,128)(2,1)} %shard_map.38.refs_1_), channel_id=1, source_target_pairs={{0,8},{4,12},{8,0},{12,4},{1,9},{5,13},{9,1},{13,5},{2,10},{6,14},... | collective-permute-start | bytes 4718600 | tf_op jit(solution)/shard_map/ppermute | solution.py:256
  21.3 75.6 %collective-permute-start.5 = (bf16[48,32,768]{2,1,0:T(8,128)(2,1)}, bf16[48,32,768]{2,1,0:T(8,128)(2,1)}, u32[]{:S(2)}, u32[]{:S(2)}) collective-permute-start(bf16[48,32,768]{2,1,0:T(8,128)(2,1)} %shard_map.39.refs_5_), channel_id=1, source_target_pairs={{0,4},{4,0},{8,12},{12,8},{1,5},{5,1},{9,13},{13,9},{2,6},{6,2},{1... | collective-permute-start | bytes 7077896 | tf_op jit(solution)/shard_map/ppermute | solution.py:256
  21.3 80.6 %collective-permute-start.2 = (bf16[48,32,768]{2,1,0:T(8,128)(2,1)}, bf16[48,32,768]{2,1,0:T(8,128)(2,1)}, u32[]{:S(2)}, u32[]{:S(2)}) collective-permute-start(bf16[48,32,768]{2,1,0:T(8,128)(2,1)} %shard_map.39.refs_5_), channel_id=1, source_target_pairs={{0,8},{4,12},{8,0},{12,4},{1,9},{5,13},{9,1},{13,5},{2,10},{6,14},... | collective-permute-start | bytes 7077896 | tf_op jit(solution)/shard_map/ppermute | solution.py:256
  21.4 75.5 %collective-permute-start.3 = (bf16[32,32,768]{2,1,0:T(8,128)(2,1)S(1)}, bf16[32,32,768]{2,1,0:T(8,128)(2,1)}, u32[]{:S(2)}, u32[]{:S(2)}) collective-permute-start(bf16[32,32,768]{2,1,0:T(8,128)(2,1)S(1)} %copy-done), channel_id=1, source_target_pairs={{0,4},{4,0},{8,12},{12,8},{1,5},{5,1},{9,13},{13,9},{2,6},{6,2},{1... | collective-permute-start | bytes 4718600 | tf_op jit(solution)/shard_map/ppermute | solution.py:256
  52.2 49.7 %collective-permute-start.4 = (bf16[32,32,768]{2,1,0:T(8,128)(2,1)}, bf16[32,32,768]{2,1,0:T(8,128)(2,1)}, u32[]{:S(2)}, u32[]{:S(2)}) collective-permute-start(bf16[32,32,768]{2,1,0:T(8,128)(2,1)} %collective-permute-done.refs_3_), channel_id=1, source_target_pairs={{0,4},{4,0},{8,12},{12,8},{1,5},{5,1},{9,13},{13,9},{2,6},{6,2},{1... | collective-permute-start | bytes 4718600 | tf_op jit(solution)/shard_map/ppermute | solution.py:256
  55.8 202.5 %all-gather.8.cloned.1.call-start = ((), (), s32[]{:S(2)}) async-start(), calls=%async_computation.3 | async-start | bytes 3932160 | tf_op jit(solution)/shard_map/all_gather | solution.py:288
  101.9 4.9 %collective-permute-start.6 = (bf16[48,32,768]{2,1,0:T(8,128)(2,1)}, bf16[48,32,768]{2,1,0:T(8,128)(2,1)}, u32[]{:S(2)}, u32[]{:S(2)}) collective-permute-start(bf16[48,32,768]{2,1,0:T(8,128)(2,1)} %collective-permute-done.2.refs_7_), channel_id=1, source_target_pairs={{0,4},{4,0},{8,12},{12,8},{1,5},{5,1},{9,13},{13,9},{2,6},{6,2},{1... | collective-permute-start | bytes 7077896 | tf_op jit(solution)/shard_map/ppermute | solution.py:256
  101.9 54.0 %collective-permute-start.1 = (bf16[48,32,768]{2,1,0:T(8,128)(2,1)}, bf16[48,32,768]{2,1,0:T(8,128)(2,1)}, u32[]{:S(2)}, u32[]{:S(2)}) collective-permute-start(bf16[48,32,768]{2,1,0:T(8,128)(2,1)} %shard_map.41.refs_1_), channel_id=1, source_target_pairs={{0,8},{4,12},{8,0},{12,4},{1,9},{5,13},{9,1},{13,5},{2,10},{6,14},... | collective-permute-start | bytes 7077896 | tf_op jit(solution)/shard_map/ppermute | solution.py:256
  103.6 54.3 %collective-permute-start.8 = (bf16[48,32,768]{2,1,0:T(8,128)(2,1)}, bf16[48,32,768]{2,1,0:T(8,128)(2,1)}, u32[]{:S(2)}, u32[]{:S(2)}) collective-permute-start(bf16[48,32,768]{2,1,0:T(8,128)(2,1)} %shard_map.41.refs_1_), channel_id=1, source_target_pairs={{0,4},{4,0},{8,12},{12,8},{1,5},{5,1},{9,13},{13,9},{2,6},{6,2},{1... | collective-permute-start | bytes 7077896 | tf_op jit(solution)/shard_map/ppermute | solution.py:256
  155.9 4.9 %collective-permute-start.9 = (bf16[48,32,768]{2,1,0:T(8,128)(2,1)}, bf16[48,32,768]{2,1,0:T(8,128)(2,1)}, u32[]{:S(2)}, u32[]{:S(2)}) collective-permute-start(bf16[48,32,768]{2,1,0:T(8,128)(2,1)} %collective-permute-done.1.refs_3_), channel_id=1, source_target_pairs={{0,4},{4,0},{8,12},{12,8},{1,5},{5,1},{9,13},{13,9},{2,6},{6,2},{1... | collective-permute-start | bytes 7077896 | tf_op jit(solution)/shard_map/ppermute | solution.py:256
  155.9 37.1 %collective-permute-start.7 = (bf16[32,32,768]{2,1,0:T(8,128)(2,1)}, bf16[32,32,768]{2,1,0:T(8,128)(2,1)}, u32[]{:S(2)}, u32[]{:S(2)}) collective-permute-start(bf16[32,32,768]{2,1,0:T(8,128)(2,1)} %shard_map.42.refs_2_.refs_5_), channel_id=1, source_target_pairs={{0,8},{4,12},{8,0},{12,4},{1,9},{5,13},{9,1},{13,5},{2,10},{6,14},... | collective-permute-start | bytes 4718600 | tf_op jit(solution)/shard_map/ppermute | solution.py:256
  157.6 35.4 %copy-start.1 = (bf16[32,32,768]{2,1,0:T(8,128)(2,1)S(1)}, bf16[32,32,768]{2,1,0:T(8,128)(2,1)}, u32[]{:S(2)}) copy-start(bf16[32,32,768]{2,1,0:T(8,128)(2,1)} %shard_map.43.refs_2_.refs_1_) | copy-start | bytes 4718596
  157.6 52.2 %collective-permute-start.11 = (bf16[32,32,768]{2,1,0:T(8,128)(2,1)}, bf16[32,32,768]{2,1,0:T(8,128)(2,1)}, u32[]{:S(2)}, u32[]{:S(2)}) collective-permute-start(bf16[32,32,768]{2,1,0:T(8,128)(2,1)} %shard_map.42.refs_2_.refs_5_), channel_id=1, source_target_pairs={{0,4},{4,0},{8,12},{12,8},{1,5},{5,1},{9,13},{13,9},{2,6},{6,2},{1... | collective-permute-start | bytes 4718600 | tf_op jit(solution)/shard_map/ppermute | solution.py:256
  193.0 16.8 %collective-permute-start.12 = (bf16[32,32,768]{2,1,0:T(8,128)(2,1)}, bf16[32,32,768]{2,1,0:T(8,128)(2,1)}, u32[]{:S(2)}, u32[]{:S(2)}) collective-permute-start(bf16[32,32,768]{2,1,0:T(8,128)(2,1)} %collective-permute-done.7.refs_4_.refs_7_), channel_id=1, source_target_pairs={{0,4},{4,0},{8,12},{12,8},{1,5},{5,1},{9,13},{13,9},{2,6},{6,2},{1... | collective-permute-start | bytes 4718600 | tf_op jit(solution)/shard_map/ppermute | solution.py:256
  193.0 36.9 %collective-permute-start.10 = (bf16[32,32,768]{2,1,0:T(8,128)(2,1)S(1)}, bf16[32,32,768]{2,1,0:T(8,128)(2,1)}, u32[]{:S(2)}, u32[]{:S(2)}) collective-permute-start(bf16[32,32,768]{2,1,0:T(8,128)(2,1)S(1)} %copy-done.1), channel_id=1, source_target_pairs={{0,8},{4,12},{8,0},{12,4},{1,9},{5,13},{9,1},{13,5},{2,10},{6,14},... | collective-permute-start | bytes 4718600 | tf_op jit(solution)/shard_map/ppermute | solution.py:256
  194.7 47.5 %collective-permute-start.14 = (bf16[32,32,768]{2,1,0:T(8,128)(2,1)S(1)}, bf16[32,32,768]{2,1,0:T(8,128)(2,1)}, u32[]{:S(2)}, u32[]{:S(2)}) collective-permute-start(bf16[32,32,768]{2,1,0:T(8,128)(2,1)S(1)} %copy-done.1), channel_id=1, source_target_pairs={{0,4},{4,0},{8,12},{12,8},{1,5},{5,1},{9,13},{13,9},{2,6},{6,2},{1... | collective-permute-start | bytes 4718600 | tf_op jit(solution)/shard_map/ppermute | solution.py:256
  229.9 12.2 %collective-permute-start.15 = (bf16[32,32,768]{2,1,0:T(8,128)(2,1)}, bf16[32,32,768]{2,1,0:T(8,128)(2,1)}, u32[]{:S(2)}, u32[]{:S(2)}) collective-permute-start(bf16[32,32,768]{2,1,0:T(8,128)(2,1)} %collective-permute-done.10.refs_4_.refs_3_), channel_id=1, source_target_pairs={{0,4},{4,0},{8,12},{12,8},{1,5},{5,1},{9,13},{13,9},{2,6},{6,2},{1... | collective-permute-start | bytes 4718600 | tf_op jit(solution)/shard_map/ppermute | solution.py:256
  229.9 43.0 %collective-permute-start.13 = (bf16[32,32,768]{2,1,0:T(8,128)(2,1)}, bf16[32,32,768]{2,1,0:T(8,128)(2,1)}, u32[]{:S(2)}, u32[]{:S(2)}) collective-permute-start(bf16[32,32,768]{2,1,0:T(8,128)(2,1)} %shard_map.44.refs_3_), channel_id=1, source_target_pairs={{0,8},{4,12},{8,0},{12,4},{1,9},{5,13},{9,1},{13,5},{2,10},{6,14},... | collective-permute-start | bytes 4718600 | tf_op jit(solution)/shard_map/ppermute | solution.py:256
  231.6 56.7 %collective-permute-start.17 = (bf16[32,32,768]{2,1,0:T(8,128)(2,1)}, bf16[32,32,768]{2,1,0:T(8,128)(2,1)}, u32[]{:S(2)}, u32[]{:S(2)}) collective-permute-start(bf16[32,32,768]{2,1,0:T(8,128)(2,1)} %shard_map.44.refs_3_), channel_id=1, source_target_pairs={{0,4},{4,0},{8,12},{12,8},{1,5},{5,1},{9,13},{13,9},{2,6},{6,2},{1... | collective-permute-start | bytes 4718600 | tf_op jit(solution)/shard_map/ppermute | solution.py:256
  258.3 15.0 %copy-start.2 = (bf16[32,32,768]{2,1,0:T(8,128)(2,1)S(1)}, bf16[32,32,768]{2,1,0:T(8,128)(2,1)}, u32[]{:S(2)}) copy-start(bf16[32,32,768]{2,1,0:T(8,128)(2,1)} %shard_map.45.refs_3_) | copy-start | bytes 4718596
  272.9 15.4 %collective-permute-start.18 = (bf16[32,32,768]{2,1,0:T(8,128)(2,1)}, bf16[32,32,768]{2,1,0:T(8,128)(2,1)}, u32[]{:S(2)}, u32[]{:S(2)}) collective-permute-start(bf16[32,32,768]{2,1,0:T(8,128)(2,1)} %collective-permute-done.13.refs_5_), channel_id=1, source_target_pairs={{0,4},{4,0},{8,12},{12,8},{1,5},{5,1},{9,13},{13,9},{2,6},{6,2},{1... | collective-permute-start | bytes 4718600 | tf_op jit(solution)/shard_map/ppermute | solution.py:256
  273.3 36.7 %collective-permute-start.16 = (bf16[32,32,768]{2,1,0:T(8,128)(2,1)S(1)}, bf16[32,32,768]{2,1,0:T(8,128)(2,1)}, u32[]{:S(2)}, u32[]{:S(2)}) collective-permute-start(bf16[32,32,768]{2,1,0:T(8,128)(2,1)S(1)} %copy-done.2), channel_id=1, source_target_pairs={{0,8},{4,12},{8,0},{12,4},{1,9},{5,13},{9,1},{13,5},{2,10},{6,14},... | collective-permute-start | bytes 4718600 | tf_op jit(solution)/shard_map/ppermute | solution.py:256
  273.6 44.8 %collective-permute-start.19 = (bf16[32,32,768]{2,1,0:T(8,128)(2,1)S(1)}, bf16[32,32,768]{2,1,0:T(8,128)(2,1)}, u32[]{:S(2)}, u32[]{:S(2)}) collective-permute-start(bf16[32,32,768]{2,1,0:T(8,128)(2,1)S(1)} %copy-done.2), channel_id=1, source_target_pairs={{0,4},{4,0},{8,12},{12,8},{1,5},{5,1},{9,13},{13,9},{2,6},{6,2},{1... | collective-permute-start | bytes 4718600 | tf_op jit(solution)/shard_map/ppermute | solution.py:256
  309.9 8.5 %collective-permute-start.20 = (bf16[32,32,768]{2,1,0:T(8,128)(2,1)}, bf16[32,32,768]{2,1,0:T(8,128)(2,1)}, u32[]{:S(2)}, u32[]{:S(2)}) collective-permute-start(bf16[32,32,768]{2,1,0:T(8,128)(2,1)} %collective-permute-done.16.refs_5_), channel_id=1, source_target_pairs={{0,4},{4,0},{8,12},{12,8},{1,5},{5,1},{9,13},{13,9},{2,6},{6,2},{1... | collective-permute-start | bytes 4718600 | tf_op jit(solution)/shard_map/ppermute | solution.py:256
Sparse Core Ops, SparseCore 0:
  10.4 118.0 all-gather.3
  130.1 61.7 all-gather.5
  193.4 62.1 all-gather.7
